TPU v7x, 256 devices: a whole 4x4x8 slice. The times are simulated.
256 devices in a mesh: layer: 16 (over z, y_lo), dp: 16 (over x, y_hi, core).
Axes of the slice: x: 4, y: 4 (y_hi: 2, y_lo: 2; y = y_hi * 2 + y_lo), z: 8, core: 2. Of those that a mesh axis runs over, the one named last changes fastest.
Arguments:
- residual: bfloat16 [2, 2048, 3584], P(None, 'dp'), may hold values from -6 to 6
- cotangent: bfloat16 [2, 2048, 3584], P(None, 'dp'), may hold values from -6 to 6
- decoder_first: bfloat16 [8192, 2, 3584], P('layer', None, 'dp'), may hold values from -0.09375 to 0.09375
- decoder_second: bfloat16 [8192, 3584], P('layer', 'dp'), may hold values from -0.09375 to 0.09375
- latent_index: int32 [2, 2048, 64], P(None, 'dp'), may hold values from 0 to 8191, all different within a row
- latent_value: bfloat16 [2, 2048, 64], P(None, 'dp'), may hold values from 0.25 to 3
- active_count: int32 [2, 2048], P(None, 'dp'), may hold values from 8 to 64
Outputs:
- decoder_first_grad: bfloat16 [8192, 2, 3584], P('layer', None, 'dp')
- decoder_second_grad: bfloat16 [8192, 3584], P('layer', 'dp')
- encoder_grad: bfloat16 [3584, 2, 8192], P('dp', None, 'layer')
- latent_grad: float32 [2, 2048, 64], P(None, 'dp')
Inputs may be any that keep to these rules, and one draw needn't show every extreme that they name: `latent_index`: the 64 slots of a token and layer name distinct latents of that layer; slots at or past active_count are padding.
All inputs are finite; a program needn't handle non-finite values.
Results may differ from a plain program's by a relative error of at most 0.02.
Values may be sent and summed in bfloat16 or wider, within the bound.
No kernel may reach another device: no remote copies, remote signals or barrier semaphores. Data moves between devices by JAX's collectives and lax.ppermute only.
A program may use at most 128 MiB of HBM per device.

v0:
```python
import jax
import jax.numpy as jnp
from jax import lax
from jax.sharding import PartitionSpec as P


def contract_last(left_side, right_side):
    return lax.dot_general(
        left_side, right_side, (((1,), (1,)), ((), ())), preferred_element_type=jnp.float32
    )


def group_slots(latent_ids, live_count, group_start, lat_width):
    slot_count = latent_ids.shape[-1]
    is_live = jnp.arange(slot_count)[None, :] < live_count[:, None]
    local_index = latent_ids - group_start
    inside = is_live & (local_index >= 0) & (local_index < lat_width)
    return (inside, jnp.where(inside, local_index, lat_width))


def block_rows():
    return 128


def dense_rows(target_cols, latent_vals, lat_width):
    row_count = target_cols.shape[0]
    slot_count = target_cols.shape[1]
    step_rows = block_rows()
    blocks = row_count // step_rows
    cols_blocks = target_cols.reshape(blocks, step_rows, slot_count)
    vals_blocks = latent_vals.reshape(blocks, step_rows, slot_count)
    columns = jnp.arange(lat_width, dtype=jnp.int32)

    def dense_one_block(pair):
        block_cols, block_vals = pair
        equal = block_cols[:, :, None] == columns[None, None, :]
        spread = jnp.where(equal, block_vals.astype(jnp.float32)[:, :, None], jnp.float32(0.0))
        return jnp.sum(spread, axis=1).astype(latent_vals.dtype)

    return lax.map(dense_one_block, (cols_blocks, vals_blocks)).reshape(row_count, lat_width)


def picked_slots(inside, target_cols, latent_grads, lat_width):
    row_count = target_cols.shape[0]
    slot_count = target_cols.shape[1]
    step_rows = block_rows()
    blocks = row_count // step_rows
    cols_blocks = target_cols.reshape(blocks, step_rows, slot_count)
    grad_blocks = latent_grads.reshape(blocks, step_rows, lat_width)
    columns = jnp.arange(lat_width, dtype=jnp.int32)

    def picked_one_block(pair):
        block_cols, block_grads = pair
        equal = block_cols[:, :, None] == columns[None, None, :]
        return jnp.sum(jnp.where(equal, block_grads[:, None, :], jnp.float32(0.0)), axis=2)

    chosen = lax.map(picked_one_block, (cols_blocks, grad_blocks)).reshape(row_count, slot_count)
    return jnp.where(inside, chosen, jnp.float32(0.0))


def shards(
    residual, cotangent, decoder_first, decoder_second, latent_index, latent_value, active_count
):
    lat_width = decoder_first.shape[0]
    group_start = lax.axis_index("layer") * lat_width
    group_first = group_slots(latent_index[0], active_count[0], group_start, lat_width)
    group_second = group_slots(latent_index[1], active_count[1], group_start, lat_width)
    stacked = jnp.concatenate([decoder_first, decoder_second[:, None, :]], axis=1)
    grad_first = cotangent[0]
    grad_second = cotangent[1]
    weight_piece = lax.all_gather(stacked, "dp", axis=2, tiled=True)
    sum_first = contract_last(grad_first, weight_piece[:, 0, :]) + contract_last(
        grad_second, weight_piece[:, 1, :]
    )
    sum_second = contract_last(grad_second, weight_piece[:, 2, :])
    slot_part = jnp.stack(
        [
            picked_slots(group_first[0], group_first[1], sum_first, lat_width),
            picked_slots(group_second[0], group_second[1], sum_second, lat_width),
        ]
    )
    codes_first = dense_rows(group_first[1], latent_value[0], lat_width)
    codes_second = dense_rows(group_second[1], latent_value[1], lat_width)
    term_first = jnp.einsum(
        "tr,atd->rad", codes_first, cotangent, preferred_element_type=jnp.float32
    )
    term_second = jnp.einsum(
        "tr,td->rd", codes_second, cotangent[1], preferred_element_type=jnp.float32
    )[:, None, :]
    summed = lax.psum_scatter(
        jnp.concatenate([term_first, term_second], axis=1).astype(jnp.bfloat16),
        "dp",
        scatter_dimension=2,
        tiled=True,
    ).astype(jnp.float32)
    first_grad = summed[:, :2, :]
    second_grad = summed[:, 2, :]
    latent_grad = lax.psum(slot_part.astype(jnp.bfloat16), "layer").astype(jnp.float32)
    grad_codes = latent_grad.astype(jnp.bfloat16)
    back_first = dense_rows(group_first[1], grad_codes[0], lat_width)
    back_second = dense_rows(group_second[1], grad_codes[1], lat_width)
    latent_codes = jnp.stack([back_first, back_second])
    encoder_part = lax.psum_scatter(
        jnp.einsum(
            "atd,atr->dar", residual, latent_codes, preferred_element_type=jnp.float32
        ).astype(jnp.bfloat16),
        "dp",
        scatter_dimension=0,
        tiled=True,
    )
    return (
        first_grad.astype(jnp.bfloat16),
        second_grad.astype(jnp.bfloat16),
        encoder_part,
        latent_grad,
    )


def solution(mesh):
    return jax.shard_map(
        shards,
        mesh=mesh,
        in_specs=(
            P(None, "dp", None),
            P(None, "dp", None),
            P("layer", None, "dp"),
            P("layer", "dp"),
            P(None, "dp", None),
            P(None, "dp", None),
            P(None, "dp"),
        ),
        out_specs=(
            P("layer", None, "dp"),
            P("layer", "dp"),
            P("dp", None, "layer"),
            P(None, "dp", None),
        ),
        check_vma=False,
    )
```

profile of v0, /device:TPU:2, one launch (start us, length us, event | category | flops | bytes accessed | tf_op | source)
XLA Modules:
  0.0 540.3 jit_solution(8257855568372168056)
XLA Ops:
  7.2 2.2 pad_maximum_fusion.1
  9.5 0.8 fusion.35
  11.4 0.8 slice_bitcast_fusion.15
  12.4 88.9 %all-gather.2.cloned.1.call-done = bf16[512,3,3584]{0,2,1:T(8,128)(2,1)} async-done(((bf16[512,3,224]{0,2,1:T(8,128)(2,1)}), bf16[512,3,3584]{0,2,1:T(8,128)(2,1)}) %all-gather.2.cloned.1.call-update) | async-done | bytes 11010064 | tf_op jit(solution)/shard_map/all_gather | solution.py:71
  101.3 3.4 fusion.3
  104.7 3.4 fusion.7
  108.3 3.4 fusion.5
  111.9 3.2 select_reduce_fusion.3
  115.1 3.2 select_reduce_fusion.2
  118.4 63.1 %psum.7 = bf16[2,128,64]{2,1,0:T(8,128)(2,1)S(1)} all-reduce(bf16[2,128,64]{2,1,0:T(8,128)(2,1)S(1)} %pad_maximum_fusion.2), channel_id=1, replica_groups=mesh['layer'=16,'dp'=16] {'layer'}, use_global_device_ids=true, to_apply=%region_5.6 | all-reduce | flops 16384 | bytes 65536 | tf_op jit(solution)/shard_map/psum | solution.py:98
  181.6 6.1 %select_reduce_fusion.1 = (bf16[128,512]{1,0:T(8,128)(2,1)S(1)}, bf16[128,512]{1,0:T(8,128)(2,1)S(1)}) fusion(f32[128,64]{1,0:T(8,128)S(1)} %get-tuple-element.100, s32[128,64]{1,0:T(8,128)S(1)} %bitcast_select_fusion.3, f32[128,64]{1,0:T(8,128)S(1)} %copy.34), kind=kLoop, calls=%fused_computation.1 | loop fusion | flops 20840448 | bytes 360448 | tf_op jit(solution)/shard_map/while/body/eval_jaxpr/reduce_sum | solution.py:38
  187.8 6.1 %select_reduce_fusion = (bf16[128,512]{1,0:T(8,128)(2,1)S(1)}, bf16[128,512]{1,0:T(8,128)(2,1)S(1)}) fusion(f32[128,64]{1,0:T(8,128)S(1)} %get-tuple-element.101, s32[128,64]{1,0:T(8,128)S(1)} %bitcast_select_fusion.2, f32[128,64]{1,0:T(8,128)S(1)} %copy.37), kind=kLoop, calls=%fused_computation | loop fusion | flops 20840448 | bytes 360448 | tf_op jit(solution)/shard_map/while/body/eval_jaxpr/reduce_sum | solution.py:38
  193.9 5.0 fusion
  199.0 18.7 %copy.42 = bf16[3584,2,512]{2,1,0:T(2,128)(2,1)} copy(bf16[3584,2,512]{0,2,1:T(8,128)(2,1)} %fusion) | data formatting | bytes 14680064 | tf_op jit(solution)/shard_map/convert_element_type | solution.py:106
  218.0 1.1 fusion.1
  219.1 2.1 convolution_convert_fusion.1
  221.2 4.8 pad_maximum_fusion
  226.0 23.9 %copy.48 = bf16[512,3,3584]{0,1,2:T(4,128)(2,1)} copy(bf16[512,3,3584]{2,0,1:T(8,128)(2,1)} %pad_maximum_fusion) | data formatting | bytes 22020096
  249.9 13.3 %copy.56 = bf16[448,8,3,512]{3,1,2,0:T(8,128)(2,1)} copy(bf16[448,8,3,512]{3,2,1,0:T(4,128)(2,1)} %bitcast.100) | data formatting | bytes 22020096
  265.8 134.6 %all-reduce.3.cloned.1.call-done = bf16[3584,2,512]{2,1,0:T(2,128)(2,1)} async-done(((bf16[3584,2,512]{2,1,0:T(2,128)(2,1)}), bf16[3584,2,512]{2,1,0:T(2,128)(2,1)}) %all-reduce.3.cloned.1.call-update) | async-done | bytes 7340048
  400.4 2.1 constant_dynamic-slice_fusion
  402.5 126.4 %reduce-scatter.4.cloned.1.call-done = bf16[224,1536]{1,0:T(8,128)(2,1)} async-done(((bf16[3584,1536]{1,0:T(8,128)(2,1)}), bf16[224,1536]{1,0:T(8,128)(2,1)}) %reduce-scatter.4.cloned.1.call-update) | async-done | bytes 688144
  528.9 2.5 reshape.176
  532.3 0.8 copy.43
  (33 shorter events, 5.8 us)
Async XLA Ops:
  7.2 186.8 %copy-start = (bf16[2,128,3584]{2,1,0:T(8,128)(2,1)S(1)}, bf16[2,128,3584]{2,1,0:T(8,128)(2,1)}, u32[]{:S(2)}) copy-start(bf16[2,128,3584]{2,1,0:T(8,128)(2,1)} %param.7) | copy-start | bytes 5505028
  7.2 94.1 %all-gather.2.cloned.1.call-start = ((), (), s32[]{:S(2)}) async-start(), calls=%async_computation.1 | async-start | bytes 11698176 | tf_op jit(solution)/shard_map/all_gather | solution.py:71
  9.4 391.0 %all-reduce.3.cloned.1.call-start = ((), (), s32[]{:S(2)}) async-start(), calls=%async_computation.3 | async-start | bytes 14680064
  199.0 19.0 %copy-start.2 = (bf16[2,128,3584]{2,1,0:T(8,128)(2,1)S(1)}, bf16[2,128,3584]{2,1,0:T(8,128)(2,1)}, u32[]{:S(2)}) copy-start(bf16[2,128,3584]{2,1,0:T(8,128)(2,1)} %param.8) | copy-start | bytes 5505028
  217.7 311.1 %reduce-scatter.4.cloned.1.call-start = ((), (), s32[]{:S(2)}) async-start(), calls=%async_computation.2 | async-start | bytes 11698176
  249.9 283.9 %copy-start.1 = (bf16[2,128,3584]{2,1,0:T(8,128)(2,1)S(1)}, bf16[2,128,3584]{2,1,0:T(8,128)(2,1)}, u32[]{:S(2)}) copy-start(bf16[2,128,3584]{2,1,0:T(8,128)(2,1)} %param.7) | copy-start | bytes 5505028
  263.2 0.7 copy-start.3
Sparse Core Ops, SparseCore 0:
  10.8 90.4 all-gather.1
  217.9 182.5 all-reduce.2
  405.1 123.7 reduce-scatter.3
where the time goes:
time: 542 us; the launch traced here: 540 us
  waiting for transfers between devices  350 us (65%)
  local copies, waits for them, and re-layouts  67.3 us (12%)
  blocking collectives  63.1 us (12%)
  other arithmetic  26.5 us (5%)
  matrix products  18.5 us (3%)
  between operations  14.6 us (3%)
    unnamed x5, waiting for transfers between devices  261 us
    all_gather x1, waiting for transfers between devices, shards(): weight_piece = lax.all_gather(stacked, 'dp', axis=2, tiled=True)  88.9 us
    psum x1, blocking collectives, shards(): lax.psum(slot_part.astype(jnp.bfloat16), 'layer').astype(jnp.float32)  63.1 us
    unnamed x17, local copies, waits for them, and re-layouts  44.8 us
    convert_element_type x1, local copies, waits for them, and re-layouts, shards(): encoder_part = lax.psum_scatter(jnp.einsum('atd,atr->dar', residual, late...  18.7 us
    reduce_sum x2, other arithmetic, dense_one_block(): return jnp.sum(spread, axis=1).astype(latent_vals.dtype)  12.1 us
  transfers between devices with their start and end apart: 3, of which 3 were waited for; matrix products, arithmetic and copies ran while one was open for 10% of the time, Pallas kernels for 0%

commit v1 on v0

v1 whole, which is shorter than its diff:
```python
import functools
import jax
import jax.numpy as jnp
from jax import lax
from jax.experimental import pallas as pl
from jax.experimental.pallas import tpu as pltpu
from jax.sharding import PartitionSpec as P

BF16 = jnp.bfloat16
F32 = jnp.float32
LANES = 128
SHIFT = 256
EMPTY = 512


def grant(mib):
    return pltpu.CompilerParams(vmem_limit_bytes=mib << 20)


def cost(flops, moved):
    return pl.CostEstimate(flops=flops, bytes_accessed=moved, transcendentals=0)


def lane_pick(table, where):
    return jnp.take_along_axis(table, where, axis=1, mode="promise_in_bounds")


def pack_kernel(lat_width, start_ref, cot_ref, res_ref, idx_ref, val_ref, live_ref, out_ref, rank_ref, slot_ref):
    slots, tokens = idx_ref.shape[1:]
    dests = out_ref.shape[0]
    cols = cot_ref.shape[2] // dests

    @pl.when(pl.program_id(0) == 0)
    def _():
        start = start_ref[0]
        place = lax.broadcasted_iota(jnp.int32, (slots, tokens), 0)
        found, values = [], []
        for layer in range(2):
            local = idx_ref[layer] - start
            inside = (place < live_ref[layer : layer + 1, :]) & (local >= 0) & (local < lat_width)
            key = jnp.where(inside, local, 1 << 20)
            rank = jnp.zeros((slots, tokens), jnp.int32)
            for slot in range(slots):
                rank = rank + jnp.where(key[slot : slot + 1, :] < key, 1, 0)
            rank = jnp.where(inside, rank, slots)
            rank_ref[layer] = rank
            key = local - SHIFT
            value = val_ref[layer].astype(F32)
            held = jnp.full((slots, tokens), EMPTY, jnp.int32)
            code = jnp.zeros((slots, tokens), F32)
            for slot in range(slots):
                here = rank[slot : slot + 1, :] == place
                held = jnp.where(here, key[slot : slot + 1, :], held)
                code = jnp.where(here, value[slot : slot + 1, :], code)
            found.append(held.astype(F32))
            values.append(code)
        slot_ref[0:tokens, :] = jnp.concatenate(found, axis=0).T.astype(BF16)
        slot_ref[tokens : 2 * tokens, :] = jnp.concatenate(values, axis=0).T.astype(BF16)

    half = 2 * cols + tokens
    for source, base in ((cot_ref, 0), (res_ref, half + tokens)):
        for layer in range(2):
            turned = source[layer].T
            for dest in range(dests):
                out_ref[dest, base + layer * cols : base + (layer + 1) * cols, :] = turned[
                    dest * cols : (dest + 1) * cols
                ]
    for dest in range(dests):
        out_ref[dest, 2 * cols : half + tokens, :] = slot_ref[...]


def pack(start, cotangent, residual, index, value, live, lat_width, parts):
    _, tokens, width = cotangent.shape
    slots = index.shape[1]
    steps = 4
    cols = width // parts
    rows = 4 * cols + 2 * tokens
    return pl.pallas_call(
        functools.partial(pack_kernel, lat_width),
        grid=(steps,),
        in_specs=[
            pl.BlockSpec(memory_space=pltpu.SMEM),
            pl.BlockSpec((2, tokens, width // steps), lambda i: (0, 0, i)),
            pl.BlockSpec((2, tokens, width // steps), lambda i: (0, 0, i)),
            pl.BlockSpec((2, slots, tokens), lambda i: (0, 0, 0)),
            pl.BlockSpec((2, slots, tokens), lambda i: (0, 0, 0)),
            pl.BlockSpec((2, tokens), lambda i: (0, 0)),
        ],
        out_specs=[
            pl.BlockSpec((parts // steps, rows, tokens), lambda i: (i, 0, 0)),
            pl.BlockSpec((2, slots, tokens), lambda i: (0, 0, 0)),
        ],
        out_shape=[
            jax.ShapeDtypeStruct((parts, rows, tokens), BF16),
            jax.ShapeDtypeStruct((2, slots, tokens), jnp.int32),
        ],
        scratch_shapes=[pltpu.VMEM((2 * tokens, LANES), BF16)],
        compiler_params=grant(40),
        cost_estimate=cost(0, 10 << 20),
    )(start, cotangent, residual, index, value, live)


def terms_kernel(wf_ref, ws_ref, got_ref, out_ref, weight_ref):
    shards, _, tokens = got_ref.shape
    cols, lat_width = ws_ref.shape

    @pl.when(pl.program_id(0) == 0)
    def _():
        weight_ref[0:cols, 0:lat_width] = wf_ref[0]
        weight_ref[cols : 2 * cols, 0:lat_width] = wf_ref[1]
        weight_ref[0:cols, lat_width:] = jnp.zeros((cols, lat_width), BF16)
        weight_ref[cols : 2 * cols, lat_width:] = ws_ref[...]

    for shard in range(shards):
        dense = lax.dot_general(
            got_ref[shard, 0 : 2 * cols, :].T,
            weight_ref[...],
            (((1,), (0,)), ((), ())),
            preferred_element_type=F32,
        )
        held = got_ref[shard, 2 * cols : 2 * cols + tokens, :].astype(F32).astype(jnp.int32) + SHIFT
        lane = lax.broadcasted_iota(jnp.int32, held.shape, 1)
        chunks = lat_width // LANES
        chunk = jnp.where(
            held < lat_width, (held >> 7) + jnp.where(lane >= LANES // 2, chunks, 0), 2 * chunks
        )
        within = held & (LANES - 1)
        picked = jnp.zeros(held.shape, F32)
        for part in range(2 * chunks):
            table = dense[:, part * LANES : (part + 1) * LANES]
            picked = jnp.where(chunk == part, lane_pick(table, within), picked)
        out_ref[shard] = picked.astype(BF16)


def slot_terms(first, second, got):
    parts, rows, tokens = got.shape
    cols, lat_width = second.shape
    shards = 2
    return pl.pallas_call(
        terms_kernel,
        grid=(parts // shards,),
        in_specs=[
            pl.BlockSpec((2, cols, lat_width), lambda i: (0, 0, 0)),
            pl.BlockSpec((cols, lat_width), lambda i: (0, 0)),
            pl.BlockSpec((shards, rows // 2, tokens), lambda i: (i, 0, 0)),
        ],
        out_specs=pl.BlockSpec((shards, tokens, LANES), lambda i: (i, 0, 0)),
        out_shape=jax.ShapeDtypeStruct((parts, tokens, LANES), BF16),
        scratch_shapes=[pltpu.VMEM((2 * cols, 2 * lat_width), BF16)],
        compiler_params=grant(40),
        cost_estimate=cost(2 * parts * tokens * cols * 3 * lat_width, 6 << 20),
    )(first, second, got)


def total_kernel(got_ref, rank_ref, grad_ref, part_ref):
    total = jnp.sum(got_ref[...].astype(F32), axis=0)
    for dest in range(grad_ref.shape[0]):
        grad_ref[dest] = total.astype(BF16)
    turned = total.T
    slots = rank_ref.shape[1]
    for layer in range(2):
        rank = rank_ref[layer]
        part = jnp.zeros(rank.shape, F32)
        for slot in range(slots):
            row = layer * slots + slot
            part = jnp.where(rank == slot, turned[row : row + 1, :], part)
        part_ref[layer] = part.astype(BF16)


def slot_totals(got, rank):
    parts, tokens, _ = got.shape
    return pl.pallas_call(
        total_kernel,
        out_shape=[
            jax.ShapeDtypeStruct(got.shape, BF16),
            jax.ShapeDtypeStruct(rank.shape, BF16),
        ],
        compiler_params=grant(40),
        cost_estimate=cost(0, 1 << 20),
    )(got, rank)


def weights_kernel(low_ref, high_ref, grad_ref, first_ref, second_ref, enc_ref, code_ref, back_ref, sum_ref):
    shards, half, tokens = low_ref.shape
    cols, lat_width = second_ref.shape
    step = pl.program_id(0)
    block = 16
    steps = (32, 16, 8, 4, 2, 1)

    def spread(at, carry):
        shard = at // (tokens // block)
        low = pl.multiple_of((at % (tokens // block)) * block, block)
        held = low_ref[shard, pl.ds(2 * cols + low, block), :].astype(F32)
        value = high_ref[shard, pl.ds(low, block), :].astype(F32)
        grad = grad_ref[shard, pl.ds(low, block), :].astype(F32)
        row = pl.multiple_of(at * block, block)
        for layer in range(2):
            base = layer * (LANES // 2)
            for chunk in range(lat_width // LANES):
                column = (
                    lax.broadcasted_iota(jnp.int32, (block, LANES), 1) + (chunk * LANES - SHIFT)
                ).astype(F32)
                spot = jnp.full((block, LANES), base, jnp.int32)
                key = lane_pick(held, spot)
                for jump in steps:
                    next_spot = spot + jump
                    next_key = lane_pick(held, next_spot)
                    before = next_key <= column
                    spot = jnp.where(before, next_spot, spot)
                    key = jnp.where(before, next_key, key)
                hit = key == column
                at_col = layer * lat_width + chunk * LANES
                code_ref[pl.ds(row, block), at_col : at_col + LANES] = jnp.where(
                    hit, lane_pick(value, spot), 0.0
                ).astype(BF16)
                back_ref[pl.ds(row, block), at_col : at_col + LANES] = jnp.where(
                    hit, lane_pick(grad, spot), 0.0
                ).astype(BF16)
        return carry

    lax.fori_loop(0, shards * tokens // block, spread, 0)

    @pl.when(step == 0)
    def _():
        sum_ref[...] = jnp.zeros_like(sum_ref)

    cot = jnp.concatenate([low_ref[shard, 0 : 2 * cols, :] for shard in range(shards)], axis=1)
    res = jnp.concatenate([high_ref[shard, tokens : tokens + 2 * cols, :] for shard in range(shards)], axis=1)
    dot = functools.partial(jnp.dot, preferred_element_type=F32)
    sum_ref[0 : 2 * cols, :] += dot(cot, code_ref[:, 0:lat_width])
    sum_ref[2 * cols : 3 * cols, :] += dot(cot[cols:], code_ref[:, lat_width:])
    sum_ref[3 * cols : 4 * cols, :] += dot(res[0:cols], back_ref[:, 0:lat_width])
    sum_ref[4 * cols : 5 * cols, :] += dot(res[cols:], back_ref[:, lat_width:])

    @pl.when(step == pl.num_programs(0) - 1)
    def _():
        first_ref[0] = sum_ref[0:cols, :].astype(BF16)
        first_ref[1] = sum_ref[cols : 2 * cols, :].astype(BF16)
        second_ref[...] = sum_ref[2 * cols : 3 * cols, :].astype(BF16)
        enc_ref[0] = sum_ref[3 * cols : 4 * cols, :].astype(BF16)
        enc_ref[1] = sum_ref[4 * cols : 5 * cols, :].astype(BF16)


def weight_grads(got, grads, cols, lat_width):
    parts, rows, tokens = got.shape
    shards = 4
    return pl.pallas_call(
        weights_kernel,
        grid=(parts // shards,),
        in_specs=[
            pl.BlockSpec((shards, rows // 2, tokens), lambda i: (i, 0, 0)),
            pl.BlockSpec((shards, rows // 2, tokens), lambda i: (i, 1, 0)),
            pl.BlockSpec((shards, tokens, LANES), lambda i: (i, 0, 0)),
        ],
        out_specs=[
            pl.BlockSpec((2, cols, lat_width), lambda i: (0, 0, 0)),
            pl.BlockSpec((cols, lat_width), lambda i: (0, 0)),
            pl.BlockSpec((2, cols, lat_width), lambda i: (0, 0, 0)),
        ],
        out_shape=[
            jax.ShapeDtypeStruct((2, cols, lat_width), BF16),
            jax.ShapeDtypeStruct((cols, lat_width), BF16),
            jax.ShapeDtypeStruct((2, cols, lat_width), BF16),
        ],
        scratch_shapes=[
            pltpu.VMEM((shards * tokens, 2 * lat_width), BF16),
            pltpu.VMEM((shards * tokens, 2 * lat_width), BF16),
            pltpu.VMEM((5 * cols, lat_width), F32),
        ],
        compiler_params=grant(40),
        cost_estimate=cost(2 * parts * tokens * cols * 5 * lat_width, 8 << 20),
    )(got, got, grads)


def exchange(array, axis):
    return lax.all_to_all(array, axis, 0, 0, tiled=True)


def union(part, axis, size):
    reach = 1
    while reach < size:
        others = [
            lax.ppermute(part, axis, [(at, at ^ (reach * hop)) for at in range(size)])
            for hop in (1, 2, 3)
            if reach * hop < size
        ]
        for other in others:
            part = part + other
        reach *= 4
    return part


def shards(layers, parts, residual, cotangent, decoder_first, decoder_second, latent_index, latent_value, active_count):
    lat_width = decoder_first.shape[0]
    cols = decoder_second.shape[1]
    start = (lax.axis_index("layer") * lat_width).astype(jnp.int32).reshape(1)
    packed, rank = pack(
        start,
        cotangent,
        residual,
        latent_index.transpose(0, 2, 1),
        latent_value.transpose(0, 2, 1),
        active_count,
        lat_width,
        parts,
    )
    got = exchange(packed, "dp")
    terms = slot_terms(decoder_first.transpose(1, 2, 0), decoder_second.T, got)
    grads, part = slot_totals(exchange(terms, "dp"), rank)
    all_grads = exchange(grads, "dp")
    first_grad, second_grad, encoder_grad = weight_grads(got, all_grads, cols, lat_width)
    latent_grad = union(part, "layer", layers)
    return (
        first_grad.transpose(2, 0, 1),
        second_grad.T,
        encoder_grad.transpose(1, 0, 2),
        latent_grad.astype(F32).transpose(0, 2, 1),
    )


def solution(mesh):
    return jax.shard_map(
        functools.partial(shards, mesh.shape["layer"], mesh.shape["dp"]),
        mesh=mesh,
        in_specs=(
            P(None, "dp", None),
            P(None, "dp", None),
            P("layer", None, "dp"),
            P("layer", "dp"),
            P(None, "dp", None),
            P(None, "dp", None),
            P(None, "dp"),
        ),
        out_specs=(
            P("layer", None, "dp"),
            P("layer", "dp"),
            P("dp", None, "layer"),
            P(None, "dp", None),
        ),
        check_vma=False,
    )
```

time: 542 us -> 200 us (0.37)
  waiting for transfers between devices: 350 us -> 5.82 us
  Pallas kernels: 0 us -> 85.9 us
  local copies, waits for them, and re-layouts: 67.3 us -> 11 us
  other arithmetic: 26.5 us -> 0.65 us
  matrix products: 18.5 us -> 0 us
  starting transfers between devices: 0.3 us -> 18.2 us
  blocking collectives: 63.1 us -> 77.2 us
  between operations: 14.6 us -> 0.73 us
    unnamed x5 -> x0, waiting for transfers between devices: 261 us -> none
    all_gather x1 -> x0, waiting for transfers between devices: 88.9 us -> none  [shards(): weight_piece = lax.all_gather(stacked, 'dp', axis=2, tiled=True)]
    pallas_call x0 -> x4, Pallas kernels: none -> 85.9 us  [the longest x1 77 us: weight_grads(): pl.pallas_call(weights_kernel, grid=(parts // shards,), in_specs=[pl.Bloc...]
    all_to_all x0 -> x2, blocking collectives: none -> 77.2 us  [exchange(): return lax.all_to_all(array, axis, 0, 0, tiled=True)]
    psum x1 -> x0, blocking collectives: 63.1 us -> none  [shards(): lax.psum(slot_part.astype(jnp.bfloat16), 'layer').astype(jnp.float32)]
    unnamed x17 -> x19, local copies, waits for them, and re-layouts: 44.8 us -> 11 us
    convert_element_type x4 -> x0, local copies, waits for them, and re-layouts: 19.6 us -> none  [the longest x1 18.7 us: shards(): encoder_part = lax.psum_scatter(jnp.einsum('atd,atr->dar', residual, late...]
    dot_general x6 -> x0, matrix products: 18.5 us -> none  [the longest x3 10.3 us: contract_last(): lax.dot_general(left_side, right_side, (((1,), (1,)), ((), ())), preferre...]
  transfers between devices with their start and end apart: 3 -> 7, of which waited for: 3 -> 1; matrix products, arithmetic and copies ran while one was open for 10% -> 0% of each run, Pallas kernels for 0% -> 0%
where the time goes in v1:
time: 200 us
  Pallas kernels  85.9 us (43%)
  blocking collectives  77.2 us (39%)
  starting transfers between devices  18.2 us (9%)
  local copies, waits for them, and re-layouts  11 us (6%)
  waiting for transfers between devices  5.82 us (3%)
    all_to_all x2, blocking collectives, exchange(): return lax.all_to_all(array, axis, 0, 0, tiled=True)  77.2 us
    pallas_call x1, Pallas kernels, weight_grads(): pl.pallas_call(weights_kernel, grid=(parts // shards,), in_specs=[pl.Bloc...  77 us
    ppermute x6, starting transfers between devices, union(): lax.ppermute(part, axis, [(at, at ^ reach * hop) for at in range(size)])  12.3 us
    unnamed x19, local copies, waits for them, and re-layouts  11 us
    all_to_all x1, starting transfers between devices, exchange(): return lax.all_to_all(array, axis, 0, 0, tiled=True)  5.89 us
    ppermute x6, waiting for transfers between devices, union(): lax.ppermute(part, axis, [(at, at ^ reach * hop) for at in range(size)])  5.82 us
    pallas_call x1, Pallas kernels, slot_terms(): pl.pallas_call(terms_kernel, grid=(parts // shards,), in_specs=[pl.BlockS...  5.25 us
  transfers between devices with their start and end apart: 7, of which 1 were waited for; matrix products, arithmetic and copies ran while one was open for 0% of the time, Pallas kernels for 0%

profile of v1, /device:TPU:2, one launch (start us, length us, event | category | flops | bytes accessed | tf_op | source)
XLA Modules:
  0.0 199.6 jit_solution(3971908759055348418)
XLA Ops:
  0.6 1.5 copy-done.2
  2.1 1.5 copy-done.3
  3.6 0.8 copy-done.6
  4.5 0.8 copy-done.7
  5.2 0.7 copy-done.8
  5.9 2.7 %shard_map.102 = (bf16[16,1152,128]{2,1,0:T(8,128)(2,1)S(1)}, s32[2,64,128]{2,1,0:T(8,128)S(1)}) custom-call(s32[1]{0:T(128)} %bitcast.start_ref, bf16[2,128,3584]{2,1,0:T(8,128)(2,1)S(1)} %copy-done.2, bf16[2,128,3584]{2,1,0:T(8,128)(2,1)S(1)} %copy-done.3, s32[2,64,128]{2,1,0:T(8,128)S(1)} %bitcast.13, bf16[2,64,128]{2,1,0:T(8,128)(2,1)S(1)} %bitcast.14, ...), custom_call_target="tpu_custom_call" | custom-call | bytes 10485760 | tf_op jit(solution)/shard_map/pallas_call | solution.py:78
  8.6 0.0 copy-start.4
  8.7 62.3 %all_to_all.15.got_ref.low_ref.high_ref = bf16[16,1152,128]{2,1,0:T(8,128)(2,1)S(1)} all-to-all(bf16[16,1152,128]{2,1,0:T(8,128)(2,1)S(1)} %get-tuple-element.11), channel_id=1, replica_groups=mesh['layer'=16,'dp'=16] {'dp'}, dimensions={0} | all-to-all | bytes 9437184 | tf_op jit(solution)/shard_map/all_to_all | solution.py:276
  71.0 5.2 %shard_map.103 = bf16[16,128,128]{2,1,0:T(8,128)(2,1)S(1)} custom-call(bf16[2,224,512]{2,1,0:T(8,128)(2,1)S(1)} %bitcast.10, bf16[224,512]{1,0:T(8,128)(2,1)S(1)} %bitcast.12, bf16[16,1152,128]{2,1,0:T(8,128)(2,1)S(1)} %all_to_all.15.got_ref.low_ref.high_ref), custom_call_target="tpu_custom_call" | custom-call | flops 1409286144 | bytes 6291456 | tf_op jit(solution)/shard_map/pallas_call | solution.py:139
  76.3 2.1 %copy-done = bf16[16,1152,128]{2,1,0:T(8,128)(2,1)} copy-done((bf16[16,1152,128]{2,1,0:T(8,128)(2,1)}, bf16[16,1152,128]{2,1,0:T(8,128)(2,1)S(1)}, u32[]{:S(2)}) %copy-start) | copy-done | bytes 4718616
  78.4 14.9 %all_to_all.16.got_ref = bf16[16,128,128]{2,1,0:T(8,128)(2,1)S(1)} all-to-all(bf16[16,128,128]{2,1,0:T(8,128)(2,1)S(1)} %shard_map.103), channel_id=1, replica_groups=mesh['layer'=16,'dp'=16] {'dp'}, dimensions={0} | all-to-all | bytes 1048576 | tf_op jit(solution)/shard_map/all_to_all | solution.py:276
  93.3 0.9 shard_map.104
  94.2 2.1 %collective-permute-start.2 = (bf16[2,64,128]{2,1,0:T(8,128)(2,1)S(1)}, bf16[2,64,128]{2,1,0:T(8,128)(2,1)S(1)}, u32[]{:S(2)}, u32[]{:S(2)}) collective-permute-start(bf16[2,64,128]{2,1,0:T(8,128)(2,1)S(1)} %get-tuple-element.17), channel_id=1, source_target_pairs={{0,48},{16,32},{32,16},{48,0},{64,112},{80,96},{96,80},{112,64},{1... | collective-permute-start | bytes 98312 | tf_op jit(solution)/shard_map/ppermute | solution.py:283
  96.3 0.1 collective-permute-start.1
  96.3 1.3 collective-permute-start
  97.7 5.9 %all-to-all-start.2 = ((bf16[16,128,128]{2,1,0:T(8,128)(2,1)}), bf16[16,128,128]{2,1,0:T(8,128)(2,1)S(1)}, u32[]{:S(2)}, u32[]{:S(2)}) async-start(bf16[16,128,128]{2,1,0:T(8,128)(2,1)} %get-tuple-element.13), calls=%async_computation.2 | async-start | bytes 1048576 | tf_op jit(solution)/shard_map/all_to_all | solution.py:276
  103.6 6.4 %collective-permute-start.5 = (bf16[2,64,128]{2,1,0:T(8,128)(2,1)S(1)}, bf16[2,64,128]{2,1,0:T(8,128)(2,1)S(1)}, u32[]{:S(2)}, u32[]{:S(2)}) collective-permute-start(bf16[2,64,128]{2,1,0:T(8,128)(2,1)S(1)} %add_add_fusion), channel_id=1, source_target_pairs={{0,192},{16,208},{32,224},{48,240},{64,128},{80,144},{96,160},{112... | collective-permute-start | bytes 98312 | tf_op jit(solution)/shard_map/ppermute | solution.py:283
  110.0 1.0 collective-permute-start.4
  111.0 1.5 collective-permute-start.3
  112.5 5.8 %collective-permute-done.4 = bf16[2,64,128]{2,1,0:T(8,128)(2,1)S(1)} collective-permute-done((bf16[2,64,128]{2,1,0:T(8,128)(2,1)S(1)}, bf16[2,64,128]{2,1,0:T(8,128)(2,1)S(1)}, u32[]{:S(2)}, u32[]{:S(2)}) %collective-permute-start.4) | collective-permute-done | bytes 32800 | tf_op jit(solution)/shard_map/ppermute | solution.py:283
  118.3 0.6 convert_bitcast_fusion
  118.9 2.3 %copy-done.1 = bf16[16,1152,128]{2,1,0:T(8,128)(2,1)S(1)} copy-done((bf16[16,1152,128]{2,1,0:T(8,128)(2,1)S(1)}, bf16[16,1152,128]{2,1,0:T(8,128)(2,1)}, u32[]{:S(2)}) %copy-start.1) | copy-done | bytes 4718616
  121.3 77.0 %shard_map.105 = (bf16[2,224,512]{2,1,0:T(8,128)(2,1)}, bf16[224,512]{1,0:T(8,128)(2,1)}, bf16[2,224,512]{2,1,0:T(8,128)(2,1)S(1)}) custom-call(bf16[16,1152,128]{2,1,0:T(8,128)(2,1)S(1)} %copy-done.1, bf16[16,1152,128]{2,1,0:T(8,128)(2,1)S(1)} %copy-done.1, bf16[16,128,128]{2,1,0:T(8,128)(2,1)S(1)} %all-to-all-done.2.grad_ref), custom_call_target="tpu_custom_call" | custom-call | flops 2348810240 | bytes 8388608 | tf_op jit(solution)/shard_map/pallas_call | solution.py:247
  198.3 1.2 copy.11
  (17 shorter events, 0.0 us)
Async XLA Ops:
  0.6 1.5 copy-start.2
  2.1 1.5 copy-start.3
  3.6 0.8 copy-start.6
  4.5 0.8 copy-start.7
  5.2 0.7 copy-start.8
  8.6 62.4 %copy-start.4 = (bf16[512,2,224]{0,2,1:T(8,128)(2,1)S(1)}, bf16[512,2,224]{0,2,1:T(8,128)(2,1)}, u32[]{:S(2)}) copy-start(bf16[512,2,224]{0,2,1:T(8,128)(2,1)} %param.9) | copy-start | bytes 1376260
  8.6 62.4 %copy-start.5 = (bf16[512,224]{0,1:T(8,128)(2,1)S(1)}, bf16[512,224]{0,1:T(8,128)(2,1)}, u32[]{:S(2)}) copy-start(bf16[512,224]{0,1:T(8,128)(2,1)} %param.10) | copy-start | bytes 688132
  76.3 2.1 %copy-start = (bf16[16,1152,128]{2,1,0:T(8,128)(2,1)}, bf16[16,1152,128]{2,1,0:T(8,128)(2,1)S(1)}, u32[]{:S(2)}) copy-start(bf16[16,1152,128]{2,1,0:T(8,128)(2,1)S(1)} %all_to_all.15.got_ref.low_ref.high_ref) | copy-start | bytes 14155780
  94.2 9.4 %collective-permute-start.2 = (bf16[2,64,128]{2,1,0:T(8,128)(2,1)S(1)}, bf16[2,64,128]{2,1,0:T(8,128)(2,1)S(1)}, u32[]{:S(2)}, u32[]{:S(2)}) collective-permute-start(bf16[2,64,128]{2,1,0:T(8,128)(2,1)S(1)} %get-tuple-element.17), channel_id=1, source_target_pairs={{0,48},{16,32},{32,16},{48,0},{64,112},{80,96},{96,80},{112,64},{1... | collective-permute-start | bytes 98312 | tf_op jit(solution)/shard_map/ppermute | solution.py:283
  96.3 7.3 %collective-permute-start.1 = (bf16[2,64,128]{2,1,0:T(8,128)(2,1)S(1)}, bf16[2,64,128]{2,1,0:T(8,128)(2,1)S(1)}, u32[]{:S(2)}, u32[]{:S(2)}) collective-permute-start(bf16[2,64,128]{2,1,0:T(8,128)(2,1)S(1)} %get-tuple-element.17), channel_id=1, source_target_pairs={{0,32},{16,48},{32,0},{48,16},{64,96},{80,112},{96,64},{112,80},{1... | collective-permute-start | bytes 98312 | tf_op jit(solution)/shard_map/ppermute | solution.py:283
  96.3 7.3 %collective-permute-start = (bf16[2,64,128]{2,1,0:T(8,128)(2,1)S(1)}, bf16[2,64,128]{2,1,0:T(8,128)(2,1)S(1)}, u32[]{:S(2)}, u32[]{:S(2)}) collective-permute-start(bf16[2,64,128]{2,1,0:T(8,128)(2,1)S(1)} %get-tuple-element.17), channel_id=1, source_target_pairs={{0,16},{16,0},{32,48},{48,32},{64,80},{80,64},{96,112},{112,96},{1... | collective-permute-start | bytes 98312 | tf_op jit(solution)/shard_map/ppermute | solution.py:283
  97.7 21.3 %all-to-all-start.2 = ((bf16[16,128,128]{2,1,0:T(8,128)(2,1)}), bf16[16,128,128]{2,1,0:T(8,128)(2,1)S(1)}, u32[]{:S(2)}, u32[]{:S(2)}) async-start(bf16[16,128,128]{2,1,0:T(8,128)(2,1)} %get-tuple-element.13), calls=%async_computation.2 | async-start | bytes 1048576 | tf_op jit(solution)/shard_map/all_to_all | solution.py:276
  103.6 8.9 %collective-permute-start.5 = (bf16[2,64,128]{2,1,0:T(8,128)(2,1)S(1)}, bf16[2,64,128]{2,1,0:T(8,128)(2,1)S(1)}, u32[]{:S(2)}, u32[]{:S(2)}) collective-permute-start(bf16[2,64,128]{2,1,0:T(8,128)(2,1)S(1)} %add_add_fusion), channel_id=1, source_target_pairs={{0,192},{16,208},{32,224},{48,240},{64,128},{80,144},{96,160},{112... | collective-permute-start | bytes 98312 | tf_op jit(solution)/shard_map/ppermute | solution.py:283
  110.0 8.3 %collective-permute-start.4 = (bf16[2,64,128]{2,1,0:T(8,128)(2,1)S(1)}, bf16[2,64,128]{2,1,0:T(8,128)(2,1)S(1)}, u32[]{:S(2)}, u32[]{:S(2)}) collective-permute-start(bf16[2,64,128]{2,1,0:T(8,128)(2,1)S(1)} %add_add_fusion), channel_id=1, source_target_pairs={{0,128},{16,144},{32,160},{48,176},{64,192},{80,208},{96,224},{112... | collective-permute-start | bytes 98312 | tf_op jit(solution)/shard_map/ppermute | solution.py:283
  111.0 7.3 %collective-permute-start.3 = (bf16[2,64,128]{2,1,0:T(8,128)(2,1)S(1)}, bf16[2,64,128]{2,1,0:T(8,128)(2,1)S(1)}, u32[]{:S(2)}, u32[]{:S(2)}) collective-permute-start(bf16[2,64,128]{2,1,0:T(8,128)(2,1)S(1)} %add_add_fusion), channel_id=1, source_target_pairs={{0,64},{16,80},{32,96},{48,112},{64,0},{80,16},{96,32},{112,48},{1... | collective-permute-start | bytes 98312 | tf_op jit(solution)/shard_map/ppermute | solution.py:283
  118.9 2.3 %copy-start.1 = (bf16[16,1152,128]{2,1,0:T(8,128)(2,1)S(1)}, bf16[16,1152,128]{2,1,0:T(8,128)(2,1)}, u32[]{:S(2)}) copy-start(bf16[16,1152,128]{2,1,0:T(8,128)(2,1)} %copy-done) | copy-start | bytes 14155780

commit v2 on v1

v2 whole, which is shorter than its diff:
```python
import functools
import jax
import jax.numpy as jnp
from jax import lax
from jax.experimental import pallas as pl
from jax.experimental.pallas import tpu as pltpu
from jax.sharding import PartitionSpec as P

BF16 = jnp.bfloat16
F32 = jnp.float32
LANES = 128
SHIFT = 256
EMPTY = 512
PACK_MIB = 60


def grant(mib):
    return pltpu.CompilerParams(vmem_limit_bytes=mib << 20)


def cost(flops, moved):
    return pl.CostEstimate(flops=flops, bytes_accessed=moved, transcendentals=0)


def lane_pick(table, where):
    return jnp.take_along_axis(table, where, axis=1, mode="promise_in_bounds")


def turn(source_ref, out_ref, layer, base):
    dests = out_ref.shape[0]
    cols = source_ref.shape[2] // dests
    turned = source_ref[layer].T
    for dest in range(dests):
        out_ref[dest, base + layer * cols : base + (layer + 1) * cols, :] = turned[dest * cols : (dest + 1) * cols]


def kept_slots(start_ref, idx_ref, live_ref, layer, lat_width):
    slots, tokens = idx_ref.shape[1:]
    place = lax.broadcasted_iota(jnp.int32, (slots, tokens), 0)
    local = idx_ref[layer] - start_ref[0]
    inside = (place < live_ref[layer : layer + 1, :]) & (local >= 0) & (local < lat_width)
    return place, local, inside


def pack_first_kernel(lat_width, start_ref, cot_ref, idx_ref, live_ref, out_ref, rank_ref, slot_ref):
    slots, tokens = idx_ref.shape[1:]
    dests = out_ref.shape[0]
    cols = cot_ref.shape[2] // dests

    @pl.when(pl.program_id(0) == 0)
    def _():
        found = []
        for layer in range(2):
            place, local, inside = kept_slots(start_ref, idx_ref, live_ref, layer, lat_width)
            key = jnp.where(inside, local, 1 << 20)
            rank = jnp.zeros((slots, tokens), jnp.int32)
            for slot in range(slots):
                rank = rank + jnp.where(key[slot : slot + 1, :] < key, 1, 0)
            rank = jnp.where(inside, rank, slots)
            rank_ref[layer] = rank
            key = local - SHIFT
            held = jnp.full((slots, tokens), EMPTY, jnp.int32)
            for slot in range(slots):
                held = jnp.where(rank[slot : slot + 1, :] == place, key[slot : slot + 1, :], held)
            found.append(held.astype(F32))
        slot_ref[...] = jnp.concatenate(found, axis=0).T.astype(BF16)

    for layer in range(2):
        turn(cot_ref, out_ref, layer, 0)
    for dest in range(dests):
        out_ref[dest, 2 * cols :, :] = slot_ref[...]


def pack_second_kernel(lat_width, start_ref, res_ref, idx_ref, val_ref, live_ref, rank_ref, out_ref, slot_ref):
    slots, tokens = idx_ref.shape[1:]
    dests = out_ref.shape[0]

    @pl.when(pl.program_id(0) == 0)
    def _():
        codes, runs = [], []
        for layer in range(2):
            place, local, inside = kept_slots(start_ref, idx_ref, live_ref, layer, lat_width)
            rank = rank_ref[layer]
            value = val_ref[layer].astype(F32)
            run = jnp.where(inside, local >> 3, lat_width)
            bit = jnp.left_shift(1, local & 7)
            code = jnp.zeros((slots, tokens), F32)
            bits = jnp.zeros((slots, tokens), jnp.int32)
            for slot in range(slots):
                code = jnp.where(rank[slot : slot + 1, :] == place, value[slot : slot + 1, :], code)
                bits = bits + jnp.where(run[slot : slot + 1, :] == place, bit[slot : slot + 1, :], 0)
            codes.append(code)
            runs.append(bits.astype(F32))
        slot_ref[0:tokens, :] = jnp.concatenate(codes, axis=0).T.astype(BF16)
        slot_ref[tokens:, :] = jnp.concatenate(runs, axis=0).T.astype(BF16)

    for layer in range(2):
        turn(res_ref, out_ref, layer, 2 * tokens)
    for dest in range(dests):
        out_ref[dest, 0 : 2 * tokens, :] = slot_ref[...]


def pack(kernel, lat_width, parts, more, start, wide, *small):
    _, tokens, width = wide.shape
    steps = 4
    rows = 2 * (width // parts) + more * tokens
    out_specs = [pl.BlockSpec((parts // steps, rows, tokens), lambda i: (i, 0, 0))]
    out_shape = [jax.ShapeDtypeStruct((parts, rows, tokens), BF16)]
    if more == 1:
        out_specs.append(pl.BlockSpec(small[0].shape, lambda i: (0, 0, 0)))
        out_shape.append(jax.ShapeDtypeStruct(small[0].shape, jnp.int32))
    return pl.pallas_call(
        functools.partial(kernel, lat_width),
        grid=(steps,),
        in_specs=[
            pl.BlockSpec(memory_space=pltpu.SMEM),
            pl.BlockSpec((2, tokens, width // steps), lambda i: (0, 0, i)),
        ]
        + [pl.BlockSpec(array.shape, lambda i, rank=array.ndim: (0,) * rank) for array in small],
        out_specs=out_specs,
        out_shape=out_shape,
        scratch_shapes=[pltpu.VMEM((more * tokens, LANES), BF16)],
        compiler_params=grant(PACK_MIB),
        cost_estimate=cost(0, 5 << 20),
    )(start, wide, *small)


def terms_kernel(wf_ref, ws_ref, got_ref, out_ref, weight_ref):
    shards, _, tokens = got_ref.shape
    cols, lat_width = ws_ref.shape

    @pl.when(pl.program_id(0) == 0)
    def _():
        weight_ref[0:cols, 0:lat_width] = wf_ref[0]
        weight_ref[cols : 2 * cols, 0:lat_width] = wf_ref[1]
        weight_ref[0:cols, lat_width:] = jnp.zeros((cols, lat_width), BF16)
        weight_ref[cols : 2 * cols, lat_width:] = ws_ref[...]

    for shard in range(shards):
        dense = lax.dot_general(
            got_ref[shard, 0 : 2 * cols, :].T,
            weight_ref[...],
            (((1,), (0,)), ((), ())),
            preferred_element_type=F32,
        )
        held = got_ref[shard, 2 * cols : 2 * cols + tokens, :].astype(F32).astype(jnp.int32) + SHIFT
        lane = lax.broadcasted_iota(jnp.int32, held.shape, 1)
        chunks = lat_width // LANES
        chunk = jnp.where(
            held < lat_width, (held >> 7) + jnp.where(lane >= LANES // 2, chunks, 0), 2 * chunks
        )
        within = held & (LANES - 1)
        picked = jnp.zeros(held.shape, F32)
        for part in range(2 * chunks):
            table = dense[:, part * LANES : (part + 1) * LANES]
            picked = jnp.where(chunk == part, lane_pick(table, within), picked)
        out_ref[shard] = picked.astype(BF16)


def slot_terms(first, second, got):
    parts, rows, tokens = got.shape
    cols, lat_width = second.shape
    shards = 2
    return pl.pallas_call(
        terms_kernel,
        grid=(parts // shards,),
        in_specs=[
            pl.BlockSpec((2, cols, lat_width), lambda i: (0, 0, 0)),
            pl.BlockSpec((cols, lat_width), lambda i: (0, 0)),
            pl.BlockSpec((shards, rows, tokens), lambda i: (i, 0, 0)),
        ],
        out_specs=pl.BlockSpec((shards, tokens, LANES), lambda i: (i, 0, 0)),
        out_shape=jax.ShapeDtypeStruct((parts, tokens, LANES), BF16),
        scratch_shapes=[pltpu.VMEM((2 * cols, 2 * lat_width), BF16)],
        compiler_params=grant(40),
        cost_estimate=cost(2 * parts * tokens * cols * 3 * lat_width, 6 << 20),
    )(first, second, got)


def total_kernel(got_ref, rank_ref, grad_ref, part_ref):
    total = jnp.sum(got_ref[...].astype(F32), axis=0)
    for dest in range(grad_ref.shape[0]):
        grad_ref[dest] = total.astype(BF16)
    turned = total.T
    slots = rank_ref.shape[1]
    for layer in range(2):
        rank = rank_ref[layer]
        part = jnp.zeros(rank.shape, F32)
        for slot in range(slots):
            row = layer * slots + slot
            part = jnp.where(rank == slot, turned[row : row + 1, :], part)
        part_ref[layer] = part.astype(BF16)


def slot_totals(got, rank):
    parts, tokens, _ = got.shape
    return pl.pallas_call(
        total_kernel,
        out_shape=[
            jax.ShapeDtypeStruct(got.shape, BF16),
            jax.ShapeDtypeStruct(rank.shape, BF16),
        ],
        compiler_params=grant(40),
        cost_estimate=cost(0, 1 << 20),
    )(got, rank)


def codes_kernel(low_ref, high_ref, first_ref, second_ref, spot_ref, code_ref, map_ref, sum_ref):
    shards, _, tokens = low_ref.shape
    cols, lat_width = second_ref.shape
    step = pl.program_id(0)
    runs = lat_width // 8
    block = 32

    @pl.when(step == 0)
    def _():
        sum_ref[...] = jnp.zeros_like(sum_ref)
        row = lax.broadcasted_iota(jnp.int32, map_ref.shape, 0)
        col = lax.broadcasted_iota(jnp.int32, map_ref.shape, 1)
        same = ((row // runs) % 2) == (col // lat_width)
        own, mine = row % runs, (col % lat_width) // 8
        weight = jnp.where(row < 2 * runs, jnp.where(own == mine, LANES, 0), jnp.where(own < mine, 1, 0))
        map_ref[...] = jnp.where(same, weight, 0).astype(F32).astype(BF16)

    for shard in range(shards):
        bits = high_ref[shard, tokens : 2 * tokens, :].astype(F32).astype(jnp.int32)
        held = lax.population_count(bits).astype(F32)
        both = jnp.concatenate([bits.astype(F32).astype(BF16), held.astype(BF16)], axis=1)
        spot_ref[shard] = jnp.dot(both, map_ref[...], preferred_element_type=F32).astype(jnp.int32)

    lane = lax.broadcasted_iota(jnp.int32, (block, LANES), 1)
    self_bit = jnp.left_shift(1, lane & 7)

    def spread(at, carry):
        shard = at // (tokens // block)
        low = pl.multiple_of((at % (tokens // block)) * block, block)
        row = pl.multiple_of(at * block, block)
        value = high_ref[shard, pl.ds(low, block), :].astype(F32)
        for chunk in range(2 * lat_width // LANES):
            base = (chunk * LANES // lat_width) * (LANES // 2)
            packed = spot_ref[shard, pl.ds(low, block), chunk * LANES : (chunk + 1) * LANES]
            bits = packed >> 7
            spot = (packed & (LANES - 1)) + lax.population_count(bits & (self_bit - 1)) + base
            spot = jnp.where((bits & self_bit) != 0, spot, LANES)
            spot_ref[shard, pl.ds(low, block), chunk * LANES : (chunk + 1) * LANES] = spot
            code = jnp.where(spot < LANES, lane_pick(value, spot & (LANES - 1)), 0.0)
            code_ref[pl.ds(row, block), chunk * LANES : (chunk + 1) * LANES] = code.astype(BF16)
        return carry

    lax.fori_loop(0, shards * tokens // block, spread, 0)

    cot = jnp.concatenate([low_ref[shard, 0 : 2 * cols, :] for shard in range(shards)], axis=1)
    dot = functools.partial(jnp.dot, preferred_element_type=F32)
    sum_ref[0 : 2 * cols, :] += dot(cot, code_ref[:, 0:lat_width])
    sum_ref[2 * cols : 3 * cols, :] += dot(cot[cols:], code_ref[:, lat_width:])

    @pl.when(step == pl.num_programs(0) - 1)
    def _():
        first_ref[0] = sum_ref[0:cols, :].astype(BF16)
        first_ref[1] = sum_ref[cols : 2 * cols, :].astype(BF16)
        second_ref[...] = sum_ref[2 * cols : 3 * cols, :].astype(BF16)


def decoder_grads(low, high, cols, lat_width):
    parts, _, tokens = low.shape
    shards = 4
    return pl.pallas_call(
        codes_kernel,
        grid=(parts // shards,),
        in_specs=[
            pl.BlockSpec((shards,) + low.shape[1:], lambda i: (i, 0, 0)),
            pl.BlockSpec((shards, 2 * tokens, tokens), lambda i: (i, 0, 0)),
        ],
        out_specs=[
            pl.BlockSpec((2, cols, lat_width), lambda i: (0, 0, 0)),
            pl.BlockSpec((cols, lat_width), lambda i: (0, 0)),
            pl.BlockSpec((shards, tokens, 2 * lat_width), lambda i: (i, 0, 0)),
        ],
        out_shape=[
            jax.ShapeDtypeStruct((2, cols, lat_width), BF16),
            jax.ShapeDtypeStruct((cols, lat_width), BF16),
            jax.ShapeDtypeStruct((parts, tokens, 2 * lat_width), jnp.int32),
        ],
        scratch_shapes=[
            pltpu.VMEM((shards * tokens, 2 * lat_width), BF16),
            pltpu.VMEM((4 * lat_width // 8, 2 * lat_width), BF16),
            pltpu.VMEM((3 * cols, lat_width), F32),
        ],
        compiler_params=grant(40),
        cost_estimate=cost(2 * parts * tokens * cols * 3 * lat_width, 16 << 20),
    )(low, high)


def back_kernel(high_ref, spot_ref, grad_ref, enc_ref, back_ref, sum_ref):
    shards, _, tokens = high_ref.shape
    _, cols, lat_width = enc_ref.shape
    step = pl.program_id(0)
    block = 32

    def spread(at, carry):
        shard = at // (tokens // block)
        low = pl.multiple_of((at % (tokens // block)) * block, block)
        row = pl.multiple_of(at * block, block)
        grad = grad_ref[shard, pl.ds(low, block), :].astype(F32)
        for chunk in range(2 * lat_width // LANES):
            spot = spot_ref[shard, pl.ds(low, block), chunk * LANES : (chunk + 1) * LANES]
            back = jnp.where(spot < LANES, lane_pick(grad, spot & (LANES - 1)), 0.0)
            back_ref[pl.ds(row, block), chunk * LANES : (chunk + 1) * LANES] = back.astype(BF16)
        return carry

    lax.fori_loop(0, shards * tokens // block, spread, 0)

    @pl.when(step == 0)
    def _():
        sum_ref[...] = jnp.zeros_like(sum_ref)

    res = jnp.concatenate([high_ref[shard, 2 * tokens :, :] for shard in range(shards)], axis=1)
    dot = functools.partial(jnp.dot, preferred_element_type=F32)
    sum_ref[0:cols, :] += dot(res[0:cols], back_ref[:, 0:lat_width])
    sum_ref[cols:, :] += dot(res[cols:], back_ref[:, lat_width:])

    @pl.when(step == pl.num_programs(0) - 1)
    def _():
        enc_ref[0] = sum_ref[0:cols, :].astype(BF16)
        enc_ref[1] = sum_ref[cols:, :].astype(BF16)


def encoder_grads(high, spots, grads, cols, lat_width):
    parts, rows, tokens = high.shape
    shards = 4
    return pl.pallas_call(
        back_kernel,
        grid=(parts // shards,),
        in_specs=[
            pl.BlockSpec((shards, rows, tokens), lambda i: (i, 0, 0)),
            pl.BlockSpec((shards,) + spots.shape[1:], lambda i: (i, 0, 0)),
            pl.BlockSpec((shards, tokens, LANES), lambda i: (i, 0, 0)),
        ],
        out_specs=pl.BlockSpec((2, cols, lat_width), lambda i: (0, 0, 0)),
        out_shape=jax.ShapeDtypeStruct((2, cols, lat_width), BF16),
        scratch_shapes=[
            pltpu.VMEM((shards * tokens, 2 * lat_width), BF16),
            pltpu.VMEM((2 * cols, lat_width), F32),
        ],
        compiler_params=grant(40),
        cost_estimate=cost(2 * parts * tokens * cols * 2 * lat_width, 16 << 20),
    )(high, spots, grads)


def exchange(array, axis):
    return lax.all_to_all(array, axis, 0, 0, tiled=True)


def union(part, axis, size):
    reach = 1
    while reach < size:
        others = [
            lax.ppermute(part, axis, [(at, at ^ (reach * hop)) for at in range(size)])
            for hop in (1, 2, 3)
            if reach * hop < size
        ]
        for other in others:
            part = part + other
        reach *= 4
    return part


def shards(layers, parts, residual, cotangent, decoder_first, decoder_second, latent_index, latent_value, active_count):
    lat_width = decoder_first.shape[0]
    cols = decoder_second.shape[1]
    start = (lax.axis_index("layer") * lat_width).astype(jnp.int32).reshape(1)
    index, value = latent_index.transpose(0, 2, 1), latent_value.transpose(0, 2, 1)
    packed, rank = pack(pack_first_kernel, lat_width, parts, 1, start, cotangent, index, active_count)
    (later,) = pack(pack_second_kernel, lat_width, parts, 2, start, residual, index, value, active_count, rank)
    got = exchange(packed, "dp")
    later, got = lax.optimization_barrier((later, got))
    got_later = exchange(later, "dp")
    terms = slot_terms(decoder_first.transpose(1, 2, 0), decoder_second.T, got)
    grads, part = slot_totals(exchange(terms, "dp"), rank)
    all_grads = exchange(grads, "dp")
    first_grad, second_grad, spots = decoder_grads(got, got_later, cols, lat_width)
    encoder_grad = encoder_grads(got_later, spots, all_grads, cols, lat_width)
    latent_grad = union(part, "layer", layers)
    return (
        first_grad.transpose(2, 0, 1),
        second_grad.T,
        encoder_grad.transpose(1, 0, 2),
        latent_grad.astype(F32).transpose(0, 2, 1),
    )


def solution(mesh):
    return jax.shard_map(
        functools.partial(shards, mesh.shape["layer"], mesh.shape["dp"]),
        mesh=mesh,
        in_specs=(
            P(None, "dp", None),
            P(None, "dp", None),
            P("layer", None, "dp"),
            P("layer", "dp"),
            P(None, "dp", None),
            P(None, "dp", None),
            P(None, "dp"),
        ),
        out_specs=(
            P("layer", None, "dp"),
            P("layer", "dp"),
            P("dp", None, "layer"),
            P(None, "dp", None),
        ),
        check_vma=False,
    )
```

time: 200 us -> 170 us (0.85)
  blocking collectives: 77.2 us -> 17 us
  waiting for transfers between devices: 5.82 us -> 62.3 us
  Pallas kernels: 85.9 us -> 43.4 us
  starting transfers between devices: 18.2 us -> 34.8 us
    all_to_all x2 -> x1, blocking collectives: 77.2 us -> 17 us  [exchange(): return lax.all_to_all(array, axis, 0, 0, tiled=True)]
    all_to_all x1 -> x3, waiting for transfers between devices: 0.01 us -> 56.4 us  [exchange(): return lax.all_to_all(array, axis, 0, 0, tiled=True)]
    pallas_call x2 -> x4, Pallas kernels: 79.8 us -> 38 us  [the longest x1 15.7 us: decoder_grads(): pl.pallas_call(codes_kernel, grid=(parts // shards,), in_specs=[pl.BlockS...]
    all_to_all x1 -> x3, starting transfers between devices: 5.89 us -> 22.4 us  [exchange(): return lax.all_to_all(array, axis, 0, 0, tiled=True)]
    unnamed x19 -> x17, local copies, waits for them, and re-layouts: 11 us -> 10.4 us
  transfers between devices with their start and end apart: 7 -> 9, of which waited for: 1 -> 3; matrix products, arithmetic and copies ran while one was open for 0% -> 0% of each run, Pallas kernels for 0% -> 13%
where the time goes in v2:
time: 170 us; the launch traced here: 169 us
  waiting for transfers between devices  62.3 us (37%)
  Pallas kernels  43.4 us (26%)
  starting transfers between devices  34.8 us (20%)
  blocking collectives  17 us (10%)
  local copies, waits for them, and re-layouts  10.4 us (6%)
    all_to_all x3, waiting for transfers between devices, exchange(): return lax.all_to_all(array, axis, 0, 0, tiled=True)  56.4 us
    all_to_all x3, starting transfers between devices, exchange(): return lax.all_to_all(array, axis, 0, 0, tiled=True)  22.4 us
    all_to_all x1, blocking collectives, exchange(): return lax.all_to_all(array, axis, 0, 0, tiled=True)  17 us
    pallas_call x1, Pallas kernels, decoder_grads(): pl.pallas_call(codes_kernel, grid=(parts // shards,), in_specs=[pl.BlockS...  15.7 us
    ppermute x6, starting transfers between devices, union(): lax.ppermute(part, axis, [(at, at ^ reach * hop) for at in range(size)])  12.3 us
    pallas_call x1, Pallas kernels, encoder_grads(): pl.pallas_call(back_kernel, grid=(parts // shards,), in_specs=[pl.BlockSp...  12 us
    unnamed x17, local copies, waits for them, and re-layouts  10.4 us
    pallas_call x2, Pallas kernels, pack(): pl.pallas_call(functools.partial(kernel, lat_width), grid=(steps,), in_sp...  10.4 us
  transfers between devices with their start and end apart: 9, of which 3 were waited for; matrix products, arithmetic and copies ran while one was open for 0% of the time, Pallas kernels for 13%

profile of v2, /device:TPU:2, one launch (start us, length us, event | category | flops | bytes accessed | tf_op | source)
XLA Modules:
  0.0 169.3 jit_solution(12175649641976606593)
XLA Ops:
  0.6 4.9 %shard_map.102 = (bf16[16,576,128]{2,1,0:T(8,128)(2,1)}, s32[2,64,128]{2,1,0:T(8,128)}) custom-call(s32[1]{0:T(128)} %bitcast.start_ref, bf16[2,128,3584]{2,1,0:T(8,128)(2,1)} %cot_ref.1, s32[2,64,128]{2,1,0:T(8,128)} %bitcast.13, s32[2,128]{1,0:T(2,128)} %live_ref.3), custom_call_target="tpu_custom_call" | custom-call | bytes 5242880 | tf_op jit(solution)/shard_map/pallas_call | solution.py:112
  5.6 7.5 %all-to-all-start = ((bf16[16,576,128]{2,1,0:T(8,128)(2,1)}), bf16[16,576,128]{2,1,0:T(8,128)(2,1)S(1)}, u32[]{:S(2)}, u32[]{:S(2)}) async-start(bf16[16,576,128]{2,1,0:T(8,128)(2,1)} %get-tuple-element.14), calls=%async_computation | async-start | bytes 4718592 | tf_op jit(solution)/shard_map/all_to_all | solution.py:351
  13.1 5.4 %shard_map.103 = bf16[16,704,128]{2,1,0:T(8,128)(2,1)} custom-call(s32[1]{0:T(128)} %bitcast.start_ref, bf16[2,128,3584]{2,1,0:T(8,128)(2,1)} %res_ref.1, s32[2,64,128]{2,1,0:T(8,128)} %bitcast.14, bf16[2,64,128]{2,1,0:T(8,128)(2,1)} %bitcast.15, s32[2,128]{1,0:T(2,128)} %live_ref.3, s32[2,64,128]{2,1,0:T(8,128)} %get-tuple-element.13.rank_ref), custom_call_target="tpu_custom_call" | custom-call | bytes 5242880 | tf_op jit(solution)/shard_map/pallas_call | solution.py:112
  18.5 25.0 %all-to-all-done.low_ref.got_ref = bf16[16,576,128]{2,1,0:T(8,128)(2,1)S(1)} async-done(((bf16[16,576,128]{2,1,0:T(8,128)(2,1)}), bf16[16,576,128]{2,1,0:T(8,128)(2,1)S(1)}, u32[]{:S(2)}, u32[]{:S(2)}) %all-to-all-start) | async-done | bytes 2359328 | tf_op jit(solution)/shard_map/all_to_all | solution.py:351
  43.5 5.0 %shard_map.105 = bf16[16,128,128]{2,1,0:T(8,128)(2,1)S(1)} custom-call(bf16[2,224,512]{2,1,0:T(8,128)(2,1)S(1)} %bitcast.11, bf16[224,512]{1,0:T(8,128)(2,1)S(1)} %bitcast.12, bf16[16,576,128]{2,1,0:T(8,128)(2,1)S(1)} %all-to-all-done.low_ref.got_ref), custom_call_target="tpu_custom_call" | custom-call | flops 1409286144 | bytes 6291456 | tf_op jit(solution)/shard_map/pallas_call | solution.py:164
  48.5 17.0 %all_to_all.20.got_ref = bf16[16,128,128]{2,1,0:T(8,128)(2,1)S(1)} all-to-all(bf16[16,128,128]{2,1,0:T(8,128)(2,1)S(1)} %shard_map.105), channel_id=1, replica_groups=mesh['layer'=16,'dp'=16] {'dp'}, dimensions={0} | all-to-all | bytes 1048576 | tf_op jit(solution)/shard_map/all_to_all | solution.py:351
  65.5 6.1 %all-to-all-start.1 = ((bf16[16,704,128]{2,1,0:T(8,128)(2,1)}), bf16[16,704,128]{2,1,0:T(8,128)(2,1)S(1)}, u32[]{:S(2)}, u32[]{:S(2)}) async-start(bf16[16,704,128]{2,1,0:T(8,128)(2,1)} %shard_map.103), calls=%async_computation.1 | async-start | bytes 5767168 | tf_op jit(solution)/shard_map/all_to_all | solution.py:351
  71.7 0.4 shard_map.106
  72.1 0.8 copy-done.4
  72.9 2.0 %collective-permute-start.2 = (bf16[2,64,128]{2,1,0:T(8,128)(2,1)S(1)}, bf16[2,64,128]{2,1,0:T(8,128)(2,1)S(1)}, u32[]{:S(2)}, u32[]{:S(2)}) collective-permute-start(bf16[2,64,128]{2,1,0:T(8,128)(2,1)S(1)} %get-tuple-element.21), channel_id=1, source_target_pairs={{0,48},{16,32},{32,16},{48,0},{64,112},{80,96},{96,80},{112,64},{1... | collective-permute-start | bytes 98312 | tf_op jit(solution)/shard_map/ppermute | solution.py:358
  75.1 1.3 collective-permute-start
  76.4 31.4 %all-to-all-done.1.high_ref = bf16[16,704,128]{2,1,0:T(8,128)(2,1)S(1)} async-done(((bf16[16,704,128]{2,1,0:T(8,128)(2,1)}), bf16[16,704,128]{2,1,0:T(8,128)(2,1)S(1)}, u32[]{:S(2)}, u32[]{:S(2)}) %all-to-all-start.1) | async-done | bytes 2883616 | tf_op jit(solution)/shard_map/all_to_all | solution.py:351
  107.8 8.8 %all-to-all-start.3 = ((bf16[16,128,128]{2,1,0:T(8,128)(2,1)}), bf16[16,128,128]{2,1,0:T(8,128)(2,1)S(1)}, u32[]{:S(2)}, u32[]{:S(2)}) async-start(bf16[16,128,128]{2,1,0:T(8,128)(2,1)} %copy-done.4), calls=%async_computation.3 | async-start | bytes 1048576 | tf_op jit(solution)/shard_map/all_to_all | solution.py:351
  116.7 6.4 %collective-permute-start.5 = (bf16[2,64,128]{2,1,0:T(8,128)(2,1)S(1)}, bf16[2,64,128]{2,1,0:T(8,128)(2,1)S(1)}, u32[]{:S(2)}, u32[]{:S(2)}) collective-permute-start(bf16[2,64,128]{2,1,0:T(8,128)(2,1)S(1)} %add_add_fusion), channel_id=1, source_target_pairs={{0,192},{16,208},{32,224},{48,240},{64,128},{80,144},{96,160},{112... | collective-permute-start | bytes 98312 | tf_op jit(solution)/shard_map/ppermute | solution.py:358
  123.1 1.0 collective-permute-start.4
  124.0 1.5 collective-permute-start.3
  125.5 5.9 %collective-permute-done.4 = bf16[2,64,128]{2,1,0:T(8,128)(2,1)S(1)} collective-permute-done((bf16[2,64,128]{2,1,0:T(8,128)(2,1)S(1)}, bf16[2,64,128]{2,1,0:T(8,128)(2,1)S(1)}, u32[]{:S(2)}, u32[]{:S(2)}) %collective-permute-start.4) | collective-permute-done | bytes 32800 | tf_op jit(solution)/shard_map/ppermute | solution.py:358
  131.4 0.6 convert_bitcast_fusion
  132.0 1.7 copy-done.1
  133.7 15.7 %shard_map.104 = (bf16[2,224,512]{2,1,0:T(8,128)(2,1)}, bf16[224,512]{1,0:T(8,128)(2,1)}, s32[16,128,1024]{2,1,0:T(8,128)S(1)}) custom-call(bf16[16,576,128]{2,1,0:T(8,128)(2,1)S(1)} %copy-done.1, bf16[16,704,128]{2,1,0:T(8,128)(2,1)S(1)} %all-to-all-done.1.high_ref), custom_call_target="tpu_custom_call" | custom-call | flops 1409286144 | bytes 16777216 | tf_op jit(solution)/shard_map/pallas_call | solution.py:267
  149.4 3.3 %copy-done.2 = s32[16,128,1024]{2,1,0:T(8,128)} copy-done((s32[16,128,1024]{2,1,0:T(8,128)}, s32[16,128,1024]{2,1,0:T(8,128)S(1)}, u32[]{:S(2)}) %copy-start.2) | copy-done | bytes 8388632
  152.7 3.4 %copy-done.3 = s32[16,128,1024]{2,1,0:T(8,128)S(1)} copy-done((s32[16,128,1024]{2,1,0:T(8,128)S(1)}, s32[16,128,1024]{2,1,0:T(8,128)}, u32[]{:S(2)}) %copy-start.3) | copy-done | bytes 8388632
  156.0 12.0 %shard_map.107 = bf16[2,224,512]{2,1,0:T(8,128)(2,1)S(1)} custom-call(bf16[16,704,128]{2,1,0:T(8,128)(2,1)S(1)} %all-to-all-done.1.high_ref, s32[16,128,1024]{2,1,0:T(8,128)S(1)} %copy-done.3, bf16[16,128,128]{2,1,0:T(8,128)(2,1)S(1)} %all-to-all-done.3.grad_ref), custom_call_target="tpu_custom_call" | custom-call | flops 939524096 | bytes 16777216 | tf_op jit(solution)/shard_map/pallas_call | solution.py:331
  168.0 1.2 copy.11
  (20 shorter events, 0.2 us)
Async XLA Ops:
  5.6 37.9 %all-to-all-start = ((bf16[16,576,128]{2,1,0:T(8,128)(2,1)}), bf16[16,576,128]{2,1,0:T(8,128)(2,1)S(1)}, u32[]{:S(2)}, u32[]{:S(2)}) async-start(bf16[16,576,128]{2,1,0:T(8,128)(2,1)} %get-tuple-element.14), calls=%async_computation | async-start | bytes 4718592 | tf_op jit(solution)/shard_map/all_to_all | solution.py:351
  13.0 30.4 %copy-start.6 = (bf16[512,2,224]{0,2,1:T(8,128)(2,1)S(1)}, bf16[512,2,224]{0,2,1:T(8,128)(2,1)}, u32[]{:S(2)}) copy-start(bf16[512,2,224]{0,2,1:T(8,128)(2,1)} %param.9) | copy-start | bytes 1376260
  13.1 30.4 %copy-start.7 = (bf16[512,224]{0,1:T(8,128)(2,1)S(1)}, bf16[512,224]{0,1:T(8,128)(2,1)}, u32[]{:S(2)}) copy-start(bf16[512,224]{0,1:T(8,128)(2,1)} %param.10) | copy-start | bytes 688132
  43.5 5.0 %copy-start = (bf16[16,576,128]{2,1,0:T(8,128)(2,1)}, bf16[16,576,128]{2,1,0:T(8,128)(2,1)S(1)}, u32[]{:S(2)}) copy-start(bf16[16,576,128]{2,1,0:T(8,128)(2,1)S(1)} %all-to-all-done.low_ref.got_ref) | copy-start | bytes 7077892
  65.5 6.2 %copy-start.5 = (s32[2,64,128]{2,1,0:T(8,128)S(1)}, s32[2,64,128]{2,1,0:T(8,128)}, u32[]{:S(2)}) copy-start(s32[2,64,128]{2,1,0:T(8,128)} %get-tuple-element.13.rank_ref) | copy-start | bytes 196612
  65.5 42.3 %all-to-all-start.1 = ((bf16[16,704,128]{2,1,0:T(8,128)(2,1)}), bf16[16,704,128]{2,1,0:T(8,128)(2,1)S(1)}, u32[]{:S(2)}, u32[]{:S(2)}) async-start(bf16[16,704,128]{2,1,0:T(8,128)(2,1)} %shard_map.103), calls=%async_computation.1 | async-start | bytes 5767168 | tf_op jit(solution)/shard_map/all_to_all | solution.py:351
  72.1 0.9 copy-start.4
  72.9 43.7 %collective-permute-start.2 = (bf16[2,64,128]{2,1,0:T(8,128)(2,1)S(1)}, bf16[2,64,128]{2,1,0:T(8,128)(2,1)S(1)}, u32[]{:S(2)}, u32[]{:S(2)}) collective-permute-start(bf16[2,64,128]{2,1,0:T(8,128)(2,1)S(1)} %get-tuple-element.21), channel_id=1, source_target_pairs={{0,48},{16,32},{32,16},{48,0},{64,112},{80,96},{96,80},{112,64},{1... | collective-permute-start | bytes 98312 | tf_op jit(solution)/shard_map/ppermute | solution.py:358
  75.0 41.7 %collective-permute-start.1 = (bf16[2,64,128]{2,1,0:T(8,128)(2,1)S(1)}, bf16[2,64,128]{2,1,0:T(8,128)(2,1)S(1)}, u32[]{:S(2)}, u32[]{:S(2)}) collective-permute-start(bf16[2,64,128]{2,1,0:T(8,128)(2,1)S(1)} %get-tuple-element.21), channel_id=1, source_target_pairs={{0,32},{16,48},{32,0},{48,16},{64,96},{80,112},{96,64},{112,80},{1... | collective-permute-start | bytes 98312 | tf_op jit(solution)/shard_map/ppermute | solution.py:358
  75.1 41.6 %collective-permute-start = (bf16[2,64,128]{2,1,0:T(8,128)(2,1)S(1)}, bf16[2,64,128]{2,1,0:T(8,128)(2,1)S(1)}, u32[]{:S(2)}, u32[]{:S(2)}) collective-permute-start(bf16[2,64,128]{2,1,0:T(8,128)(2,1)S(1)} %get-tuple-element.21), channel_id=1, source_target_pairs={{0,16},{16,0},{32,48},{48,32},{64,80},{80,64},{96,112},{112,96},{1... | collective-permute-start | bytes 98312 | tf_op jit(solution)/shard_map/ppermute | solution.py:358
  107.8 44.9 %all-to-all-start.3 = ((bf16[16,128,128]{2,1,0:T(8,128)(2,1)}), bf16[16,128,128]{2,1,0:T(8,128)(2,1)S(1)}, u32[]{:S(2)}, u32[]{:S(2)}) async-start(bf16[16,128,128]{2,1,0:T(8,128)(2,1)} %copy-done.4), calls=%async_computation.3 | async-start | bytes 1048576 | tf_op jit(solution)/shard_map/all_to_all | solution.py:351
  116.7 8.9 %collective-permute-start.5 = (bf16[2,64,128]{2,1,0:T(8,128)(2,1)S(1)}, bf16[2,64,128]{2,1,0:T(8,128)(2,1)S(1)}, u32[]{:S(2)}, u32[]{:S(2)}) collective-permute-start(bf16[2,64,128]{2,1,0:T(8,128)(2,1)S(1)} %add_add_fusion), channel_id=1, source_target_pairs={{0,192},{16,208},{32,224},{48,240},{64,128},{80,144},{96,160},{112... | collective-permute-start | bytes 98312 | tf_op jit(solution)/shard_map/ppermute | solution.py:358
  123.1 8.3 %collective-permute-start.4 = (bf16[2,64,128]{2,1,0:T(8,128)(2,1)S(1)}, bf16[2,64,128]{2,1,0:T(8,128)(2,1)S(1)}, u32[]{:S(2)}, u32[]{:S(2)}) collective-permute-start(bf16[2,64,128]{2,1,0:T(8,128)(2,1)S(1)} %add_add_fusion), channel_id=1, source_target_pairs={{0,128},{16,144},{32,160},{48,176},{64,192},{80,208},{96,224},{112... | collective-permute-start | bytes 98312 | tf_op jit(solution)/shard_map/ppermute | solution.py:358
  124.0 7.4 %collective-permute-start.3 = (bf16[2,64,128]{2,1,0:T(8,128)(2,1)S(1)}, bf16[2,64,128]{2,1,0:T(8,128)(2,1)S(1)}, u32[]{:S(2)}, u32[]{:S(2)}) collective-permute-start(bf16[2,64,128]{2,1,0:T(8,128)(2,1)S(1)} %add_add_fusion), channel_id=1, source_target_pairs={{0,64},{16,80},{32,96},{48,112},{64,0},{80,16},{96,32},{112,48},{1... | collective-permute-start | bytes 98312 | tf_op jit(solution)/shard_map/ppermute | solution.py:358
  132.0 1.7 copy-start.1
  149.4 3.3 %copy-start.2 = (s32[16,128,1024]{2,1,0:T(8,128)}, s32[16,128,1024]{2,1,0:T(8,128)S(1)}, u32[]{:S(2)}) copy-start(s32[16,128,1024]{2,1,0:T(8,128)S(1)} %get-tuple-element.19.spot_ref) | copy-start | bytes 25165828
  152.7 3.4 %copy-start.3 = (s32[16,128,1024]{2,1,0:T(8,128)S(1)}, s32[16,128,1024]{2,1,0:T(8,128)}, u32[]{:S(2)}) copy-start(s32[16,128,1024]{2,1,0:T(8,128)} %copy-done.2) | copy-start | bytes 25165828

commit v3 on v2

v3 whole, which is shorter than its diff:
```python
import functools
import jax
import jax.numpy as jnp
from jax import lax
from jax.experimental import pallas as pl
from jax.experimental.pallas import tpu as pltpu
from jax.sharding import PartitionSpec as P

BF16 = jnp.bfloat16
F32 = jnp.float32
LANES = 128
SHIFT = 256
EMPTY = 512
PACK_MIB = 60


def grant(mib):
    return pltpu.CompilerParams(vmem_limit_bytes=mib << 20)


def cost(flops, moved):
    return pl.CostEstimate(flops=flops, bytes_accessed=moved, transcendentals=0)


def lane_pick(table, where):
    return jnp.take_along_axis(table, where, axis=1, mode="promise_in_bounds")


def turn(source_ref, out_ref, layer, base):
    dests = out_ref.shape[0]
    cols = source_ref.shape[2] // dests
    turned = source_ref[layer].T
    for dest in range(dests):
        out_ref[dest, base + layer * cols : base + (layer + 1) * cols, :] = turned[dest * cols : (dest + 1) * cols]


def kept_slots(start_ref, idx_ref, live_ref, layer, lat_width):
    slots, tokens = idx_ref.shape[1:]
    place = lax.broadcasted_iota(jnp.int32, (slots, tokens), 0)
    local = idx_ref[layer] - start_ref[0]
    inside = (place < live_ref[layer : layer + 1, :]) & (local >= 0) & (local < lat_width)
    return place, local, inside


def pack_kernel(lat_width, start_ref, cot_ref, res_ref, idx_ref, live_ref, out_ref, rank_ref, slot_ref):
    slots, tokens = idx_ref.shape[1:]
    dests = out_ref.shape[0]
    cols = cot_ref.shape[2] // dests
    rows = res_ref.shape[1]

    @pl.when(pl.program_id(0) == 0)
    def _():
        found = []
        for layer in range(2):
            place, local, inside = kept_slots(start_ref, idx_ref, live_ref, layer, lat_width)
            key = jnp.where(inside, local, 1 << 20)
            rank = jnp.zeros((slots, tokens), jnp.int32)
            for slot in range(slots):
                rank = rank + jnp.where(key[slot : slot + 1, :] < key, 1, 0)
            rank = jnp.where(inside, rank, slots)
            rank_ref[layer] = rank
            key = local - SHIFT
            held = jnp.full((slots, tokens), EMPTY, jnp.int32)
            for slot in range(slots):
                held = jnp.where(rank[slot : slot + 1, :] == place, key[slot : slot + 1, :], held)
            found.append(held.astype(F32))
        slot_ref[...] = jnp.concatenate(found, axis=0).T.astype(BF16)

    for layer in range(2):
        turn(cot_ref, out_ref, layer, 0)
    base = 2 * cols + tokens
    for dest in range(dests):
        out_ref[dest, 2 * cols : base, :] = slot_ref[...]
        piece = res_ref[0, :, dest * cols : (dest + 1) * cols]
        out_ref[dest, base : base + rows, :] = piece[:, 0:LANES]
        rest = jnp.concatenate([piece[:, LANES:], jnp.zeros((rows, 2 * LANES - cols), BF16)], axis=1)
        out_ref[dest, base + rows : base + 2 * rows, :] = rest


def pack(lat_width, parts, start, cotangent, residual, index, live):
    _, tokens, width = cotangent.shape
    slots = index.shape[1]
    steps = 4
    share = residual.shape[1]
    rows = 2 * (width // parts) + tokens + 2 * share
    return pl.pallas_call(
        functools.partial(pack_kernel, lat_width),
        grid=(steps,),
        in_specs=[
            pl.BlockSpec(memory_space=pltpu.SMEM),
            pl.BlockSpec((2, tokens, width // steps), lambda i: (0, 0, i)),
            pl.BlockSpec((1, share, width // steps), lambda i: (0, 0, i)),
            pl.BlockSpec((2, slots, tokens), lambda i: (0, 0, 0)),
            pl.BlockSpec((2, tokens), lambda i: (0, 0)),
        ],
        out_specs=[
            pl.BlockSpec((parts // steps, rows, tokens), lambda i: (i, 0, 0)),
            pl.BlockSpec((2, slots, tokens), lambda i: (0, 0, 0)),
        ],
        out_shape=[
            jax.ShapeDtypeStruct((parts, rows, tokens), BF16),
            jax.ShapeDtypeStruct((2, slots, tokens), jnp.int32),
        ],
        scratch_shapes=[pltpu.VMEM((tokens, LANES), BF16)],
        compiler_params=grant(PACK_MIB),
        cost_estimate=cost(0, 5 << 20),
    )(start, cotangent, residual, index, live)


def values_kernel(rank_ref, val_ref, out_ref):
    slots, tokens = val_ref.shape[1:]
    place = lax.broadcasted_iota(jnp.int32, (slots, tokens), 0)
    codes = []
    for layer in range(2):
        rank = rank_ref[layer]
        value = val_ref[layer].astype(F32)
        code = jnp.zeros((slots, tokens), F32)
        for slot in range(slots):
            code = jnp.where(rank[slot : slot + 1, :] == place, value[slot : slot + 1, :], code)
        codes.append(code)
    out_ref[...] = jnp.concatenate(codes, axis=0).T.astype(BF16)


def slot_values(rank, value):
    return pl.pallas_call(
        values_kernel,
        out_shape=jax.ShapeDtypeStruct((value.shape[2], LANES), BF16),
        compiler_params=grant(40),
        cost_estimate=cost(0, 1 << 20),
    )(rank, value)


def terms_kernel(wf_ref, ws_ref, val_ref, got_ref, out_ref, weight_ref):
    shards, _, tokens = got_ref.shape
    cols, lat_width = ws_ref.shape

    @pl.when(pl.program_id(0) == 0)
    def _():
        weight_ref[0:cols, 0:lat_width] = wf_ref[0]
        weight_ref[cols : 2 * cols, 0:lat_width] = wf_ref[1]
        weight_ref[0:cols, lat_width:] = jnp.zeros((cols, lat_width), BF16)
        weight_ref[cols : 2 * cols, lat_width:] = ws_ref[...]

    for shard in range(shards):
        dense = lax.dot_general(
            got_ref[shard, 0 : 2 * cols, :].T,
            weight_ref[...],
            (((1,), (0,)), ((), ())),
            preferred_element_type=F32,
        )
        held = got_ref[shard, 2 * cols : 2 * cols + tokens, :].astype(F32).astype(jnp.int32) + SHIFT
        lane = lax.broadcasted_iota(jnp.int32, held.shape, 1)
        chunks = lat_width // LANES
        chunk = jnp.where(
            held < lat_width, (held >> 7) + jnp.where(lane >= LANES // 2, chunks, 0), 2 * chunks
        )
        within = held & (LANES - 1)
        picked = jnp.zeros(held.shape, F32)
        for part in range(2 * chunks):
            table = dense[:, part * LANES : (part + 1) * LANES]
            picked = jnp.where(chunk == part, lane_pick(table, within), picked)
        out_ref[shard, 0:tokens, :] = picked.astype(BF16)
        out_ref[shard, tokens:, :] = val_ref[...]


def slot_terms(first, second, values, got):
    parts, rows, tokens = got.shape
    cols, lat_width = second.shape
    shards = 2
    return pl.pallas_call(
        terms_kernel,
        grid=(parts // shards,),
        in_specs=[
            pl.BlockSpec((2, cols, lat_width), lambda i: (0, 0, 0)),
            pl.BlockSpec((cols, lat_width), lambda i: (0, 0)),
            pl.BlockSpec((tokens, LANES), lambda i: (0, 0)),
            pl.BlockSpec((shards, rows, tokens), lambda i: (i, 0, 0)),
        ],
        out_specs=pl.BlockSpec((shards, 2 * tokens, LANES), lambda i: (i, 0, 0)),
        out_shape=jax.ShapeDtypeStruct((parts, 2 * tokens, LANES), BF16),
        scratch_shapes=[pltpu.VMEM((2 * cols, 2 * lat_width), BF16)],
        compiler_params=grant(40),
        cost_estimate=cost(2 * parts * tokens * cols * 3 * lat_width, 6 << 20),
    )(first, second, values, got)


def total_kernel(got_ref, rank_ref, grad_ref, part_ref):
    tokens = grad_ref.shape[1]
    total = jnp.sum(got_ref[:, 0:tokens, :].astype(F32), axis=0)
    for dest in range(grad_ref.shape[0]):
        grad_ref[dest] = total.astype(BF16)
    turned = total.T
    slots = rank_ref.shape[1]
    for layer in range(2):
        rank = rank_ref[layer]
        part = jnp.zeros(rank.shape, F32)
        for slot in range(slots):
            row = layer * slots + slot
            part = jnp.where(rank == slot, turned[row : row + 1, :], part)
        part_ref[layer] = part.astype(BF16)


def slot_totals(got, rank):
    parts, rows, _ = got.shape
    return pl.pallas_call(
        total_kernel,
        out_shape=[
            jax.ShapeDtypeStruct((parts, rows // 2, LANES), BF16),
            jax.ShapeDtypeStruct(rank.shape, BF16),
        ],
        compiler_params=grant(40),
        cost_estimate=cost(0, 1 << 20),
    )(got, rank)


def spots_kernel(cols, got_ref, spot_ref, map_ref):
    shards, _, tokens = got_ref.shape
    lat_width = spot_ref.shape[2] // 2
    runs = lat_width // 8

    @pl.when(pl.program_id(0) == 0)
    def _():
        row = lax.broadcasted_iota(jnp.int32, map_ref.shape, 0)
        col = lax.broadcasted_iota(jnp.int32, map_ref.shape, 1)
        same = (row % (2 * runs)) == (col // 8)
        map_ref[...] = jnp.where(same, jnp.where(row < 2 * runs, LANES, 1), 0).astype(F32).astype(BF16)

    lane = lax.broadcasted_iota(jnp.int32, (tokens, LANES), 1)
    half = LANES // 2
    base = lane & half
    start = 8 * (lane & (half - 1)) - SHIFT
    self_bit = jnp.left_shift(1, lane & 7)
    for shard in range(shards):
        held = got_ref[shard, 2 * cols : 2 * cols + tokens, :].astype(F32).astype(jnp.int32)
        below = base
        for jump in (32, 16, 8, 4, 2, 1):
            further = below + jump
            below = jnp.where(lane_pick(held, further - 1) < start, further, below)
        last = base + (half - 1)
        bits = jnp.zeros((tokens, LANES), jnp.int32)
        for hop in range(8):
            spot = below if hop == 0 else jnp.minimum(below + hop, last)
            ahead = lane_pick(held, spot) - start
            bits = bits | jnp.where((ahead & -8) == 0, jnp.left_shift(1, ahead & 7), 0)
        both = jnp.concatenate([bits.astype(F32).astype(BF16), below.astype(F32).astype(BF16)], axis=1)
        spread = jnp.dot(both, map_ref[...], preferred_element_type=F32).astype(jnp.int32)
        for chunk in range(2 * lat_width // LANES):
            packed = spread[:, chunk * LANES : (chunk + 1) * LANES]
            bits = packed >> 7
            spot = (packed & (LANES - 1)) + lax.population_count(bits & (self_bit - 1))
            spot = jnp.where((bits & self_bit) != 0, spot, LANES)
            spot_ref[shard, :, chunk * LANES : (chunk + 1) * LANES] = spot.astype(F32).astype(BF16)


def slot_spots(got, cols, lat_width):
    parts, rows, tokens = got.shape
    shards = 2
    return pl.pallas_call(
        functools.partial(spots_kernel, cols),
        grid=(parts // shards,),
        in_specs=[pl.BlockSpec((shards, rows, tokens), lambda i: (i, 0, 0))],
        out_specs=pl.BlockSpec((shards, tokens, 2 * lat_width), lambda i: (i, 0, 0)),
        out_shape=jax.ShapeDtypeStruct((parts, tokens, 2 * lat_width), BF16),
        scratch_shapes=[pltpu.VMEM((2 * LANES, 2 * lat_width), BF16)],
        compiler_params=grant(40),
        cost_estimate=cost(2 * parts * tokens * 2 * LANES * 2 * lat_width, 8 << 20),
    )(got)


def dense(table_ref, first_row, spot_ref, out_ref):
    shards, tokens, width = spot_ref.shape
    for shard in range(shards):
        table = table_ref[shard, first_row : first_row + tokens, :].astype(F32)
        for chunk in range(width // LANES):
            at = slice(chunk * LANES, (chunk + 1) * LANES)
            spot = spot_ref[shard, :, at].astype(F32).astype(jnp.int32)
            found = jnp.where(spot < LANES, lane_pick(table, spot & (LANES - 1)), 0.0)
            out_ref[shard * tokens : (shard + 1) * tokens, at] = found.astype(BF16)


def codes_kernel(got_ref, val_ref, spot_ref, first_ref, second_ref, code_ref, sum_ref):
    shards, tokens, _ = spot_ref.shape
    cols, lat_width = second_ref.shape
    step = pl.program_id(0)

    @pl.when(step == 0)
    def _():
        sum_ref[...] = jnp.zeros_like(sum_ref)

    dense(val_ref, tokens, spot_ref, code_ref)
    cot = jnp.concatenate([got_ref[shard, 0 : 2 * cols, :] for shard in range(shards)], axis=1)
    dot = functools.partial(jnp.dot, preferred_element_type=F32)
    sum_ref[0 : 2 * cols, :] += dot(cot, code_ref[:, 0:lat_width])
    sum_ref[2 * cols : 3 * cols, :] += dot(cot[cols:], code_ref[:, lat_width:])

    @pl.when(step == pl.num_programs(0) - 1)
    def _():
        first_ref[0] = sum_ref[0:cols, :].astype(BF16)
        first_ref[1] = sum_ref[cols : 2 * cols, :].astype(BF16)
        second_ref[...] = sum_ref[2 * cols : 3 * cols, :].astype(BF16)


def decoder_grads(got, slots, spots, cols, lat_width):
    parts, rows, tokens = got.shape
    shards = 4
    return pl.pallas_call(
        codes_kernel,
        grid=(parts // shards,),
        in_specs=[
            pl.BlockSpec((shards, rows, tokens), lambda i: (i, 0, 0)),
            pl.BlockSpec((shards, 2 * tokens, LANES), lambda i: (i, 0, 0)),
            pl.BlockSpec((shards, tokens, 2 * lat_width), lambda i: (i, 0, 0)),
        ],
        out_specs=[
            pl.BlockSpec((2, cols, lat_width), lambda i: (0, 0, 0)),
            pl.BlockSpec((cols, lat_width), lambda i: (0, 0)),
        ],
        out_shape=[
            jax.ShapeDtypeStruct((2, cols, lat_width), BF16),
            jax.ShapeDtypeStruct((cols, lat_width), BF16),
        ],
        scratch_shapes=[
            pltpu.VMEM((shards * tokens, 2 * lat_width), BF16),
            pltpu.VMEM((3 * cols, lat_width), F32),
        ],
        compiler_params=grant(40),
        cost_estimate=cost(2 * parts * tokens * cols * 3 * lat_width, 8 << 20),
    )(got, slots, spots)


def back_kernel(res_ref, spot_ref, grad_ref, enc_ref, back_ref, sum_ref):
    shards, tokens, _ = spot_ref.shape
    _, cols, lat_width = enc_ref.shape
    owners = res_ref.shape[0] // 2
    rows = res_ref.shape[2] // 2
    step = pl.program_id(0)
    dense(grad_ref, 0, spot_ref, back_ref)

    @pl.when(step == 0)
    def _():
        sum_ref[...] = jnp.zeros_like(sum_ref)

    for layer in range(2):
        sides = []
        for side in range(2):
            pieces = [
                res_ref[layer * owners + owner, shard, side * rows : (side + 1) * rows, :]
                for shard in range(shards)
                for owner in range(owners)
            ]
            sides.append(jnp.concatenate(pieces, axis=0).T)
        left = jnp.concatenate(sides, axis=0)[0:cols]
        sum_ref[layer * cols : (layer + 1) * cols, :] += jnp.dot(
            left, back_ref[:, layer * lat_width : (layer + 1) * lat_width], preferred_element_type=F32
        )

    @pl.when(step == pl.num_programs(0) - 1)
    def _():
        enc_ref[0] = sum_ref[0:cols, :].astype(BF16)
        enc_ref[1] = sum_ref[cols:, :].astype(BF16)


def encoder_grads(res, spots, grads, cols, lat_width):
    owners, parts, rows, _ = res.shape
    tokens = spots.shape[1]
    shards = 4
    return pl.pallas_call(
        back_kernel,
        grid=(parts // shards,),
        in_specs=[
            pl.BlockSpec((owners, shards, rows, LANES), lambda i: (0, i, 0, 0)),
            pl.BlockSpec((shards,) + spots.shape[1:], lambda i: (i, 0, 0)),
            pl.BlockSpec((shards, tokens, LANES), lambda i: (i, 0, 0)),
        ],
        out_specs=pl.BlockSpec((2, cols, lat_width), lambda i: (0, 0, 0)),
        out_shape=jax.ShapeDtypeStruct((2, cols, lat_width), BF16),
        scratch_shapes=[
            pltpu.VMEM((shards * tokens, 2 * lat_width), BF16),
            pltpu.VMEM((2 * cols, lat_width), F32),
        ],
        compiler_params=grant(40),
        cost_estimate=cost(2 * parts * tokens * cols * 2 * lat_width, 8 << 20),
    )(res, spots, grads)


def exchange(array, axis):
    return lax.all_to_all(array, axis, 0, 0, tiled=True)


def union(part, axis, size):
    reach = 1
    while reach < size:
        others = [
            lax.ppermute(part, axis, [(at, at ^ (reach * hop)) for at in range(size)])
            for hop in (1, 2, 3)
            if reach * hop < size
        ]
        for other in others:
            part = part + other
        reach *= 4
    return part


def shards(layers, parts, residual, cotangent, decoder_first, decoder_second, latent_index, latent_value, active_count):
    lat_width = decoder_first.shape[0]
    cols = decoder_second.shape[1]
    start = (lax.axis_index("layer") * lat_width).astype(jnp.int32).reshape(1)
    index, value = latent_index.transpose(0, 2, 1), latent_value.transpose(0, 2, 1)
    tokens = residual.shape[1]
    place = lax.axis_index("layer")
    share = 2 * tokens // layers
    own = lax.dynamic_slice(
        residual,
        (place * 2 // layers, place % (layers // 2) * share, 0),
        (1, share, residual.shape[2]),
    )
    packed, rank = pack(lat_width, parts, start, cotangent, own, index, active_count)
    values = slot_values(rank, value)
    got = exchange(packed, "dp")
    res = lax.all_gather(got[:, 2 * cols + tokens :, :], "layer", axis=0)
    terms = slot_terms(decoder_first.transpose(1, 2, 0), decoder_second.T, values, got)
    slots = exchange(terms, "dp")
    spots = slot_spots(got, cols, lat_width)
    grads, part = slot_totals(slots, rank)
    all_grads = exchange(grads, "dp")
    first_grad, second_grad = decoder_grads(got, slots, spots, cols, lat_width)
    encoder_grad = encoder_grads(res, spots, all_grads, cols, lat_width)
    latent_grad = union(part, "layer", layers)
    return (
        first_grad.transpose(2, 0, 1),
        second_grad.T,
        encoder_grad.transpose(1, 0, 2),
        latent_grad.astype(F32).transpose(0, 2, 1),
    )


def solution(mesh):
    return jax.shard_map(
        functools.partial(shards, mesh.shape["layer"], mesh.shape["dp"]),
        mesh=mesh,
        in_specs=(
            P(None, "dp", None),
            P(None, "dp", None),
            P("layer", None, "dp"),
            P("layer", "dp"),
            P(None, "dp", None),
            P(None, "dp", None),
            P(None, "dp"),
        ),
        out_specs=(
            P("layer", None, "dp"),
            P("layer", "dp"),
            P("dp", None, "layer"),
            P(None, "dp", None),
        ),
        check_vma=False,
    )
```

time: 170 us -> 166 us (0.976)
  waiting for transfers between devices: 62.3 us -> 8 us
  blocking collectives: 17 us -> 63.4 us
  starting transfers between devices: 34.8 us -> 18.9 us
  between operations: 0.73 us -> 14.2 us
  local copies, waits for them, and re-layouts: 10.4 us -> 17.6 us
    all_to_all x3 -> x1, waiting for transfers between devices: 56.4 us -> 0.01 us  [exchange(): return lax.all_to_all(array, axis, 0, 0, tiled=True)]
    all_to_all x1 -> x2, blocking collectives: 17 us -> 63.4 us  [exchange(): return lax.all_to_all(array, axis, 0, 0, tiled=True)]
    all_to_all x3 -> x1, starting transfers between devices: 22.4 us -> 5.89 us  [exchange(): return lax.all_to_all(array, axis, 0, 0, tiled=True)]
    pallas_call x3 -> x4, Pallas kernels: 10.8 us -> 20 us  [the longest x1 14.2 us: slot_spots(): pl.pallas_call(functools.partial(spots_kernel, cols), grid=(parts // shar...]
    all_gather x0 -> x1, waiting for transfers between devices: none -> 7.96 us  [shards(): res = lax.all_gather(got[:, 2 * cols + tokens:, :], 'layer', axis=0)]
    pallas_call x1, Pallas kernels: 15.7 us -> 8.61 us  [decoder_grads(): pl.pallas_call(codes_kernel, grid=(parts // shards,), in_specs=[pl.BlockS...]
    unnamed x17 -> x29, local copies, waits for them, and re-layouts: 10.4 us -> 16.3 us
    ppermute x6, waiting for transfers between devices: 5.89 us -> 0.02 us  [union(): lax.ppermute(part, axis, [(at, at ^ reach * hop) for at in range(size)])]
  transfers between devices with their start and end apart: 9 -> 8, of which waited for: 3 -> 1; matrix products, arithmetic and copies ran while one was open for 0% -> 0% of each run, Pallas kernels for 13% -> 17%
where the time goes in v3:
time: 166 us; the launch traced here: 164 us
  blocking collectives  63.4 us (38%)
  Pallas kernels  41.7 us (25%)
  starting transfers between devices  18.9 us (11%)
  local copies, waits for them, and re-layouts  17.6 us (11%)
  between operations  14.2 us (9%)
  waiting for transfers between devices  8 us (5%)
    all_to_all x2, blocking collectives, exchange(): return lax.all_to_all(array, axis, 0, 0, tiled=True)  63.4 us
    unnamed x29, local copies, waits for them, and re-layouts  16.3 us
    pallas_call x1, Pallas kernels, slot_spots(): pl.pallas_call(functools.partial(spots_kernel, cols), grid=(parts // shar...  14.2 us
    ppermute x6, starting transfers between devices, union(): lax.ppermute(part, axis, [(at, at ^ reach * hop) for at in range(size)])  13 us
    pallas_call x1, Pallas kernels, decoder_grads(): pl.pallas_call(codes_kernel, grid=(parts // shards,), in_specs=[pl.BlockS...  8.61 us
    pallas_call x1, Pallas kernels, encoder_grads(): pl.pallas_call(back_kernel, grid=(parts // shards,), in_specs=[pl.BlockSp...  8.04 us
    all_gather x1, waiting for transfers between devices, shards(): res = lax.all_gather(got[:, 2 * cols + tokens:, :], 'layer', axis=0)  7.96 us
    all_to_all x1, starting transfers between devices, exchange(): return lax.all_to_all(array, axis, 0, 0, tiled=True)  5.89 us
  transfers between devices with their start and end apart: 8, of which 1 were waited for; matrix products, arithmetic and copies ran while one was open for 0% of the time, Pallas kernels for 17%

profile of v3, /device:TPU:2, one launch (start us, length us, event | category | flops | bytes accessed | tf_op | source)
XLA Modules:
  0.0 164.5 jit_solution(1187273009095145173)
XLA Ops:
  7.3 1.4 copy-done
  9.3 5.0 %shard_map.102 = (bf16[16,608,128]{2,1,0:T(8,128)(2,1)}, s32[2,64,128]{2,1,0:T(8,128)}) custom-call(s32[1]{0:T(128)} %bitcast.start_ref, bf16[2,128,3584]{2,1,0:T(8,128)(2,1)} %cot_ref.1, bf16[1,16,3584]{2,1,0:T(8,128)(2,1)} %constant_dynamic-slice_fusion.res_ref, s32[2,64,128]{2,1,0:T(8,128)} %bitcast.16, s32[2,128]{1,0:T(2,128)} %live_ref.1), custom_call_target="tpu_custom_call" | custom-call | bytes 5242880 | tf_op jit(solution)/shard_map/pallas_call | solution.py:86
  14.4 38.6 %all_to_all.15.got_ref = bf16[16,608,128]{2,1,0:T(8,128)(2,1)S(1)} all-to-all(bf16[16,608,128]{2,1,0:T(8,128)(2,1)} %get-tuple-element.10), channel_id=1, replica_groups=mesh['layer'=16,'dp'=16] {'dp'}, dimensions={0} | all-to-all | bytes 4980736 | tf_op jit(solution)/shard_map/all_to_all | solution.py:387
  53.6 1.5 copy-done.4
  55.5 1.7 %copy-done.5 = bf16[16,608,128]{2,1,0:T(8,128)(2,1)S(1)} copy-done((bf16[16,608,128]{2,1,0:T(8,128)(2,1)S(1)}, bf16[16,608,128]{2,1,0:T(8,128)(2,1)}, u32[]{:S(2)}) %copy-start.5) | copy-done | bytes 2490392
  57.2 5.0 %shard_map.104 = bf16[16,256,128]{2,1,0:T(8,128)(2,1)S(1)} custom-call(bf16[2,224,512]{2,1,0:T(8,128)(2,1)S(1)} %bitcast.14, bf16[224,512]{1,0:T(8,128)(2,1)S(1)} %bitcast.15, bf16[128,128]{1,0:T(8,128)(2,1)S(1)} %shard_map.103.val_ref, bf16[16,608,128]{2,1,0:T(8,128)(2,1)S(1)} %copy-done.5), custom_call_target="tpu_custom_call" | custom-call | flops 1409286144 | bytes 6291456 | tf_op jit(solution)/shard_map/pallas_call | solution.py:170
  62.3 24.8 %all_to_all.16.val_ref.got_ref = bf16[16,256,128]{2,1,0:T(8,128)(2,1)S(1)} all-to-all(bf16[16,256,128]{2,1,0:T(8,128)(2,1)S(1)} %shard_map.104), channel_id=1, replica_groups=mesh['layer'=16,'dp'=16] {'dp'}, dimensions={0} | all-to-all | bytes 2097152 | tf_op jit(solution)/shard_map/all_to_all | solution.py:387
  87.5 0.8 copy-done.9
  88.3 2.0 %collective-permute-start.2 = (bf16[2,64,128]{2,1,0:T(8,128)(2,1)S(1)}, bf16[2,64,128]{2,1,0:T(8,128)(2,1)S(1)}, u32[]{:S(2)}, u32[]{:S(2)}) collective-permute-start(bf16[2,64,128]{2,1,0:T(8,128)(2,1)S(1)} %get-tuple-element.15), channel_id=1, source_target_pairs={{0,48},{16,32},{32,16},{48,0},{64,112},{80,96},{96,80},{112,64},{1... | collective-permute-start | bytes 98312 | tf_op jit(solution)/shard_map/ppermute | solution.py:394
  90.4 0.8 collective-permute-start.1
  91.2 0.7 collective-permute-start
  91.9 14.2 %shard_map.105.spot_ref = bf16[16,128,1024]{2,1,0:T(8,128)(2,1)S(1)} custom-call(bf16[16,608,128]{2,1,0:T(8,128)(2,1)S(1)} %copy-done.6), custom_call_target="tpu_custom_call" | custom-call | flops 1073741824 | bytes 8388608 | tf_op jit(solution)/shard_map/pallas_call | solution.py:258
  106.1 1.9 %copy-done.1 = bf16[16,128,1024]{2,1,0:T(8,128)(2,1)} copy-done((bf16[16,128,1024]{2,1,0:T(8,128)(2,1)}, bf16[16,128,1024]{2,1,0:T(8,128)(2,1)S(1)}, u32[]{:S(2)}) %copy-start.1) | copy-done | bytes 4194328
  108.0 5.9 %all-to-all-start.2 = ((bf16[16,128,128]{2,1,0:T(8,128)(2,1)}), bf16[16,128,128]{2,1,0:T(8,128)(2,1)S(1)}, u32[]{:S(2)}, u32[]{:S(2)}) async-start(bf16[16,128,128]{2,1,0:T(8,128)(2,1)} %copy-done.9), calls=%async_computation.2 | async-start | bytes 1048576 | tf_op jit(solution)/shard_map/all_to_all | solution.py:387
  113.9 7.0 %collective-permute-start.5 = (bf16[2,64,128]{2,1,0:T(8,128)(2,1)S(1)}, bf16[2,64,128]{2,1,0:T(8,128)(2,1)S(1)}, u32[]{:S(2)}, u32[]{:S(2)}) collective-permute-start(bf16[2,64,128]{2,1,0:T(8,128)(2,1)S(1)} %add_add_fusion), channel_id=1, source_target_pairs={{0,192},{16,208},{32,224},{48,240},{64,128},{80,144},{96,160},{112... | collective-permute-start | bytes 98312 | tf_op jit(solution)/shard_map/ppermute | solution.py:394
  121.0 2.4 %collective-permute-start.3 = (bf16[2,64,128]{2,1,0:T(8,128)(2,1)S(1)}, bf16[2,64,128]{2,1,0:T(8,128)(2,1)S(1)}, u32[]{:S(2)}, u32[]{:S(2)}) collective-permute-start(bf16[2,64,128]{2,1,0:T(8,128)(2,1)S(1)} %add_add_fusion), channel_id=1, source_target_pairs={{0,64},{16,80},{32,96},{48,112},{64,0},{80,16},{96,32},{112,48},{1... | collective-permute-start | bytes 98312 | tf_op jit(solution)/shard_map/ppermute | solution.py:394
  123.4 2.2 %copy-done.2 = bf16[16,128,1024]{2,1,0:T(8,128)(2,1)S(1)} copy-done((bf16[16,128,1024]{2,1,0:T(8,128)(2,1)S(1)}, bf16[16,128,1024]{2,1,0:T(8,128)(2,1)}, u32[]{:S(2)}) %copy-start.2) | copy-done | bytes 4194328
  125.6 1.7 %copy-done.7 = bf16[16,608,128]{2,1,0:T(8,128)(2,1)S(1)} copy-done((bf16[16,608,128]{2,1,0:T(8,128)(2,1)S(1)}, bf16[16,608,128]{2,1,0:T(8,128)(2,1)}, u32[]{:S(2)}) %copy-start.7) | copy-done | bytes 2490392
  127.3 8.6 %shard_map.106 = (bf16[2,224,512]{2,1,0:T(8,128)(2,1)}, bf16[224,512]{1,0:T(8,128)(2,1)}) custom-call(bf16[16,608,128]{2,1,0:T(8,128)(2,1)S(1)} %copy-done.7, bf16[16,256,128]{2,1,0:T(8,128)(2,1)S(1)} %all_to_all.16.val_ref.got_ref, bf16[16,128,1024]{2,1,0:T(8,128)(2,1)S(1)} %copy-done.2), custom_call_target="tpu_custom_call" | custom-call | flops 1409286144 | bytes 8388608 | tf_op jit(solution)/shard_map/pallas_call | solution.py:306
  136.6 8.0 %all-gather.3.cloned.1.call-done = bf16[256,32,128]{2,1,0:T(8,128)(2,1)} async-done(((bf16[16,32,128]{2,1,0:T(8,128)(2,1)}), bf16[256,32,128]{2,1,0:T(8,128)(2,1)}) %all-gather.3.cloned.1.call-update) | async-done | bytes 2097168 | tf_op jit(solution)/shard_map/all_gather | solution.py:420
  144.6 2.2 %copy-done.3 = bf16[16,128,1024]{2,1,0:T(8,128)(2,1)S(1)} copy-done((bf16[16,128,1024]{2,1,0:T(8,128)(2,1)S(1)}, bf16[16,128,1024]{2,1,0:T(8,128)(2,1)}, u32[]{:S(2)}) %copy-start.3) | copy-done | bytes 4194328
  146.8 1.6 copy-done.8
  148.4 8.0 %shard_map.108 = bf16[2,224,512]{2,1,0:T(8,128)(2,1)S(1)} custom-call(bf16[16,16,32,128]{3,2,1,0:T(8,128)(2,1)S(1)} %bitcast.11, bf16[16,128,1024]{2,1,0:T(8,128)(2,1)S(1)} %copy-done.3, bf16[16,128,128]{2,1,0:T(8,128)(2,1)S(1)} %all-to-all-done.2.grad_ref), custom_call_target="tpu_custom_call" | custom-call | flops 939524096 | bytes 8388608 | tf_op jit(solution)/shard_map/pallas_call | solution.py:367
  156.4 1.2 copy.12
  (35 shorter events, 2.9 us)
Async XLA Ops:
  7.2 1.5 copy-start
  7.2 137.4 %all-gather.3.cloned.1.call-start = ((), (), s32[]{:S(2)}) async-start(), calls=%async_computation.3 | async-start | bytes 2228224 | tf_op jit(solution)/shard_map/all_gather | solution.py:420
  14.3 40.8 %copy-start.10 = (s32[2,64,128]{2,1,0:T(8,128)S(1)}, s32[2,64,128]{2,1,0:T(8,128)}, u32[]{:S(2)}) copy-start(s32[2,64,128]{2,1,0:T(8,128)} %get-tuple-element.11.rank_ref) | copy-start | bytes 196612
  14.3 40.8 %copy-start.11 = (bf16[2,128,64]{1,2,0:T(8,128)(2,1)S(1)}, bf16[2,128,64]{1,2,0:T(8,128)(2,1)}, u32[]{:S(2)}) copy-start(bf16[2,128,64]{1,2,0:T(8,128)(2,1)} %param.12) | copy-start | bytes 98308
  14.3 41.2 %copy-start.12 = (bf16[512,2,224]{0,2,1:T(8,128)(2,1)S(1)}, bf16[512,2,224]{0,2,1:T(8,128)(2,1)}, u32[]{:S(2)}) copy-start(bf16[512,2,224]{0,2,1:T(8,128)(2,1)} %param.9) | copy-start | bytes 1376260
  14.4 41.2 %copy-start.13 = (bf16[512,224]{0,1:T(8,128)(2,1)S(1)}, bf16[512,224]{0,1:T(8,128)(2,1)}, u32[]{:S(2)}) copy-start(bf16[512,224]{0,1:T(8,128)(2,1)} %param.10) | copy-start | bytes 688132
  53.6 1.5 copy-start.4
  55.5 1.7 %copy-start.5 = (bf16[16,608,128]{2,1,0:T(8,128)(2,1)S(1)}, bf16[16,608,128]{2,1,0:T(8,128)(2,1)}, u32[]{:S(2)}) copy-start(bf16[16,608,128]{2,1,0:T(8,128)(2,1)} %copy-done.4) | copy-start | bytes 7471108
  62.3 29.6 %copy-start.6 = (bf16[16,608,128]{2,1,0:T(8,128)(2,1)S(1)}, bf16[16,608,128]{2,1,0:T(8,128)(2,1)}, u32[]{:S(2)}) copy-start(bf16[16,608,128]{2,1,0:T(8,128)(2,1)} %copy-done.4) | copy-start | bytes 7471108
  87.5 0.8 copy-start.9
  88.3 25.6 %collective-permute-start.2 = (bf16[2,64,128]{2,1,0:T(8,128)(2,1)S(1)}, bf16[2,64,128]{2,1,0:T(8,128)(2,1)S(1)}, u32[]{:S(2)}, u32[]{:S(2)}) collective-permute-start(bf16[2,64,128]{2,1,0:T(8,128)(2,1)S(1)} %get-tuple-element.15), channel_id=1, source_target_pairs={{0,48},{16,32},{32,16},{48,0},{64,112},{80,96},{96,80},{112,64},{1... | collective-permute-start | bytes 98312 | tf_op jit(solution)/shard_map/ppermute | solution.py:394
  90.4 23.5 %collective-permute-start.1 = (bf16[2,64,128]{2,1,0:T(8,128)(2,1)S(1)}, bf16[2,64,128]{2,1,0:T(8,128)(2,1)S(1)}, u32[]{:S(2)}, u32[]{:S(2)}) collective-permute-start(bf16[2,64,128]{2,1,0:T(8,128)(2,1)S(1)} %get-tuple-element.15), channel_id=1, source_target_pairs={{0,32},{16,48},{32,0},{48,16},{64,96},{80,112},{96,64},{112,80},{1... | collective-permute-start | bytes 98312 | tf_op jit(solution)/shard_map/ppermute | solution.py:394
  91.2 22.7 %collective-permute-start = (bf16[2,64,128]{2,1,0:T(8,128)(2,1)S(1)}, bf16[2,64,128]{2,1,0:T(8,128)(2,1)S(1)}, u32[]{:S(2)}, u32[]{:S(2)}) collective-permute-start(bf16[2,64,128]{2,1,0:T(8,128)(2,1)S(1)} %get-tuple-element.15), channel_id=1, source_target_pairs={{0,16},{16,0},{32,48},{48,32},{64,80},{80,64},{96,112},{112,96},{1... | collective-permute-start | bytes 98312 | tf_op jit(solution)/shard_map/ppermute | solution.py:394
  106.1 2.0 %copy-start.1 = (bf16[16,128,1024]{2,1,0:T(8,128)(2,1)}, bf16[16,128,1024]{2,1,0:T(8,128)(2,1)S(1)}, u32[]{:S(2)}) copy-start(bf16[16,128,1024]{2,1,0:T(8,128)(2,1)S(1)} %shard_map.105.spot_ref) | copy-start | bytes 12582916
  108.0 28.6 %all-to-all-start.2 = ((bf16[16,128,128]{2,1,0:T(8,128)(2,1)}), bf16[16,128,128]{2,1,0:T(8,128)(2,1)S(1)}, u32[]{:S(2)}, u32[]{:S(2)}) async-start(bf16[16,128,128]{2,1,0:T(8,128)(2,1)} %copy-done.9), calls=%async_computation.2 | async-start | bytes 1048576 | tf_op jit(solution)/shard_map/all_to_all | solution.py:387
  113.9 22.0 %collective-permute-start.5 = (bf16[2,64,128]{2,1,0:T(8,128)(2,1)S(1)}, bf16[2,64,128]{2,1,0:T(8,128)(2,1)S(1)}, u32[]{:S(2)}, u32[]{:S(2)}) collective-permute-start(bf16[2,64,128]{2,1,0:T(8,128)(2,1)S(1)} %add_add_fusion), channel_id=1, source_target_pairs={{0,192},{16,208},{32,224},{48,240},{64,128},{80,144},{96,160},{112... | collective-permute-start | bytes 98312 | tf_op jit(solution)/shard_map/ppermute | solution.py:394
  121.0 15.0 %collective-permute-start.4 = (bf16[2,64,128]{2,1,0:T(8,128)(2,1)S(1)}, bf16[2,64,128]{2,1,0:T(8,128)(2,1)S(1)}, u32[]{:S(2)}, u32[]{:S(2)}) collective-permute-start(bf16[2,64,128]{2,1,0:T(8,128)(2,1)S(1)} %add_add_fusion), channel_id=1, source_target_pairs={{0,128},{16,144},{32,160},{48,176},{64,192},{80,208},{96,224},{112... | collective-permute-start | bytes 98312 | tf_op jit(solution)/shard_map/ppermute | solution.py:394
  121.0 15.0 %collective-permute-start.3 = (bf16[2,64,128]{2,1,0:T(8,128)(2,1)S(1)}, bf16[2,64,128]{2,1,0:T(8,128)(2,1)S(1)}, u32[]{:S(2)}, u32[]{:S(2)}) collective-permute-start(bf16[2,64,128]{2,1,0:T(8,128)(2,1)S(1)} %add_add_fusion), channel_id=1, source_target_pairs={{0,64},{16,80},{32,96},{48,112},{64,0},{80,16},{96,32},{112,48},{1... | collective-permute-start | bytes 98312 | tf_op jit(solution)/shard_map/ppermute | solution.py:394
  123.4 2.2 %copy-start.2 = (bf16[16,128,1024]{2,1,0:T(8,128)(2,1)S(1)}, bf16[16,128,1024]{2,1,0:T(8,128)(2,1)}, u32[]{:S(2)}) copy-start(bf16[16,128,1024]{2,1,0:T(8,128)(2,1)} %copy-done.1) | copy-start | bytes 12582916
  125.6 1.7 %copy-start.7 = (bf16[16,608,128]{2,1,0:T(8,128)(2,1)S(1)}, bf16[16,608,128]{2,1,0:T(8,128)(2,1)}, u32[]{:S(2)}) copy-start(bf16[16,608,128]{2,1,0:T(8,128)(2,1)} %copy-done.4) | copy-start | bytes 7471108
  144.6 2.2 %copy-start.3 = (bf16[16,128,1024]{2,1,0:T(8,128)(2,1)S(1)}, bf16[16,128,1024]{2,1,0:T(8,128)(2,1)}, u32[]{:S(2)}) copy-start(bf16[16,128,1024]{2,1,0:T(8,128)(2,1)} %copy-done.1) | copy-start | bytes 12582916
  146.8 1.6 copy-start.8
Sparse Core Ops, SparseCore 0:
  55.2 89.2 all-gather.2

commit v4 on v3

--- a/solution.py
+++ b/solution.py
@@ -11,10 +11,11 @@
 LANES = 128
 SHIFT = 256
 EMPTY = 512
-PACK_MIB = 60
-
-
-def grant(mib):
+STREAM_MIB = 60
+KERNEL_MIB = 16
+
+
+def grant(mib=KERNEL_MIB):
     return pltpu.CompilerParams(vmem_limit_bytes=mib << 20)
 
 
@@ -66,43 +67,46 @@
             found.append(held.astype(F32))
         slot_ref[...] = jnp.concatenate(found, axis=0).T.astype(BF16)
 
+    more = 4 * rows
     for layer in range(2):
-        turn(cot_ref, out_ref, layer, 0)
-    base = 2 * cols + tokens
+        turn(cot_ref, out_ref, layer, more)
     for dest in range(dests):
-        out_ref[dest, 2 * cols : base, :] = slot_ref[...]
-        piece = res_ref[0, :, dest * cols : (dest + 1) * cols]
-        out_ref[dest, base : base + rows, :] = piece[:, 0:LANES]
-        rest = jnp.concatenate([piece[:, LANES:], jnp.zeros((rows, 2 * LANES - cols), BF16)], axis=1)
-        out_ref[dest, base + rows : base + 2 * rows, :] = rest
-
-
-def pack(lat_width, parts, start, cotangent, residual, index, live):
+        out_ref[dest, more + 2 * cols :, :] = slot_ref[...]
+        for layer in range(2):
+            piece = res_ref[layer, :, dest * cols : (dest + 1) * cols]
+            out_ref[dest, 2 * layer * rows : (2 * layer + 1) * rows, :] = piece[:, 0:LANES]
+            rest = jnp.concatenate([piece[:, LANES:], jnp.zeros((rows, 2 * LANES - cols), BF16)], axis=1)
+            out_ref[dest, (2 * layer + 1) * rows : (2 * layer + 2) * rows, :] = rest
+
+
+def pack(lat_width, parts, members, start, cotangent, residual, index, live):
     _, tokens, width = cotangent.shape
     slots = index.shape[1]
     steps = 4
-    share = residual.shape[1]
-    rows = 2 * (width // parts) + tokens + 2 * share
+    share = tokens // members
+    rows = 2 * (width // parts) + tokens + 4 * share
     return pl.pallas_call(
         functools.partial(pack_kernel, lat_width),
-        grid=(steps,),
-        in_specs=[
-            pl.BlockSpec(memory_space=pltpu.SMEM),
-            pl.BlockSpec((2, tokens, width // steps), lambda i: (0, 0, i)),
-            pl.BlockSpec((1, share, width // steps), lambda i: (0, 0, i)),
-            pl.BlockSpec((2, slots, tokens), lambda i: (0, 0, 0)),
-            pl.BlockSpec((2, tokens), lambda i: (0, 0)),
-        ],
-        out_specs=[
-            pl.BlockSpec((parts // steps, rows, tokens), lambda i: (i, 0, 0)),
-            pl.BlockSpec((2, slots, tokens), lambda i: (0, 0, 0)),
-        ],
+        grid_spec=pltpu.PrefetchScalarGridSpec(
+            num_scalar_prefetch=1,
+            grid=(steps,),
+            in_specs=[
+                pl.BlockSpec((2, tokens, width // steps), lambda i, own: (0, 0, i)),
+                pl.BlockSpec((2, share, width // steps), lambda i, own: (0, own[1], i)),
+                pl.BlockSpec((2, slots, tokens), lambda i, own: (0, 0, 0)),
+                pl.BlockSpec((2, tokens), lambda i, own: (0, 0)),
+            ],
+            out_specs=[
+                pl.BlockSpec((parts // steps, rows, tokens), lambda i, own: (i, 0, 0)),
+                pl.BlockSpec((2, slots, tokens), lambda i, own: (0, 0, 0)),
+            ],
+            scratch_shapes=[pltpu.VMEM((tokens, LANES), BF16)],
+        ),
         out_shape=[
             jax.ShapeDtypeStruct((parts, rows, tokens), BF16),
             jax.ShapeDtypeStruct((2, slots, tokens), jnp.int32),
         ],
-        scratch_shapes=[pltpu.VMEM((tokens, LANES), BF16)],
-        compiler_params=grant(PACK_MIB),
+        compiler_params=grant(STREAM_MIB),
         cost_estimate=cost(0, 5 << 20),
     )(start, cotangent, residual, index, live)
 
@@ -125,12 +129,12 @@
     return pl.pallas_call(
         values_kernel,
         out_shape=jax.ShapeDtypeStruct((value.shape[2], LANES), BF16),
-        compiler_params=grant(40),
+        compiler_params=grant(),
         cost_estimate=cost(0, 1 << 20),
     )(rank, value)
 
 
-def terms_kernel(wf_ref, ws_ref, val_ref, got_ref, out_ref, weight_ref):
+def terms_kernel(more, wf_ref, ws_ref, val_ref, got_ref, out_ref, weight_ref):
     shards, _, tokens = got_ref.shape
     cols, lat_width = ws_ref.shape
 
@@ -143,12 +147,12 @@
 
     for shard in range(shards):
         dense = lax.dot_general(
-            got_ref[shard, 0 : 2 * cols, :].T,
+            got_ref[shard, more : more + 2 * cols, :].T,
             weight_ref[...],
             (((1,), (0,)), ((), ())),
             preferred_element_type=F32,
         )
-        held = got_ref[shard, 2 * cols : 2 * cols + tokens, :].astype(F32).astype(jnp.int32) + SHIFT
+        held = got_ref[shard, more + 2 * cols :, :].astype(F32).astype(jnp.int32) + SHIFT
         lane = lax.broadcasted_iota(jnp.int32, held.shape, 1)
         chunks = lat_width // LANES
         chunk = jnp.where(
@@ -168,7 +172,7 @@
     cols, lat_width = second.shape
     shards = 2
     return pl.pallas_call(
-        terms_kernel,
+        functools.partial(terms_kernel, rows - tokens - 2 * cols),
         grid=(parts // shards,),
         in_specs=[
             pl.BlockSpec((2, cols, lat_width), lambda i: (0, 0, 0)),
@@ -179,7 +183,7 @@
         out_specs=pl.BlockSpec((shards, 2 * tokens, LANES), lambda i: (i, 0, 0)),
         out_shape=jax.ShapeDtypeStruct((parts, 2 * tokens, LANES), BF16),
         scratch_shapes=[pltpu.VMEM((2 * cols, 2 * lat_width), BF16)],
-        compiler_params=grant(40),
+        compiler_params=grant(),
         cost_estimate=cost(2 * parts * tokens * cols * 3 * lat_width, 6 << 20),
     )(first, second, values, got)
 
@@ -208,12 +212,12 @@
             jax.ShapeDtypeStruct((parts, rows // 2, LANES), BF16),
             jax.ShapeDtypeStruct(rank.shape, BF16),
         ],
-        compiler_params=grant(40),
+        compiler_params=grant(),
         cost_estimate=cost(0, 1 << 20),
     )(got, rank)
 
 
-def spots_kernel(cols, got_ref, spot_ref, map_ref):
+def spots_kernel(got_ref, spot_ref, map_ref):
     shards, _, tokens = got_ref.shape
     lat_width = spot_ref.shape[2] // 2
     runs = lat_width // 8
@@ -231,7 +235,7 @@
     start = 8 * (lane & (half - 1)) - SHIFT
     self_bit = jnp.left_shift(1, lane & 7)
     for shard in range(shards):
-        held = got_ref[shard, 2 * cols : 2 * cols + tokens, :].astype(F32).astype(jnp.int32)
+        held = got_ref[shard, got_ref.shape[1] - tokens :, :].astype(F32).astype(jnp.int32)
         below = base
         for jump in (32, 16, 8, 4, 2, 1):
             further = below + jump
@@ -252,17 +256,17 @@
             spot_ref[shard, :, chunk * LANES : (chunk + 1) * LANES] = spot.astype(F32).astype(BF16)
 
 
-def slot_spots(got, cols, lat_width):
+def slot_spots(got, lat_width):
     parts, rows, tokens = got.shape
     shards = 2
     return pl.pallas_call(
-        functools.partial(spots_kernel, cols),
+        spots_kernel,
         grid=(parts // shards,),
         in_specs=[pl.BlockSpec((shards, rows, tokens), lambda i: (i, 0, 0))],
         out_specs=pl.BlockSpec((shards, tokens, 2 * lat_width), lambda i: (i, 0, 0)),
         out_shape=jax.ShapeDtypeStruct((parts, tokens, 2 * lat_width), BF16),
         scratch_shapes=[pltpu.VMEM((2 * LANES, 2 * lat_width), BF16)],
-        compiler_params=grant(40),
+        compiler_params=grant(),
         cost_estimate=cost(2 * parts * tokens * 2 * LANES * 2 * lat_width, 8 << 20),
     )(got)
 
@@ -288,7 +292,8 @@
         sum_ref[...] = jnp.zeros_like(sum_ref)
 
     dense(val_ref, tokens, spot_ref, code_ref)
-    cot = jnp.concatenate([got_ref[shard, 0 : 2 * cols, :] for shard in range(shards)], axis=1)
+    more = got_ref.shape[1] - tokens - 2 * cols
+    cot = jnp.concatenate([got_ref[shard, more : more + 2 * cols, :] for shard in range(shards)], axis=1)
     dot = functools.partial(jnp.dot, preferred_element_type=F32)
     sum_ref[0 : 2 * cols, :] += dot(cot, code_ref[:, 0:lat_width])
     sum_ref[2 * cols : 3 * cols, :] += dot(cot[cols:], code_ref[:, lat_width:])
@@ -323,18 +328,28 @@
             pltpu.VMEM((shards * tokens, 2 * lat_width), BF16),
             pltpu.VMEM((3 * cols, lat_width), F32),
         ],
-        compiler_params=grant(40),
+        compiler_params=grant(STREAM_MIB),
         cost_estimate=cost(2 * parts * tokens * cols * 3 * lat_width, 8 << 20),
     )(got, slots, spots)
 
 
-def back_kernel(res_ref, spot_ref, grad_ref, enc_ref, back_ref, sum_ref):
-    shards, tokens, _ = spot_ref.shape
+def back_kernel(own_ref, *refs):
+    res_refs, (spot_ref, grad_ref, enc_ref, back_ref, sum_ref) = refs[:-5], refs[-5:]
+    members = len(res_refs)
+    shards, tokens, width = spot_ref.shape
     _, cols, lat_width = enc_ref.shape
-    owners = res_ref.shape[0] // 2
-    rows = res_ref.shape[2] // 2
+    rows = tokens // members
     step = pl.program_id(0)
-    dense(grad_ref, 0, spot_ref, back_ref)
+    for shard in range(shards):
+        for member in range(members):
+            low = pl.multiple_of((own_ref[1] ^ member) * rows, rows)
+            table = grad_ref[shard, pl.ds(low, rows), :].astype(F32)
+            to = shard * tokens + member * rows
+            for chunk in range(width // LANES):
+                at = slice(chunk * LANES, (chunk + 1) * LANES)
+                spot = spot_ref[shard, pl.ds(low, rows), at].astype(F32).astype(jnp.int32)
+                found = jnp.where(spot < LANES, lane_pick(table, spot & (LANES - 1)), 0.0)
+                back_ref[to : to + rows, at] = found.astype(BF16)
 
     @pl.when(step == 0)
     def _():
@@ -343,11 +358,8 @@
     for layer in range(2):
         sides = []
         for side in range(2):
-            pieces = [
-                res_ref[layer * owners + owner, shard, side * rows : (side + 1) * rows, :]
-                for shard in range(shards)
-                for owner in range(owners)
-            ]
+            low = (2 * layer + side) * rows
+            pieces = [res_ref[shard, low : low + rows, :] for shard in range(shards) for res_ref in res_refs]
             sides.append(jnp.concatenate(pieces, axis=0).T)
         left = jnp.concatenate(sides, axis=0)[0:cols]
         sum_ref[layer * cols : (layer + 1) * cols, :] += jnp.dot(
@@ -360,15 +372,16 @@
         enc_ref[1] = sum_ref[cols:, :].astype(BF16)
 
 
-def encoder_grads(res, spots, grads, cols, lat_width):
-    owners, parts, rows, _ = res.shape
-    tokens = spots.shape[1]
+def encoder_grads(own, res, spots, grads, cols, lat_width):
+    parts, tokens, _ = spots.shape
+    rows = 4 * tokens // len(res)
     shards = 4
     return pl.pallas_call(
         back_kernel,
         grid=(parts // shards,),
-        in_specs=[
-            pl.BlockSpec((owners, shards, rows, LANES), lambda i: (0, i, 0, 0)),
+        in_specs=[pl.BlockSpec(memory_space=pltpu.SMEM)]
+        + [pl.BlockSpec((shards, rows, LANES), lambda i: (i, 0, 0)) for _ in res]
+        + [
             pl.BlockSpec((shards,) + spots.shape[1:], lambda i: (i, 0, 0)),
             pl.BlockSpec((shards, tokens, LANES), lambda i: (i, 0, 0)),
         ],
@@ -378,24 +391,23 @@
             pltpu.VMEM((shards * tokens, 2 * lat_width), BF16),
             pltpu.VMEM((2 * cols, lat_width), F32),
         ],
-        compiler_params=grant(40),
+        compiler_params=grant(STREAM_MIB),
         cost_estimate=cost(2 * parts * tokens * cols * 2 * lat_width, 8 << 20),
-    )(res, spots, grads)
+    )(own, *res, spots, grads)
 
 
 def exchange(array, axis):
     return lax.all_to_all(array, axis, 0, 0, tiled=True)
+
+
+def from_hops(array, axis, size, hops):
+    return [lax.ppermute(array, axis, [(at, at ^ hop) for at in range(size)]) for hop in hops]
 
 
 def union(part, axis, size):
     reach = 1
     while reach < size:
-        others = [
-            lax.ppermute(part, axis, [(at, at ^ (reach * hop)) for at in range(size)])
-            for hop in (1, 2, 3)
-            if reach * hop < size
-        ]
-        for other in others:
+        for other in from_hops(part, axis, size, [reach * hop for hop in (1, 2, 3) if reach * hop < size]):
             part = part + other
         reach *= 4
     return part
@@ -404,27 +416,25 @@
 def shards(layers, parts, residual, cotangent, decoder_first, decoder_second, latent_index, latent_value, active_count):
     lat_width = decoder_first.shape[0]
     cols = decoder_second.shape[1]
-    start = (lax.axis_index("layer") * lat_width).astype(jnp.int32).reshape(1)
+    tokens = residual.shape[1]
+    members = 4
+    place = lax.axis_index("layer")
+    own = jnp.stack([place * lat_width, place % members]).astype(jnp.int32)
     index, value = latent_index.transpose(0, 2, 1), latent_value.transpose(0, 2, 1)
-    tokens = residual.shape[1]
-    place = lax.axis_index("layer")
-    share = 2 * tokens // layers
-    own = lax.dynamic_slice(
-        residual,
-        (place * 2 // layers, place % (layers // 2) * share, 0),
-        (1, share, residual.shape[2]),
-    )
-    packed, rank = pack(lat_width, parts, start, cotangent, own, index, active_count)
+    packed, rank = pack(lat_width, parts, members, own, cotangent, residual, index, active_count)
     values = slot_values(rank, value)
     got = exchange(packed, "dp")
-    res = lax.all_gather(got[:, 2 * cols + tokens :, :], "layer", axis=0)
+    share = got[:, : 4 * tokens // members, :]
+    res = [got] + from_hops(share, "layer", layers, range(1, members))
     terms = slot_terms(decoder_first.transpose(1, 2, 0), decoder_second.T, values, got)
     slots = exchange(terms, "dp")
-    spots = slot_spots(got, cols, lat_width)
+    spots = slot_spots(got, lat_width)
+    slots, spots, *res[1:3] = lax.optimization_barrier((slots, spots, *res[1:3]))
     grads, part = slot_totals(slots, rank)
     all_grads = exchange(grads, "dp")
     first_grad, second_grad = decoder_grads(got, slots, spots, cols, lat_width)
-    encoder_grad = encoder_grads(res, spots, all_grads, cols, lat_width)
+    all_grads, first_grad = lax.optimization_barrier((all_grads, first_grad))
+    encoder_grad = encoder_grads(own, res, spots, all_grads, cols, lat_width)
     latent_grad = union(part, "layer", layers)
     return (
         first_grad.transpose(2, 0, 1),

time: 166 us -> 151 us (0.910)
  blocking collectives: 63.4 us -> 0 us
  waiting for transfers between devices: 8 us -> 41.2 us
  starting transfers between devices: 18.9 us -> 50.5 us
  between operations: 14.2 us -> 0.79 us
  local copies, waits for them, and re-layouts: 17.6 us -> 8.12 us
  Pallas kernels: 41.7 us -> 48.1 us
    all_to_all x2 -> x0, blocking collectives: 63.4 us -> none  [exchange(): return lax.all_to_all(array, axis, 0, 0, tiled=True)]
    all_to_all x1 -> x3, waiting for transfers between devices: 0.01 us -> 35.7 us  [exchange(): return lax.all_to_all(array, axis, 0, 0, tiled=True)]
    all_to_all x1 -> x3, starting transfers between devices: 5.89 us -> 24.1 us  [exchange(): return lax.all_to_all(array, axis, 0, 0, tiled=True)]
    ppermute x6 -> x9, starting transfers between devices: 13 us -> 26.4 us  [from_hops(): lax.ppermute(array, axis, [(at, at ^ hop) for at in range(size)])]
    unnamed x29 -> x23, local copies, waits for them, and re-layouts: 16.3 us -> 8.08 us
    all_gather x1 -> x0, waiting for transfers between devices: 7.96 us -> none  [shards(): res = lax.all_gather(got[:, 2 * cols + tokens:, :], 'layer', axis=0)]
    ppermute x6 -> x9, waiting for transfers between devices: 0.02 us -> 5.55 us  [from_hops(): lax.ppermute(array, axis, [(at, at ^ hop) for at in range(size)])]
    pallas_call x1, Pallas kernels: 8.04 us -> 10.3 us  [encoder_grads(): pl.pallas_call(back_kernel, grid=(parts // shards,), in_specs=[pl.BlockSp...]
  transfers between devices with their start and end apart: 8 -> 12, of which waited for: 1 -> 2; matrix products, arithmetic and copies ran while one was open for 0% -> 0% of each run, Pallas kernels for 17% -> 17%
where the time goes in v4:
time: 151 us; the launch traced here: 150 us
  starting transfers between devices  50.5 us (33%)
  Pallas kernels  48.1 us (32%)
  waiting for transfers between devices  41.2 us (27%)
  local copies, waits for them, and re-layouts  8.12 us (5%)
    all_to_all x3, waiting for transfers between devices, exchange(): return lax.all_to_all(array, axis, 0, 0, tiled=True)  35.7 us
    ppermute x9, starting transfers between devices, from_hops(): lax.ppermute(array, axis, [(at, at ^ hop) for at in range(size)])  26.4 us
    all_to_all x3, starting transfers between devices, exchange(): return lax.all_to_all(array, axis, 0, 0, tiled=True)  24.1 us
    pallas_call x1, Pallas kernels, slot_spots(): pl.pallas_call(spots_kernel, grid=(parts // shards,), in_specs=[pl.BlockS...  14.2 us
    pallas_call x1, Pallas kernels, encoder_grads(): pl.pallas_call(back_kernel, grid=(parts // shards,), in_specs=[pl.BlockSp...  10.3 us
    pallas_call x1, Pallas kernels, decoder_grads(): pl.pallas_call(codes_kernel, grid=(parts // shards,), in_specs=[pl.BlockS...  10.2 us
    unnamed x23, local copies, waits for them, and re-layouts  8.08 us
    pallas_call x1, Pallas kernels, pack(): pl.pallas_call(functools.partial(pack_kernel, lat_width), grid_spec=pltpu...  5.87 us
  transfers between devices with their start and end apart: 12, of which 2 were waited for; matrix products, arithmetic and copies ran while one was open for 0% of the time, Pallas kernels for 17%

profile of v4, /device:TPU:2, one launch (start us, length us, event | category | flops | bytes accessed | tf_op | source)
XLA Modules:
  0.0 150.0 jit_solution(5753456286500960124)
XLA Ops:
  1.2 5.9 %shard_map.102 = (bf16[16,704,128]{2,1,0:T(8,128)(2,1)}, s32[2,64,128]{2,1,0:T(8,128)}) custom-call(s32[2]{0:T(128)} %pad_add_fusion.start_ref.own_ref, bf16[2,128,3584]{2,1,0:T(8,128)(2,1)} %cot_ref.1, bf16[2,128,3584]{2,1,0:T(8,128)(2,1)} %res_ref.1, s32[2,64,128]{2,1,0:T(8,128)} %bitcast.15, s32[2,128]{1,0:T(2,128)} %live_ref.1), custom_call_target="tpu_custom_call" | custom-call | bytes 5242880 | tf_op jit(solution)/shard_map/pallas_call | solution.py:88
  7.1 7.6 %all-to-all-start = ((bf16[16,704,128]{2,1,0:T(8,128)(2,1)}), bf16[16,704,128]{2,1,0:T(8,128)(2,1)S(1)}, u32[]{:S(2)}, u32[]{:S(2)}) async-start(bf16[16,704,128]{2,1,0:T(8,128)(2,1)} %get-tuple-element.17), calls=%async_computation | async-start | bytes 5767168 | tf_op jit(solution)/shard_map/all_to_all | solution.py:400
  15.1 35.7 %all-to-all-done.got_ref.refs_0_ = bf16[16,704,128]{2,1,0:T(8,128)(2,1)S(1)} async-done(((bf16[16,704,128]{2,1,0:T(8,128)(2,1)}), bf16[16,704,128]{2,1,0:T(8,128)(2,1)S(1)}, u32[]{:S(2)}, u32[]{:S(2)}) %all-to-all-start) | async-done | bytes 2883616 | tf_op jit(solution)/shard_map/all_to_all | solution.py:400
  50.8 1.2 copy-done.6
  52.0 5.0 %shard_map.104 = bf16[16,256,128]{2,1,0:T(8,128)(2,1)S(1)} custom-call(bf16[2,224,512]{2,1,0:T(8,128)(2,1)S(1)} %bitcast.12, bf16[224,512]{1,0:T(8,128)(2,1)S(1)} %bitcast.13, bf16[128,128]{1,0:T(8,128)(2,1)S(1)} %shard_map.103.val_ref, bf16[16,704,128]{2,1,0:T(8,128)(2,1)S(1)} %all-to-all-done.got_ref.refs_0_), custom_call_target="tpu_custom_call" | custom-call | flops 1409286144 | bytes 6291456 | tf_op jit(solution)/shard_map/pallas_call | solution.py:174
  57.0 1.0 copy-done.2
  58.1 9.3 %all-to-all-start.1 = ((bf16[16,256,128]{2,1,0:T(8,128)(2,1)}), bf16[16,256,128]{2,1,0:T(8,128)(2,1)}, u32[]{:S(2)}, u32[]{:S(2)}) async-start(bf16[16,256,128]{2,1,0:T(8,128)(2,1)} %copy-done.2), calls=%async_computation.1 | async-start | bytes 2097152 | tf_op jit(solution)/shard_map/all_to_all | solution.py:400
  67.4 2.0 %collective-permute-start.1 = (bf16[16,128,128]{2,1,0:T(8,128)(2,1)S(1)}, bf16[16,128,128]{2,1,0:T(8,128)(2,1)S(1)}, u32[]{:S(2)}, u32[]{:S(2)}) collective-permute-start(bf16[16,128,128]{2,1,0:T(8,128)(2,1)S(1)} %slice.4), channel_id=1, source_target_pairs={{0,32},{16,48},{32,0},{48,16},{64,96},{80,112},{96,64},{112,80},{1... | collective-permute-start | bytes 1572872 | tf_op jit(solution)/shard_map/ppermute | solution.py:404
  70.1 14.2 %shard_map.105.spot_ref.refs_4_ = bf16[16,128,1024]{2,1,0:T(8,128)(2,1)S(1)} custom-call(bf16[16,704,128]{2,1,0:T(8,128)(2,1)S(1)} %all-to-all-done.got_ref.refs_0_), custom_call_target="tpu_custom_call" | custom-call | flops 1073741824 | bytes 8388608 | tf_op jit(solution)/shard_map/pallas_call | solution.py:262
  84.4 1.9 %copy-done.1 = bf16[16,128,1024]{2,1,0:T(8,128)(2,1)} copy-done((bf16[16,128,1024]{2,1,0:T(8,128)(2,1)}, bf16[16,128,1024]{2,1,0:T(8,128)(2,1)S(1)}, u32[]{:S(2)}) %copy-start.1) | copy-done | bytes 4194328
  86.3 5.5 %collective-permute-done.refs_1_ = bf16[16,128,128]{2,1,0:T(8,128)(2,1)} collective-permute-done((bf16[16,128,128]{2,1,0:T(8,128)(2,1)S(1)}, bf16[16,128,128]{2,1,0:T(8,128)(2,1)}, u32[]{:S(2)}, u32[]{:S(2)}) %collective-permute-start) | collective-permute-done | bytes 524320 | tf_op jit(solution)/shard_map/ppermute | solution.py:404
  91.8 2.2 %shard_map.106 = (bf16[16,128,128]{2,1,0:T(8,128)(2,1)}, bf16[2,64,128]{2,1,0:T(8,128)(2,1)S(1)}) custom-call(bf16[16,256,128]{2,1,0:T(8,128)(2,1)} %all-to-all-done.1.got_ref.val_ref, s32[2,64,128]{2,1,0:T(8,128)S(1)} %copy-done.3), custom_call_target="tpu_custom_call" | custom-call | bytes 1048576 | tf_op jit(solution)/shard_map/pallas_call | solution.py:209
  94.0 2.7 %collective-permute-start.5 = (bf16[2,64,128]{2,1,0:T(8,128)(2,1)S(1)}, bf16[2,64,128]{2,1,0:T(8,128)(2,1)S(1)}, u32[]{:S(2)}, u32[]{:S(2)}) collective-permute-start(bf16[2,64,128]{2,1,0:T(8,128)(2,1)S(1)} %get-tuple-element.27), channel_id=1, source_target_pairs={{0,48},{16,32},{32,16},{48,0},{64,112},{80,96},{96,80},{112,64},{1... | collective-permute-start | bytes 98312 | tf_op jit(solution)/shard_map/ppermute | solution.py:404
  96.8 0.7 collective-permute-start.3
  97.5 2.7 %collective-permute-start.2 = (bf16[16,128,128]{2,1,0:T(8,128)(2,1)}, bf16[16,128,128]{2,1,0:T(8,128)(2,1)S(1)}, u32[]{:S(2)}, u32[]{:S(2)}) collective-permute-start(bf16[16,128,128]{2,1,0:T(8,128)(2,1)} %copy-done.10), channel_id=1, source_target_pairs={{0,48},{16,32},{32,16},{48,0},{64,112},{80,96},{96,80},{112,64},{1... | collective-permute-start | bytes 1572872 | tf_op jit(solution)/shard_map/ppermute | solution.py:404
  100.2 7.2 %all-to-all-start.2 = ((bf16[16,128,128]{2,1,0:T(8,128)(2,1)}), bf16[16,128,128]{2,1,0:T(8,128)(2,1)S(1)}, u32[]{:S(2)}, u32[]{:S(2)}) async-start(bf16[16,128,128]{2,1,0:T(8,128)(2,1)} %get-tuple-element.19), calls=%async_computation.2 | async-start | bytes 1048576 | tf_op jit(solution)/shard_map/all_to_all | solution.py:400
  107.5 15.0 %collective-permute-start.8 = (bf16[2,64,128]{2,1,0:T(8,128)(2,1)S(1)}, bf16[2,64,128]{2,1,0:T(8,128)(2,1)S(1)}, u32[]{:S(2)}, u32[]{:S(2)}) collective-permute-start(bf16[2,64,128]{2,1,0:T(8,128)(2,1)S(1)} %add_add_fusion), channel_id=1, source_target_pairs={{0,192},{16,208},{32,224},{48,240},{64,128},{80,144},{96,160},{112... | collective-permute-start | bytes 98312 | tf_op jit(solution)/shard_map/ppermute | solution.py:404
  122.5 1.0 collective-permute-start.7
  123.5 1.5 collective-permute-start.6
  124.9 10.2 %shard_map.107 = (bf16[2,224,512]{2,1,0:T(8,128)(2,1)}, bf16[224,512]{1,0:T(8,128)(2,1)}) custom-call(bf16[16,704,128]{2,1,0:T(8,128)(2,1)} %copy-done, bf16[16,256,128]{2,1,0:T(8,128)(2,1)} %all-to-all-done.1.got_ref.val_ref, bf16[16,128,1024]{2,1,0:T(8,128)(2,1)} %copy-done.1), custom_call_target="tpu_custom_call" | custom-call | flops 1409286144 | bytes 8388608 | tf_op jit(solution)/shard_map/pallas_call | solution.py:311
  135.8 0.8 copy-done.7
  136.6 0.8 copy-done.9
  137.4 10.3 %shard_map.108 = bf16[2,224,512]{2,1,0:T(8,128)(2,1)} custom-call(s32[2]{0:T(128)} %pad_add_fusion.start_ref.own_ref, bf16[16,704,128]{2,1,0:T(8,128)(2,1)} %copy-done, bf16[16,128,128]{2,1,0:T(8,128)(2,1)} %collective-permute-done.refs_1_, bf16[16,128,128]{2,1,0:T(8,128)(2,1)} %copy-done.8, bf16[16,128,128]{2,1,0:T(8,128)(2,1)} %copy-done.9, ...), custom_call_target="tpu_custom_call" | custom-call | flops 939524096 | bytes 8388608 | tf_op jit(solution)/shard_map/pallas_call | solution.py:379
  147.7 2.3 %copy.11 = bf16[224,2,512]{2,1,0:T(2,128)(2,1)} copy(bf16[224,2,512]{2,0,1:T(8,128)(2,1)} %bitcast.14) | data formatting | bytes 917504
  (34 shorter events, 2.4 us)
Async XLA Ops:
  7.1 7.6 %copy-start.3 = (s32[2,64,128]{2,1,0:T(8,128)S(1)}, s32[2,64,128]{2,1,0:T(8,128)}, u32[]{:S(2)}) copy-start(s32[2,64,128]{2,1,0:T(8,128)} %get-tuple-element.16.rank_ref) | copy-start | bytes 196612
  7.1 7.6 %copy-start.4 = (bf16[2,128,64]{1,2,0:T(8,128)(2,1)S(1)}, bf16[2,128,64]{1,2,0:T(8,128)(2,1)}, u32[]{:S(2)}) copy-start(bf16[2,128,64]{1,2,0:T(8,128)(2,1)} %param.12) | copy-start | bytes 98308
  7.1 43.7 %copy-start.5 = (bf16[512,2,224]{0,2,1:T(8,128)(2,1)S(1)}, bf16[512,2,224]{0,2,1:T(8,128)(2,1)}, u32[]{:S(2)}) copy-start(bf16[512,2,224]{0,2,1:T(8,128)(2,1)} %param.9) | copy-start | bytes 1376260
  7.1 43.7 %all-to-all-start = ((bf16[16,704,128]{2,1,0:T(8,128)(2,1)}), bf16[16,704,128]{2,1,0:T(8,128)(2,1)S(1)}, u32[]{:S(2)}, u32[]{:S(2)}) async-start(bf16[16,704,128]{2,1,0:T(8,128)(2,1)} %get-tuple-element.17), calls=%async_computation | async-start | bytes 5767168 | tf_op jit(solution)/shard_map/all_to_all | solution.py:400
  50.8 19.3 %copy-start = (bf16[16,704,128]{2,1,0:T(8,128)(2,1)}, bf16[16,704,128]{2,1,0:T(8,128)(2,1)S(1)}, u32[]{:S(2)}) copy-start(bf16[16,704,128]{2,1,0:T(8,128)(2,1)S(1)} %all-to-all-done.got_ref.refs_0_) | copy-start | bytes 8650756
  50.8 1.2 copy-start.6
  57.0 1.1 copy-start.2
  58.1 33.8 %all-to-all-start.1 = ((bf16[16,256,128]{2,1,0:T(8,128)(2,1)}), bf16[16,256,128]{2,1,0:T(8,128)(2,1)}, u32[]{:S(2)}, u32[]{:S(2)}) async-start(bf16[16,256,128]{2,1,0:T(8,128)(2,1)} %copy-done.2), calls=%async_computation.1 | async-start | bytes 2097152 | tf_op jit(solution)/shard_map/all_to_all | solution.py:400
  67.4 16.9 %copy-start.10 = (bf16[16,128,128]{2,1,0:T(8,128)(2,1)}, bf16[16,128,128]{2,1,0:T(8,128)(2,1)S(1)}, u32[]{:S(2)}) copy-start(bf16[16,128,128]{2,1,0:T(8,128)(2,1)S(1)} %slice.4) | copy-start | bytes 1572868
  67.4 18.9 %collective-permute-start.1 = (bf16[16,128,128]{2,1,0:T(8,128)(2,1)S(1)}, bf16[16,128,128]{2,1,0:T(8,128)(2,1)S(1)}, u32[]{:S(2)}, u32[]{:S(2)}) collective-permute-start(bf16[16,128,128]{2,1,0:T(8,128)(2,1)S(1)} %slice.4), channel_id=1, source_target_pairs={{0,32},{16,48},{32,0},{48,16},{64,96},{80,112},{96,64},{112,80},{1... | collective-permute-start | bytes 1572872 | tf_op jit(solution)/shard_map/ppermute | solution.py:404
  69.5 22.4 %collective-permute-start = (bf16[16,128,128]{2,1,0:T(8,128)(2,1)S(1)}, bf16[16,128,128]{2,1,0:T(8,128)(2,1)}, u32[]{:S(2)}, u32[]{:S(2)}) collective-permute-start(bf16[16,128,128]{2,1,0:T(8,128)(2,1)S(1)} %slice.4), channel_id=1, source_target_pairs={{0,16},{16,0},{32,48},{48,32},{64,80},{80,64},{96,112},{112,96},{1... | collective-permute-start | bytes 1572872 | tf_op jit(solution)/shard_map/ppermute | solution.py:404
  84.3 1.9 %copy-start.1 = (bf16[16,128,1024]{2,1,0:T(8,128)(2,1)}, bf16[16,128,1024]{2,1,0:T(8,128)(2,1)S(1)}, u32[]{:S(2)}) copy-start(bf16[16,128,1024]{2,1,0:T(8,128)(2,1)S(1)} %shard_map.105.spot_ref.refs_4_) | copy-start | bytes 12582916
  86.3 48.8 %copy-start.8 = (bf16[16,128,128]{2,1,0:T(8,128)(2,1)}, bf16[16,128,128]{2,1,0:T(8,128)(2,1)S(1)}, u32[]{:S(2)}) copy-start(bf16[16,128,128]{2,1,0:T(8,128)(2,1)S(1)} %collective-permute-done.1.refs_2_) | copy-start | bytes 1572868
  94.0 13.5 %collective-permute-start.5 = (bf16[2,64,128]{2,1,0:T(8,128)(2,1)S(1)}, bf16[2,64,128]{2,1,0:T(8,128)(2,1)S(1)}, u32[]{:S(2)}, u32[]{:S(2)}) collective-permute-start(bf16[2,64,128]{2,1,0:T(8,128)(2,1)S(1)} %get-tuple-element.27), channel_id=1, source_target_pairs={{0,48},{16,32},{32,16},{48,0},{64,112},{80,96},{96,80},{112,64},{1... | collective-permute-start | bytes 98312 | tf_op jit(solution)/shard_map/ppermute | solution.py:404
  96.7 10.7 %collective-permute-start.4 = (bf16[2,64,128]{2,1,0:T(8,128)(2,1)S(1)}, bf16[2,64,128]{2,1,0:T(8,128)(2,1)S(1)}, u32[]{:S(2)}, u32[]{:S(2)}) collective-permute-start(bf16[2,64,128]{2,1,0:T(8,128)(2,1)S(1)} %get-tuple-element.27), channel_id=1, source_target_pairs={{0,32},{16,48},{32,0},{48,16},{64,96},{80,112},{96,64},{112,80},{1... | collective-permute-start | bytes 98312 | tf_op jit(solution)/shard_map/ppermute | solution.py:404
  96.8 10.7 %collective-permute-start.3 = (bf16[2,64,128]{2,1,0:T(8,128)(2,1)S(1)}, bf16[2,64,128]{2,1,0:T(8,128)(2,1)S(1)}, u32[]{:S(2)}, u32[]{:S(2)}) collective-permute-start(bf16[2,64,128]{2,1,0:T(8,128)(2,1)S(1)} %get-tuple-element.27), channel_id=1, source_target_pairs={{0,16},{16,0},{32,48},{48,32},{64,80},{80,64},{96,112},{112,96},{1... | collective-permute-start | bytes 98312 | tf_op jit(solution)/shard_map/ppermute | solution.py:404
  97.5 38.3 %collective-permute-start.2 = (bf16[16,128,128]{2,1,0:T(8,128)(2,1)}, bf16[16,128,128]{2,1,0:T(8,128)(2,1)S(1)}, u32[]{:S(2)}, u32[]{:S(2)}) collective-permute-start(bf16[16,128,128]{2,1,0:T(8,128)(2,1)} %copy-done.10), channel_id=1, source_target_pairs={{0,48},{16,32},{32,16},{48,0},{64,112},{80,96},{96,80},{112,64},{1... | collective-permute-start | bytes 1572872 | tf_op jit(solution)/shard_map/ppermute | solution.py:404
  100.2 35.6 %all-to-all-start.2 = ((bf16[16,128,128]{2,1,0:T(8,128)(2,1)}), bf16[16,128,128]{2,1,0:T(8,128)(2,1)S(1)}, u32[]{:S(2)}, u32[]{:S(2)}) async-start(bf16[16,128,128]{2,1,0:T(8,128)(2,1)} %get-tuple-element.19), calls=%async_computation.2 | async-start | bytes 1048576 | tf_op jit(solution)/shard_map/all_to_all | solution.py:400
  107.5 27.6 %collective-permute-start.8 = (bf16[2,64,128]{2,1,0:T(8,128)(2,1)S(1)}, bf16[2,64,128]{2,1,0:T(8,128)(2,1)S(1)}, u32[]{:S(2)}, u32[]{:S(2)}) collective-permute-start(bf16[2,64,128]{2,1,0:T(8,128)(2,1)S(1)} %add_add_fusion), channel_id=1, source_target_pairs={{0,192},{16,208},{32,224},{48,240},{64,128},{80,144},{96,160},{112... | collective-permute-start | bytes 98312 | tf_op jit(solution)/shard_map/ppermute | solution.py:404
  122.5 12.7 %collective-permute-start.7 = (bf16[2,64,128]{2,1,0:T(8,128)(2,1)S(1)}, bf16[2,64,128]{2,1,0:T(8,128)(2,1)S(1)}, u32[]{:S(2)}, u32[]{:S(2)}) collective-permute-start(bf16[2,64,128]{2,1,0:T(8,128)(2,1)S(1)} %add_add_fusion), channel_id=1, source_target_pairs={{0,128},{16,144},{32,160},{48,176},{64,192},{80,208},{96,224},{112... | collective-permute-start | bytes 98312 | tf_op jit(solution)/shard_map/ppermute | solution.py:404
  123.5 11.7 %collective-permute-start.6 = (bf16[2,64,128]{2,1,0:T(8,128)(2,1)S(1)}, bf16[2,64,128]{2,1,0:T(8,128)(2,1)S(1)}, u32[]{:S(2)}, u32[]{:S(2)}) collective-permute-start(bf16[2,64,128]{2,1,0:T(8,128)(2,1)S(1)} %add_add_fusion), channel_id=1, source_target_pairs={{0,64},{16,80},{32,96},{48,112},{64,0},{80,16},{96,32},{112,48},{1... | collective-permute-start | bytes 98312 | tf_op jit(solution)/shard_map/ppermute | solution.py:404
  135.8 0.8 copy-start.7
  136.6 0.8 copy-start.9

commit v5 on v4

--- a/solution.py
+++ b/solution.py
@@ -183,7 +183,7 @@
         out_specs=pl.BlockSpec((shards, 2 * tokens, LANES), lambda i: (i, 0, 0)),
         out_shape=jax.ShapeDtypeStruct((parts, 2 * tokens, LANES), BF16),
         scratch_shapes=[pltpu.VMEM((2 * cols, 2 * lat_width), BF16)],
-        compiler_params=grant(),
+        compiler_params=grant(50),
         cost_estimate=cost(2 * parts * tokens * cols * 3 * lat_width, 6 << 20),
     )(first, second, values, got)
 
@@ -266,7 +266,7 @@
         out_specs=pl.BlockSpec((shards, tokens, 2 * lat_width), lambda i: (i, 0, 0)),
         out_shape=jax.ShapeDtypeStruct((parts, tokens, 2 * lat_width), BF16),
         scratch_shapes=[pltpu.VMEM((2 * LANES, 2 * lat_width), BF16)],
-        compiler_params=grant(),
+        compiler_params=grant(56),
         cost_estimate=cost(2 * parts * tokens * 2 * LANES * 2 * lat_width, 8 << 20),
     )(got)
 
@@ -328,7 +328,7 @@
             pltpu.VMEM((shards * tokens, 2 * lat_width), BF16),
             pltpu.VMEM((3 * cols, lat_width), F32),
         ],
-        compiler_params=grant(STREAM_MIB),
+        compiler_params=grant(52),
         cost_estimate=cost(2 * parts * tokens * cols * 3 * lat_width, 8 << 20),
     )(got, slots, spots)
 
@@ -337,7 +337,7 @@
     res_refs, (spot_ref, grad_ref, enc_ref, back_ref, sum_ref) = refs[:-5], refs[-5:]
     members = len(res_refs)
     shards, tokens, width = spot_ref.shape
-    _, cols, lat_width = enc_ref.shape
+    cols, _, lat_width = enc_ref.shape
     rows = tokens // members
     step = pl.program_id(0)
     for shard in range(shards):
@@ -368,8 +368,8 @@
 
     @pl.when(step == pl.num_programs(0) - 1)
     def _():
-        enc_ref[0] = sum_ref[0:cols, :].astype(BF16)
-        enc_ref[1] = sum_ref[cols:, :].astype(BF16)
+        enc_ref[:, 0, :] = sum_ref[0:cols, :].astype(BF16)
+        enc_ref[:, 1, :] = sum_ref[cols:, :].astype(BF16)
 
 
 def encoder_grads(own, res, spots, grads, cols, lat_width):
@@ -385,13 +385,13 @@
             pl.BlockSpec((shards,) + spots.shape[1:], lambda i: (i, 0, 0)),
             pl.BlockSpec((shards, tokens, LANES), lambda i: (i, 0, 0)),
         ],
-        out_specs=pl.BlockSpec((2, cols, lat_width), lambda i: (0, 0, 0)),
-        out_shape=jax.ShapeDtypeStruct((2, cols, lat_width), BF16),
+        out_specs=pl.BlockSpec((cols, 2, lat_width), lambda i: (0, 0, 0)),
+        out_shape=jax.ShapeDtypeStruct((cols, 2, lat_width), BF16),
         scratch_shapes=[
             pltpu.VMEM((shards * tokens, 2 * lat_width), BF16),
             pltpu.VMEM((2 * cols, lat_width), F32),
         ],
-        compiler_params=grant(STREAM_MIB),
+        compiler_params=grant(50),
         cost_estimate=cost(2 * parts * tokens * cols * 2 * lat_width, 8 << 20),
     )(own, *res, spots, grads)
 
@@ -402,15 +402,6 @@
 
 def from_hops(array, axis, size, hops):
     return [lax.ppermute(array, axis, [(at, at ^ hop) for at in range(size)]) for hop in hops]
-
-
-def union(part, axis, size):
-    reach = 1
-    while reach < size:
-        for other in from_hops(part, axis, size, [reach * hop for hop in (1, 2, 3) if reach * hop < size]):
-            part = part + other
-        reach *= 4
-    return part
 
 
 def shards(layers, parts, residual, cotangent, decoder_first, decoder_second, latent_index, latent_value, active_count):
@@ -425,21 +416,27 @@
     values = slot_values(rank, value)
     got = exchange(packed, "dp")
     share = got[:, : 4 * tokens // members, :]
-    res = [got] + from_hops(share, "layer", layers, range(1, members))
+    res_near, res_next = from_hops(share, "layer", layers, (1, 2))
     terms = slot_terms(decoder_first.transpose(1, 2, 0), decoder_second.T, values, got)
     slots = exchange(terms, "dp")
     spots = slot_spots(got, lat_width)
-    slots, spots, *res[1:3] = lax.optimization_barrier((slots, spots, *res[1:3]))
+    slots, spots, res_next = lax.optimization_barrier((slots, spots, res_next))
     grads, part = slot_totals(slots, rank)
+    grads, res_near = lax.optimization_barrier((grads, res_near))
+    (res_last,) = from_hops(res_near, "layer", layers, (2,))
     all_grads = exchange(grads, "dp")
     first_grad, second_grad = decoder_grads(got, slots, spots, cols, lat_width)
-    all_grads, first_grad = lax.optimization_barrier((all_grads, first_grad))
+    part = functools.reduce(jnp.add, from_hops(part, "layer", layers, (1, 2, 3)), part)
+    all_grads, first_grad, part = lax.optimization_barrier((all_grads, first_grad, part))
+    res = [got, res_near, res_next, res_last]
     encoder_grad = encoder_grads(own, res, spots, all_grads, cols, lat_width)
-    latent_grad = union(part, "layer", layers)
+    far = from_hops(part, "layer", layers, (4, 8, 12))
+    *far, encoder_grad = lax.optimization_barrier((*far, encoder_grad))
+    latent_grad = functools.reduce(jnp.add, far, part)
     return (
         first_grad.transpose(2, 0, 1),
         second_grad.T,
-        encoder_grad.transpose(1, 0, 2),
+        encoder_grad,
         latent_grad.astype(F32).transpose(0, 2, 1),
     )
 

time: 151 us -> 136 us (0.901)
  starting transfers between devices: 50.5 us -> 40.7 us
  local copies, waits for them, and re-layouts: 8.12 us -> 2.72 us
  Pallas kernels: 48.1 us -> 51.3 us
  waiting for transfers between devices: 41.2 us -> 38.4 us
    ppermute x9, starting transfers between devices: 26.4 us -> 15.9 us  [from_hops(): lax.ppermute(array, axis, [(at, at ^ hop) for at in range(size)])]
    unnamed x23 -> x12, local copies, waits for them, and re-layouts: 8.08 us -> 0.8 us
    pallas_call x1, Pallas kernels: 5.02 us -> 8 us  [slot_terms(): pl.pallas_call(functools.partial(terms_kernel, rows - tokens - 2 * cols),...]
    ppermute x9, waiting for transfers between devices: 5.55 us -> 2.58 us  [from_hops(): lax.ppermute(array, axis, [(at, at ^ hop) for at in range(size)])]
    slice x1, local copies, waits for them, and re-layouts: 0.03 us -> 1.93 us  [shards(): share = got[:, :4 * tokens // members, :]]
    pallas_call x1, Pallas kernels: 14.2 us -> 16 us  [slot_spots(): pl.pallas_call(spots_kernel, grid=(parts // shards,), in_specs=[pl.BlockS...]
    pallas_call x1, Pallas kernels: 2.17 us -> 0.43 us  [slot_totals(): pl.pallas_call(total_kernel, out_shape=[jax.ShapeDtypeStruct((parts, rows...]
  transfers between devices with their start and end apart: 12 -> 12, of which waited for: 2 -> 2; matrix products, arithmetic and copies ran while one was open for 0% -> 1% of each run, Pallas kernels for 17% -> 28%
where the time goes in v5:
time: 136 us; the launch traced here: 135 us
  Pallas kernels  51.3 us (38%)
  starting transfers between devices  40.7 us (30%)
  waiting for transfers between devices  38.4 us (28%)
  local copies, waits for them, and re-layouts  2.72 us (2%)
    all_to_all x3, waiting for transfers between devices, exchange(): return lax.all_to_all(array, axis, 0, 0, tiled=True)  35.8 us
    all_to_all x3, starting transfers between devices, exchange(): return lax.all_to_all(array, axis, 0, 0, tiled=True)  24.8 us
    pallas_call x1, Pallas kernels, slot_spots(): pl.pallas_call(spots_kernel, grid=(parts // shards,), in_specs=[pl.BlockS...  16 us
    ppermute x9, starting transfers between devices, from_hops(): lax.ppermute(array, axis, [(at, at ^ hop) for at in range(size)])  15.9 us
    pallas_call x1, Pallas kernels, encoder_grads(): pl.pallas_call(back_kernel, grid=(parts // shards,), in_specs=[pl.BlockSp...  10.5 us
    pallas_call x1, Pallas kernels, decoder_grads(): pl.pallas_call(codes_kernel, grid=(parts // shards,), in_specs=[pl.BlockS...  10.1 us
    pallas_call x1, Pallas kernels, slot_terms(): pl.pallas_call(functools.partial(terms_kernel, rows - tokens - 2 * cols),...  8 us
    pallas_call x1, Pallas kernels, pack(): pl.pallas_call(functools.partial(pack_kernel, lat_width), grid_spec=pltpu...  5.87 us
  transfers between devices with their start and end apart: 12, of which 2 were waited for; matrix products, arithmetic and copies ran while one was open for 1% of the time, Pallas kernels for 28%

profile of v5, /device:TPU:2, one launch (start us, length us, event | category | flops | bytes accessed | tf_op | source)
XLA Modules:
  0.0 135.1 jit_solution(7162116031989185408)
XLA Ops:
  0.6 0.6 pad_add_fusion.start_ref.own_ref
  1.2 5.9 %shard_map.102 = (bf16[16,704,128]{2,1,0:T(8,128)(2,1)}, s32[2,64,128]{2,1,0:T(8,128)}) custom-call(s32[2]{0:T(128)} %pad_add_fusion.start_ref.own_ref, bf16[2,128,3584]{2,1,0:T(8,128)(2,1)} %cot_ref.1, bf16[2,128,3584]{2,1,0:T(8,128)(2,1)} %res_ref.1, s32[2,64,128]{2,1,0:T(8,128)} %bitcast.13, s32[2,128]{1,0:T(2,128)} %live_ref.1), custom_call_target="tpu_custom_call" | custom-call | bytes 5242880 | tf_op jit(solution)/shard_map/pallas_call | solution.py:88
  7.1 7.6 %all-to-all-start = ((bf16[16,704,128]{2,1,0:T(8,128)(2,1)}), bf16[16,704,128]{2,1,0:T(8,128)(2,1)}, u32[]{:S(2)}, u32[]{:S(2)}) async-start(bf16[16,704,128]{2,1,0:T(8,128)(2,1)} %get-tuple-element.23), calls=%async_computation | async-start | bytes 5767168 | tf_op jit(solution)/shard_map/all_to_all | solution.py:400
  14.8 0.4 shard_map.103.val_ref
  15.1 35.8 %all-to-all-done.got_ref.refs_0_ = bf16[16,704,128]{2,1,0:T(8,128)(2,1)} async-done(((bf16[16,704,128]{2,1,0:T(8,128)(2,1)}), bf16[16,704,128]{2,1,0:T(8,128)(2,1)}, u32[]{:S(2)}, u32[]{:S(2)}) %all-to-all-start) | async-done | bytes 2883616 | tf_op jit(solution)/shard_map/all_to_all | solution.py:400
  50.9 8.0 %shard_map.104 = bf16[16,256,128]{2,1,0:T(8,128)(2,1)} custom-call(bf16[2,224,512]{2,1,0:T(8,128)(2,1)S(1)} %bitcast.11, bf16[224,512]{1,0:T(8,128)(2,1)S(1)} %bitcast.12, bf16[128,128]{1,0:T(8,128)(2,1)S(1)} %shard_map.103.val_ref, bf16[16,704,128]{2,1,0:T(8,128)(2,1)} %all-to-all-done.got_ref.refs_0_), custom_call_target="tpu_custom_call" | custom-call | flops 1409286144 | bytes 6291456 | tf_op jit(solution)/shard_map/pallas_call | solution.py:174
  58.9 9.3 %all-to-all-start.1 = ((bf16[16,256,128]{2,1,0:T(8,128)(2,1)}), bf16[16,256,128]{2,1,0:T(8,128)(2,1)S(1)}, u32[]{:S(2)}, u32[]{:S(2)}) async-start(bf16[16,256,128]{2,1,0:T(8,128)(2,1)} %shard_map.104), calls=%async_computation.1 | async-start | bytes 2097152 | tf_op jit(solution)/shard_map/all_to_all | solution.py:400
  68.3 1.9 %slice.4 = bf16[16,128,128]{2,1,0:T(8,128)(2,1)} slice(bf16[16,704,128]{2,1,0:T(8,128)(2,1)} %all-to-all-done.got_ref.refs_0_), slice={[0:16], [0:128], [0:128]} | slice | bytes 1048576 | tf_op jit(solution)/shard_map/slice | solution.py:418
  70.2 1.9 %collective-permute-start = (bf16[16,128,128]{2,1,0:T(8,128)(2,1)}, bf16[16,128,128]{2,1,0:T(8,128)(2,1)S(1)}, u32[]{:S(2)}, u32[]{:S(2)}) collective-permute-start(bf16[16,128,128]{2,1,0:T(8,128)(2,1)} %slice.4), channel_id=1, source_target_pairs={{0,32},{16,48},{32,0},{48,16},{64,96},{80,112},{96,64},{112,80},{1... | collective-permute-start | bytes 1572872 | tf_op jit(solution)/shard_map/ppermute | solution.py:404
  72.1 0.7 collective-permute-start.1
  72.8 16.0 %shard_map.105.spot_ref.refs_4_ = bf16[16,128,1024]{2,1,0:T(8,128)(2,1)} custom-call(bf16[16,704,128]{2,1,0:T(8,128)(2,1)} %all-to-all-done.got_ref.refs_0_), custom_call_target="tpu_custom_call" | custom-call | flops 1073741824 | bytes 8388608 | tf_op jit(solution)/shard_map/pallas_call | solution.py:262
  88.8 0.4 shard_map.106
  89.3 0.8 copy-done
  90.0 2.6 %collective-permute-done.1.refs_1_ = bf16[16,128,128]{2,1,0:T(8,128)(2,1)S(1)} collective-permute-done((bf16[16,128,128]{2,1,0:T(8,128)(2,1)}, bf16[16,128,128]{2,1,0:T(8,128)(2,1)S(1)}, u32[]{:S(2)}, u32[]{:S(2)}) %collective-permute-start.1) | collective-permute-done | bytes 524320 | tf_op jit(solution)/shard_map/ppermute | solution.py:404
  92.6 1.9 %collective-permute-start.8 = (bf16[16,128,128]{2,1,0:T(8,128)(2,1)S(1)}, bf16[16,128,128]{2,1,0:T(8,128)(2,1)S(1)}, u32[]{:S(2)}, u32[]{:S(2)}) collective-permute-start(bf16[16,128,128]{2,1,0:T(8,128)(2,1)S(1)} %collective-permute-done.1.refs_1_), channel_id=1, source_target_pairs={{0,32},{16,48},{32,0},{48,16},{64,96},{80,112},{96,64},{112,80},{1... | collective-permute-start | bytes 1572872 | tf_op jit(solution)/shard_map/ppermute | solution.py:404
  94.5 7.8 %all-to-all-start.2 = ((bf16[16,128,128]{2,1,0:T(8,128)(2,1)}), bf16[16,128,128]{2,1,0:T(8,128)(2,1)S(1)}, u32[]{:S(2)}, u32[]{:S(2)}) async-start(bf16[16,128,128]{2,1,0:T(8,128)(2,1)} %copy-done), calls=%async_computation.2 | async-start | bytes 1048576 | tf_op jit(solution)/shard_map/all_to_all | solution.py:400
  102.4 0.2 collective-permute-start.2
  102.6 0.1 collective-permute-start.3
  102.7 3.2 %collective-permute-start.4 = (bf16[2,64,128]{2,1,0:T(8,128)(2,1)S(1)}, bf16[2,64,128]{2,1,0:T(8,128)(2,1)S(1)}, u32[]{:S(2)}, u32[]{:S(2)}) collective-permute-start(bf16[2,64,128]{2,1,0:T(8,128)(2,1)S(1)} %get-tuple-element.29), channel_id=1, source_target_pairs={{0,48},{16,32},{32,16},{48,0},{64,112},{80,96},{96,80},{112,64},{1... | collective-permute-start | bytes 98312 | tf_op jit(solution)/shard_map/ppermute | solution.py:404
  105.9 10.1 %shard_map.107 = (bf16[2,224,512]{2,1,0:T(8,128)(2,1)}, bf16[224,512]{1,0:T(8,128)(2,1)}) custom-call(bf16[16,704,128]{2,1,0:T(8,128)(2,1)} %all-to-all-done.got_ref.refs_0_, bf16[16,256,128]{2,1,0:T(8,128)(2,1)S(1)} %all-to-all-done.1.got_ref.val_ref, bf16[16,128,1024]{2,1,0:T(8,128)(2,1)} %shard_map.105.spot_ref.refs_4_), custom_call_target="tpu_custom_call" | custom-call | flops 1409286144 | bytes 8388608 | tf_op jit(solution)/shard_map/pallas_call | solution.py:311
  116.1 3.4 %collective-permute-start.5 = (bf16[2,64,128]{2,1,0:T(8,128)(2,1)S(1)}, bf16[2,64,128]{2,1,0:T(8,128)(2,1)S(1)}, u32[]{:S(2)}, u32[]{:S(2)}) collective-permute-start(bf16[2,64,128]{2,1,0:T(8,128)(2,1)S(1)} %add_add_fusion), channel_id=1, source_target_pairs={{0,64},{16,80},{32,96},{48,112},{64,0},{80,16},{96,32},{112,48},{1... | collective-permute-start | bytes 98312 | tf_op jit(solution)/shard_map/ppermute | solution.py:404
  119.4 4.5 %collective-permute-start.6 = (bf16[2,64,128]{2,1,0:T(8,128)(2,1)S(1)}, bf16[2,64,128]{2,1,0:T(8,128)(2,1)S(1)}, u32[]{:S(2)}, u32[]{:S(2)}) collective-permute-start(bf16[2,64,128]{2,1,0:T(8,128)(2,1)S(1)} %add_add_fusion), channel_id=1, source_target_pairs={{0,128},{16,144},{32,160},{48,176},{64,192},{80,208},{96,224},{112... | collective-permute-start | bytes 98312 | tf_op jit(solution)/shard_map/ppermute | solution.py:404
  124.0 10.5 %shard_map.108 = bf16[224,2,512]{2,1,0:T(2,128)(2,1)} custom-call(s32[2]{0:T(128)S(1)} %copy-done.3, bf16[16,704,128]{2,1,0:T(8,128)(2,1)} %all-to-all-done.got_ref.refs_0_, bf16[16,128,128]{2,1,0:T(8,128)(2,1)S(1)} %collective-permute-done.1.refs_1_, bf16[16,128,128]{2,1,0:T(8,128)(2,1)S(1)} %collective-permute-done.refs_2_, ...), custom_call_target="tpu_custom_call" | custom-call | flops 939524096 | bytes 8388608 | tf_op jit(solution)/shard_map/pallas_call | solution.py:379
  134.4 0.6 convert_bitcast_fusion
  (23 shorter events, 0.1 us)
Async XLA Ops:
  7.1 7.7 %copy-start.1 = (s32[2,64,128]{2,1,0:T(8,128)S(1)}, s32[2,64,128]{2,1,0:T(8,128)}, u32[]{:S(2)}) copy-start(s32[2,64,128]{2,1,0:T(8,128)} %get-tuple-element.22.rank_ref) | copy-start | bytes 196612
  7.1 7.7 %copy-start.2 = (bf16[2,128,64]{1,2,0:T(8,128)(2,1)S(1)}, bf16[2,128,64]{1,2,0:T(8,128)(2,1)}, u32[]{:S(2)}) copy-start(bf16[2,128,64]{1,2,0:T(8,128)(2,1)} %param.12) | copy-start | bytes 98308
  7.1 43.8 %copy-start.4 = (bf16[512,2,224]{0,2,1:T(8,128)(2,1)S(1)}, bf16[512,2,224]{0,2,1:T(8,128)(2,1)}, u32[]{:S(2)}) copy-start(bf16[512,2,224]{0,2,1:T(8,128)(2,1)} %param.9) | copy-start | bytes 1376260
  7.1 43.8 %copy-start.5 = (bf16[512,224]{0,1:T(8,128)(2,1)S(1)}, bf16[512,224]{0,1:T(8,128)(2,1)}, u32[]{:S(2)}) copy-start(bf16[512,224]{0,1:T(8,128)(2,1)} %param.10) | copy-start | bytes 688132
  7.1 43.8 %all-to-all-start = ((bf16[16,704,128]{2,1,0:T(8,128)(2,1)}), bf16[16,704,128]{2,1,0:T(8,128)(2,1)}, u32[]{:S(2)}, u32[]{:S(2)}) async-start(bf16[16,704,128]{2,1,0:T(8,128)(2,1)} %get-tuple-element.23), calls=%async_computation | async-start | bytes 5767168 | tf_op jit(solution)/shard_map/all_to_all | solution.py:400
  58.9 29.9 %all-to-all-start.1 = ((bf16[16,256,128]{2,1,0:T(8,128)(2,1)}), bf16[16,256,128]{2,1,0:T(8,128)(2,1)S(1)}, u32[]{:S(2)}, u32[]{:S(2)}) async-start(bf16[16,256,128]{2,1,0:T(8,128)(2,1)} %shard_map.104), calls=%async_computation.1 | async-start | bytes 2097152 | tf_op jit(solution)/shard_map/all_to_all | solution.py:400
  70.2 18.6 %collective-permute-start = (bf16[16,128,128]{2,1,0:T(8,128)(2,1)}, bf16[16,128,128]{2,1,0:T(8,128)(2,1)S(1)}, u32[]{:S(2)}, u32[]{:S(2)}) collective-permute-start(bf16[16,128,128]{2,1,0:T(8,128)(2,1)} %slice.4), channel_id=1, source_target_pairs={{0,32},{16,48},{32,0},{48,16},{64,96},{80,112},{96,64},{112,80},{1... | collective-permute-start | bytes 1572872 | tf_op jit(solution)/shard_map/ppermute | solution.py:404
  72.1 20.5 %collective-permute-start.1 = (bf16[16,128,128]{2,1,0:T(8,128)(2,1)}, bf16[16,128,128]{2,1,0:T(8,128)(2,1)S(1)}, u32[]{:S(2)}, u32[]{:S(2)}) collective-permute-start(bf16[16,128,128]{2,1,0:T(8,128)(2,1)} %slice.4), channel_id=1, source_target_pairs={{0,16},{16,0},{32,48},{48,32},{64,80},{80,64},{96,112},{112,96},{1... | collective-permute-start | bytes 1572872 | tf_op jit(solution)/shard_map/ppermute | solution.py:404
  89.3 0.8 copy-start
  92.6 31.3 %collective-permute-start.8 = (bf16[16,128,128]{2,1,0:T(8,128)(2,1)S(1)}, bf16[16,128,128]{2,1,0:T(8,128)(2,1)S(1)}, u32[]{:S(2)}, u32[]{:S(2)}) collective-permute-start(bf16[16,128,128]{2,1,0:T(8,128)(2,1)S(1)} %collective-permute-done.1.refs_1_), channel_id=1, source_target_pairs={{0,32},{16,48},{32,0},{48,16},{64,96},{80,112},{96,64},{112,80},{1... | collective-permute-start | bytes 1572872 | tf_op jit(solution)/shard_map/ppermute | solution.py:404
  94.5 21.6 %all-to-all-start.2 = ((bf16[16,128,128]{2,1,0:T(8,128)(2,1)}), bf16[16,128,128]{2,1,0:T(8,128)(2,1)S(1)}, u32[]{:S(2)}, u32[]{:S(2)}) async-start(bf16[16,128,128]{2,1,0:T(8,128)(2,1)} %copy-done), calls=%async_computation.2 | async-start | bytes 1048576 | tf_op jit(solution)/shard_map/all_to_all | solution.py:400
  102.4 21.6 %copy-start.3 = (s32[2]{0:T(128)S(1)}, s32[2]{0:T(128)}, u32[]{:S(2)}) copy-start(s32[2]{0:T(128)} %pad_add_fusion.start_ref.own_ref) | copy-start | bytes 28
  102.4 13.7 %collective-permute-start.2 = (bf16[2,64,128]{2,1,0:T(8,128)(2,1)S(1)}, bf16[2,64,128]{2,1,0:T(8,128)(2,1)S(1)}, u32[]{:S(2)}, u32[]{:S(2)}) collective-permute-start(bf16[2,64,128]{2,1,0:T(8,128)(2,1)S(1)} %get-tuple-element.29), channel_id=1, source_target_pairs={{0,16},{16,0},{32,48},{48,32},{64,80},{80,64},{96,112},{112,96},{1... | collective-permute-start | bytes 98312 | tf_op jit(solution)/shard_map/ppermute | solution.py:404
  102.6 13.5 %collective-permute-start.3 = (bf16[2,64,128]{2,1,0:T(8,128)(2,1)S(1)}, bf16[2,64,128]{2,1,0:T(8,128)(2,1)S(1)}, u32[]{:S(2)}, u32[]{:S(2)}) collective-permute-start(bf16[2,64,128]{2,1,0:T(8,128)(2,1)S(1)} %get-tuple-element.29), channel_id=1, source_target_pairs={{0,32},{16,48},{32,0},{48,16},{64,96},{80,112},{96,64},{112,80},{1... | collective-permute-start | bytes 98312 | tf_op jit(solution)/shard_map/ppermute | solution.py:404
  102.7 13.4 %collective-permute-start.4 = (bf16[2,64,128]{2,1,0:T(8,128)(2,1)S(1)}, bf16[2,64,128]{2,1,0:T(8,128)(2,1)S(1)}, u32[]{:S(2)}, u32[]{:S(2)}) collective-permute-start(bf16[2,64,128]{2,1,0:T(8,128)(2,1)S(1)} %get-tuple-element.29), channel_id=1, source_target_pairs={{0,48},{16,32},{32,16},{48,0},{64,112},{80,96},{96,80},{112,64},{1... | collective-permute-start | bytes 98312 | tf_op jit(solution)/shard_map/ppermute | solution.py:404
  116.1 18.3 %collective-permute-start.5 = (bf16[2,64,128]{2,1,0:T(8,128)(2,1)S(1)}, bf16[2,64,128]{2,1,0:T(8,128)(2,1)S(1)}, u32[]{:S(2)}, u32[]{:S(2)}) collective-permute-start(bf16[2,64,128]{2,1,0:T(8,128)(2,1)S(1)} %add_add_fusion), channel_id=1, source_target_pairs={{0,64},{16,80},{32,96},{48,112},{64,0},{80,16},{96,32},{112,48},{1... | collective-permute-start | bytes 98312 | tf_op jit(solution)/shard_map/ppermute | solution.py:404
  119.4 15.0 %collective-permute-start.6 = (bf16[2,64,128]{2,1,0:T(8,128)(2,1)S(1)}, bf16[2,64,128]{2,1,0:T(8,128)(2,1)S(1)}, u32[]{:S(2)}, u32[]{:S(2)}) collective-permute-start(bf16[2,64,128]{2,1,0:T(8,128)(2,1)S(1)} %add_add_fusion), channel_id=1, source_target_pairs={{0,128},{16,144},{32,160},{48,176},{64,192},{80,208},{96,224},{112... | collective-permute-start | bytes 98312 | tf_op jit(solution)/shard_map/ppermute | solution.py:404
  123.9 10.5 %collective-permute-start.7 = (bf16[2,64,128]{2,1,0:T(8,128)(2,1)S(1)}, bf16[2,64,128]{2,1,0:T(8,128)(2,1)S(1)}, u32[]{:S(2)}, u32[]{:S(2)}) collective-permute-start(bf16[2,64,128]{2,1,0:T(8,128)(2,1)S(1)} %add_add_fusion), channel_id=1, source_target_pairs={{0,192},{16,208},{32,224},{48,240},{64,128},{80,144},{96,160},{112... | collective-permute-start | bytes 98312 | tf_op jit(solution)/shard_map/ppermute | solution.py:404

commit v6 on v5

--- a/solution.py
+++ b/solution.py
@@ -9,10 +9,12 @@
 BF16 = jnp.bfloat16
 F32 = jnp.float32
 LANES = 128
+RUNS = LANES // 2
 SHIFT = 256
 EMPTY = 512
 STREAM_MIB = 60
 KERNEL_MIB = 16
+SPOTS_FLOPS = 1 << 32
 
 
 def grant(mib=KERNEL_MIB):
@@ -54,16 +56,17 @@
         found = []
         for layer in range(2):
             place, local, inside = kept_slots(start_ref, idx_ref, live_ref, layer, lat_width)
-            key = jnp.where(inside, local, 1 << 20)
+            key = (local & (RUNS - 1)) * 8 + (local >> 6)
+            held_key = key - SHIFT
+            key = jnp.where(inside, key, 1 << 20)
             rank = jnp.zeros((slots, tokens), jnp.int32)
             for slot in range(slots):
                 rank = rank + jnp.where(key[slot : slot + 1, :] < key, 1, 0)
             rank = jnp.where(inside, rank, slots)
             rank_ref[layer] = rank
-            key = local - SHIFT
             held = jnp.full((slots, tokens), EMPTY, jnp.int32)
             for slot in range(slots):
-                held = jnp.where(rank[slot : slot + 1, :] == place, key[slot : slot + 1, :], held)
+                held = jnp.where(rank[slot : slot + 1, :] == place, held_key[slot : slot + 1, :], held)
             found.append(held.astype(F32))
         slot_ref[...] = jnp.concatenate(found, axis=0).T.astype(BF16)
 
@@ -134,7 +137,7 @@
     )(rank, value)
 
 
-def terms_kernel(more, wf_ref, ws_ref, val_ref, got_ref, out_ref, weight_ref):
+def terms_kernel(more, wf_ref, ws_ref, val_ref, got_ref, out_ref, share_ref, weight_ref):
     shards, _, tokens = got_ref.shape
     cols, lat_width = ws_ref.shape
 
@@ -145,34 +148,35 @@
         weight_ref[0:cols, lat_width:] = jnp.zeros((cols, lat_width), BF16)
         weight_ref[cols : 2 * cols, lat_width:] = ws_ref[...]
 
-    for shard in range(shards):
-        dense = lax.dot_general(
-            got_ref[shard, more : more + 2 * cols, :].T,
-            weight_ref[...],
-            (((1,), (0,)), ((), ())),
-            preferred_element_type=F32,
-        )
-        held = got_ref[shard, more + 2 * cols :, :].astype(F32).astype(jnp.int32) + SHIFT
+    share_ref[...] = got_ref[:, 0:more, :]
+    pair = 2
+    for first in range(0, shards, pair):
+        some = range(first, first + pair)
+        cot = jnp.concatenate([got_ref[shard, more : more + 2 * cols, :] for shard in some], axis=1)
+        dense = jnp.dot(cot.T, weight_ref[...], preferred_element_type=F32)
+        held = jnp.concatenate([got_ref[shard, more + 2 * cols :, :] for shard in some], axis=0)
+        held = held.astype(F32).astype(jnp.int32) + SHIFT
         lane = lax.broadcasted_iota(jnp.int32, held.shape, 1)
         chunks = lat_width // LANES
-        chunk = jnp.where(
-            held < lat_width, (held >> 7) + jnp.where(lane >= LANES // 2, chunks, 0), 2 * chunks
-        )
-        within = held & (LANES - 1)
+        chunk = ((held & 7) >> 1) + jnp.where(lane >= RUNS, chunks, 0)
+        chunk = jnp.where(held < lat_width, chunk, 2 * chunks)
+        within = jnp.where((held & 1) == 1, RUNS, 0) + (held >> 3)
         picked = jnp.zeros(held.shape, F32)
         for part in range(2 * chunks):
             table = dense[:, part * LANES : (part + 1) * LANES]
             picked = jnp.where(chunk == part, lane_pick(table, within), picked)
-        out_ref[shard, 0:tokens, :] = picked.astype(BF16)
-        out_ref[shard, tokens:, :] = val_ref[...]
+        for shard in some:
+            out_ref[shard, 0:tokens, :] = picked[(shard - first) * tokens : (shard - first + 1) * tokens].astype(BF16)
+            out_ref[shard, tokens:, :] = val_ref[...]
 
 
 def slot_terms(first, second, values, got):
     parts, rows, tokens = got.shape
     cols, lat_width = second.shape
-    shards = 2
-    return pl.pallas_call(
-        functools.partial(terms_kernel, rows - tokens - 2 * cols),
+    more = rows - tokens - 2 * cols
+    shards = 4
+    return pl.pallas_call(
+        functools.partial(terms_kernel, more),
         grid=(parts // shards,),
         in_specs=[
             pl.BlockSpec((2, cols, lat_width), lambda i: (0, 0, 0)),
@@ -180,8 +184,14 @@
             pl.BlockSpec((tokens, LANES), lambda i: (0, 0)),
             pl.BlockSpec((shards, rows, tokens), lambda i: (i, 0, 0)),
         ],
-        out_specs=pl.BlockSpec((shards, 2 * tokens, LANES), lambda i: (i, 0, 0)),
-        out_shape=jax.ShapeDtypeStruct((parts, 2 * tokens, LANES), BF16),
+        out_specs=[
+            pl.BlockSpec((shards, 2 * tokens, LANES), lambda i: (i, 0, 0)),
+            pl.BlockSpec((shards, more, tokens), lambda i: (i, 0, 0)),
+        ],
+        out_shape=[
+            jax.ShapeDtypeStruct((parts, 2 * tokens, LANES), BF16),
+            jax.ShapeDtypeStruct((parts, more, tokens), BF16),
+        ],
         scratch_shapes=[pltpu.VMEM((2 * cols, 2 * lat_width), BF16)],
         compiler_params=grant(50),
         cost_estimate=cost(2 * parts * tokens * cols * 3 * lat_width, 6 << 20),
@@ -217,73 +227,126 @@
     )(got, rank)
 
 
-def spots_kernel(got_ref, spot_ref, map_ref):
+FEW = ((8, 4, 2, 1), 3)
+ALL = ((32, 16, 8, 4, 2, 1), 8)
+
+
+def spots_kernel(got_ref, spot_ref):
     shards, _, tokens = got_ref.shape
-    lat_width = spot_ref.shape[2] // 2
-    runs = lat_width // 8
-
-    @pl.when(pl.program_id(0) == 0)
-    def _():
-        row = lax.broadcasted_iota(jnp.int32, map_ref.shape, 0)
-        col = lax.broadcasted_iota(jnp.int32, map_ref.shape, 1)
-        same = (row % (2 * runs)) == (col // 8)
-        map_ref[...] = jnp.where(same, jnp.where(row < 2 * runs, LANES, 1), 0).astype(F32).astype(BF16)
-
+    top = got_ref.shape[1] - tokens
     lane = lax.broadcasted_iota(jnp.int32, (tokens, LANES), 1)
-    half = LANES // 2
-    base = lane & half
-    start = 8 * (lane & (half - 1)) - SHIFT
-    self_bit = jnp.left_shift(1, lane & 7)
+    place = lane & (RUNS - 1)
+    base = lane & RUNS
+    last = base + (RUNS - 1)
+    start = 8 * place - SHIFT
+
+    def fill(jumps, hops):
+        for shard in range(shards):
+            held = got_ref[shard, top:, :].astype(F32).astype(jnp.int32)
+            below = base
+            for jump in jumps:
+                further = below + jump
+                below = jnp.where(lane_pick(held, further - 1) < start, further, below)
+            codes = jnp.zeros((tokens, LANES), jnp.int32)
+            for hop in range(hops):
+                spot = below if hop == 0 else jnp.minimum(below + hop, last)
+                ahead = lane_pick(held, spot) - start
+                code = jnp.where((ahead & -8) == 0, ahead + 1, 0)
+                if hop > 0:
+                    code = jnp.where(below + hop <= last, code, 0)
+                codes = codes | jnp.left_shift(code, 4 * hop)
+            spot_ref[shard, 0:tokens, :] = below
+            spot_ref[shard, tokens:, :] = codes
+
+    deep = jnp.zeros((tokens, LANES), jnp.int32)
     for shard in range(shards):
-        held = got_ref[shard, got_ref.shape[1] - tokens :, :].astype(F32).astype(jnp.int32)
-        below = base
-        for jump in (32, 16, 8, 4, 2, 1):
-            further = below + jump
-            below = jnp.where(lane_pick(held, further - 1) < start, further, below)
-        last = base + (half - 1)
-        bits = jnp.zeros((tokens, LANES), jnp.int32)
-        for hop in range(8):
-            spot = below if hop == 0 else jnp.minimum(below + hop, last)
-            ahead = lane_pick(held, spot) - start
-            bits = bits | jnp.where((ahead & -8) == 0, jnp.left_shift(1, ahead & 7), 0)
-        both = jnp.concatenate([bits.astype(F32).astype(BF16), below.astype(F32).astype(BF16)], axis=1)
-        spread = jnp.dot(both, map_ref[...], preferred_element_type=F32).astype(jnp.int32)
-        for chunk in range(2 * lat_width // LANES):
-            packed = spread[:, chunk * LANES : (chunk + 1) * LANES]
-            bits = packed >> 7
-            spot = (packed & (LANES - 1)) + lax.population_count(bits & (self_bit - 1))
-            spot = jnp.where((bits & self_bit) != 0, spot, LANES)
-            spot_ref[shard, :, chunk * LANES : (chunk + 1) * LANES] = spot.astype(F32).astype(BF16)
-
-
-def slot_spots(got, lat_width):
+        held = got_ref[shard, top:, :].astype(F32).astype(jnp.int32)
+        ahead = pltpu.roll(held, LANES - FEW[1], 1)
+        crowd = ((held >> 3) == (ahead >> 3)) & (place < RUNS - FEW[1])
+        many = place == sum(FEW[0])
+        deep = jnp.where((held < EMPTY) & (crowd | many), 1, deep)
+    deep = jnp.max(deep)
+
+    @pl.when(deep == 0)
+    def _():
+        fill(*FEW)
+
+    @pl.when(deep != 0)
+    def _():
+        fill(*ALL)
+
+
+def slot_spots(got):
     parts, rows, tokens = got.shape
     shards = 2
     return pl.pallas_call(
         spots_kernel,
         grid=(parts // shards,),
         in_specs=[pl.BlockSpec((shards, rows, tokens), lambda i: (i, 0, 0))],
-        out_specs=pl.BlockSpec((shards, tokens, 2 * lat_width), lambda i: (i, 0, 0)),
-        out_shape=jax.ShapeDtypeStruct((parts, tokens, 2 * lat_width), BF16),
-        scratch_shapes=[pltpu.VMEM((2 * LANES, 2 * lat_width), BF16)],
+        out_specs=pl.BlockSpec((shards, 2 * tokens, LANES), lambda i: (i, 0, 0)),
+        out_shape=jax.ShapeDtypeStruct((parts, 2 * tokens, LANES), jnp.int32),
         compiler_params=grant(56),
-        cost_estimate=cost(2 * parts * tokens * 2 * LANES * 2 * lat_width, 8 << 20),
+        cost_estimate=cost(SPOTS_FLOPS, 8 << 20),
     )(got)
 
 
-def dense(table_ref, first_row, spot_ref, out_ref):
-    shards, tokens, width = spot_ref.shape
+def dense(table, below, codes, hops):
+    rows = below.shape[0]
+    lane = lax.broadcasted_iota(jnp.int32, (rows, LANES), 1)
+    near = lane < RUNS
+    far_codes = pltpu.roll(codes, RUNS, 1)
+    out = [jnp.zeros((rows, LANES), F32) for _ in range(8)]
+    for hop in range(hops):
+        spot = below if hop == 0 else jnp.minimum(below + hop, LANES - 1)
+        value = lane_pick(table, spot)
+        far_value = pltpu.roll(value, RUNS, 1)
+        code = (codes >> (4 * hop)) & 15
+        far_code = (far_codes >> (4 * hop)) & 15
+        for layer, (kept, moved, one, two) in enumerate(
+            ((value, far_value, code, far_code - 1), (far_value, value, far_code, code - 1))
+        ):
+            kept = jnp.where(near, kept, moved)
+            which = jnp.where(near, one, two)
+            for chunk in range(4):
+                at = 4 * layer + chunk
+                out[at] = jnp.where(which == 2 * chunk + 1, kept, out[at])
+    return out
+
+
+def fill_dense(table_ref, spot_ref, out_ref, row_of):
+    shards, tokens = spot_ref.shape[0], spot_ref.shape[1] // 2
+    block = 16
+    crowd = jnp.zeros((tokens, LANES), jnp.int32)
     for shard in range(shards):
-        table = table_ref[shard, first_row : first_row + tokens, :].astype(F32)
-        for chunk in range(width // LANES):
-            at = slice(chunk * LANES, (chunk + 1) * LANES)
-            spot = spot_ref[shard, :, at].astype(F32).astype(jnp.int32)
-            found = jnp.where(spot < LANES, lane_pick(table, spot & (LANES - 1)), 0.0)
-            out_ref[shard * tokens : (shard + 1) * tokens, at] = found.astype(BF16)
+        crowd = jnp.where((spot_ref[shard, tokens:, :] >> (4 * FEW[1])) != 0, 1, crowd)
+    crowd = jnp.max(crowd)
+
+    def fill(hops, shard, part):
+        low = row_of(part * block)
+        table = table_ref[shard, pl.ds(low, block), :].astype(F32)
+        below = spot_ref[shard, pl.ds(low, block), :]
+        codes = spot_ref[shard, pl.ds(low + tokens, block), :]
+        to = pl.multiple_of(shard * tokens + part * block, block)
+        for chunk, found in enumerate(dense(table, below, codes, hops)):
+            out_ref[pl.ds(to, block), chunk * LANES : (chunk + 1) * LANES] = found.astype(BF16)
+
+    @pl.when(crowd == 0)
+    def _():
+        for shard in range(shards):
+            for part in range(tokens // block):
+                fill(FEW[1], shard, part)
+
+    @pl.when(crowd != 0)
+    def _():
+        def one(at, carry):
+            fill(ALL[1], at // (tokens // block), at % (tokens // block))
+            return carry
+
+        lax.fori_loop(0, shards * tokens // block, one, 0)
 
 
 def codes_kernel(got_ref, val_ref, spot_ref, first_ref, second_ref, code_ref, sum_ref):
-    shards, tokens, _ = spot_ref.shape
+    shards, tokens = spot_ref.shape[0], spot_ref.shape[1] // 2
     cols, lat_width = second_ref.shape
     step = pl.program_id(0)
 
@@ -291,7 +354,7 @@
     def _():
         sum_ref[...] = jnp.zeros_like(sum_ref)
 
-    dense(val_ref, tokens, spot_ref, code_ref)
+    fill_dense(val_ref, spot_ref, code_ref, lambda row: row)
     more = got_ref.shape[1] - tokens - 2 * cols
     cot = jnp.concatenate([got_ref[shard, more : more + 2 * cols, :] for shard in range(shards)], axis=1)
     dot = functools.partial(jnp.dot, preferred_element_type=F32)
@@ -313,8 +376,8 @@
         grid=(parts // shards,),
         in_specs=[
             pl.BlockSpec((shards, rows, tokens), lambda i: (i, 0, 0)),
+            pl.BlockSpec((shards, tokens, LANES), lambda i: (i, 1, 0)),
             pl.BlockSpec((shards, 2 * tokens, LANES), lambda i: (i, 0, 0)),
-            pl.BlockSpec((shards, tokens, 2 * lat_width), lambda i: (i, 0, 0)),
         ],
         out_specs=[
             pl.BlockSpec((2, cols, lat_width), lambda i: (0, 0, 0)),
@@ -336,20 +399,15 @@
 def back_kernel(own_ref, *refs):
     res_refs, (spot_ref, grad_ref, enc_ref, back_ref, sum_ref) = refs[:-5], refs[-5:]
     members = len(res_refs)
-    shards, tokens, width = spot_ref.shape
+    shards, tokens = spot_ref.shape[0], spot_ref.shape[1] // 2
     cols, _, lat_width = enc_ref.shape
     rows = tokens // members
     step = pl.program_id(0)
-    for shard in range(shards):
-        for member in range(members):
-            low = pl.multiple_of((own_ref[1] ^ member) * rows, rows)
-            table = grad_ref[shard, pl.ds(low, rows), :].astype(F32)
-            to = shard * tokens + member * rows
-            for chunk in range(width // LANES):
-                at = slice(chunk * LANES, (chunk + 1) * LANES)
-                spot = spot_ref[shard, pl.ds(low, rows), at].astype(F32).astype(jnp.int32)
-                found = jnp.where(spot < LANES, lane_pick(table, spot & (LANES - 1)), 0.0)
-                back_ref[to : to + rows, at] = found.astype(BF16)
+
+    def row_of(row):
+        return pl.multiple_of((own_ref[1] ^ (row // rows)) * rows + row % rows, 16)
+
+    fill_dense(grad_ref, spot_ref, back_ref, row_of)
 
     @pl.when(step == 0)
     def _():
@@ -373,7 +431,7 @@
 
 
 def encoder_grads(own, res, spots, grads, cols, lat_width):
-    parts, tokens, _ = spots.shape
+    parts, tokens, _ = grads.shape
     rows = 4 * tokens // len(res)
     shards = 4
     return pl.pallas_call(
@@ -415,11 +473,10 @@
     packed, rank = pack(lat_width, parts, members, own, cotangent, residual, index, active_count)
     values = slot_values(rank, value)
     got = exchange(packed, "dp")
-    share = got[:, : 4 * tokens // members, :]
+    terms, share = slot_terms(decoder_first.transpose(1, 2, 0), decoder_second.T, values, got)
     res_near, res_next = from_hops(share, "layer", layers, (1, 2))
-    terms = slot_terms(decoder_first.transpose(1, 2, 0), decoder_second.T, values, got)
     slots = exchange(terms, "dp")
-    spots = slot_spots(got, lat_width)
+    spots = slot_spots(got)
     slots, spots, res_next = lax.optimization_barrier((slots, spots, res_next))
     grads, part = slot_totals(slots, rank)
     grads, res_near = lax.optimization_barrier((grads, res_near))
@@ -428,7 +485,7 @@
     first_grad, second_grad = decoder_grads(got, slots, spots, cols, lat_width)
     part = functools.reduce(jnp.add, from_hops(part, "layer", layers, (1, 2, 3)), part)
     all_grads, first_grad, part = lax.optimization_barrier((all_grads, first_grad, part))
-    res = [got, res_near, res_next, res_last]
+    res = [share, res_near, res_next, res_last]
     encoder_grad = encoder_grads(own, res, spots, all_grads, cols, lat_width)
     far = from_hops(part, "layer", layers, (4, 8, 12))
     *far, encoder_grad = lax.optimization_barrier((*far, encoder_grad))

time: 136 us -> 167 us (1.23)
  Pallas kernels: 51.3 us -> 76.8 us
  waiting for transfers between devices: 38.4 us -> 46.6 us
  local copies, waits for them, and re-layouts: 2.72 us -> 0.02 us
    pallas_call x1, Pallas kernels: 10.1 us -> 26.9 us  [decoder_grads(): pl.pallas_call(codes_kernel, grid=(parts // shards,), in_specs=[pl.BlockS...]
    pallas_call x1, Pallas kernels: 10.5 us -> 26.5 us  [encoder_grads(): pl.pallas_call(back_kernel, grid=(parts // shards,), in_specs=[pl.BlockSp...]
    ppermute x9, waiting for transfers between devices: 2.58 us -> 9.04 us  [from_hops(): lax.ppermute(array, axis, [(at, at ^ hop) for at in range(size)])]
    pallas_call x1, Pallas kernels: 16 us -> 10.1 us  [slot_spots(): pl.pallas_call(spots_kernel, grid=(parts // shards,), in_specs=[pl.BlockS...]
    slice x1 -> x0, local copies, waits for them, and re-layouts: 1.93 us -> none  [shards(): share = got[:, :4 * tokens // members, :]]
    pallas_call x1, Pallas kernels: 8 us -> 6.14 us  [slot_terms(): pl.pallas_call(functools.partial(terms_kernel, more), grid=(parts // shar...]
    all_to_all x3, waiting for transfers between devices: 35.8 us -> 37.5 us  [exchange(): return lax.all_to_all(array, axis, 0, 0, tiled=True)]
  transfers between devices with their start and end apart: 12 -> 12, of which waited for: 2 -> 4; matrix products, arithmetic and copies ran while one was open for 1% -> 0% of each run, Pallas kernels for 28% -> 39%
where the time goes in v6:
time: 167 us; the launch traced here: 166 us
  Pallas kernels  76.8 us (46%)
  waiting for transfers between devices  46.6 us (28%)
  starting transfers between devices  40.7 us (24%)
    all_to_all x3, waiting for transfers between devices, exchange(): return lax.all_to_all(array, axis, 0, 0, tiled=True)  37.5 us
    pallas_call x1, Pallas kernels, decoder_grads(): pl.pallas_call(codes_kernel, grid=(parts // shards,), in_specs=[pl.BlockS...  26.9 us
    pallas_call x1, Pallas kernels, encoder_grads(): pl.pallas_call(back_kernel, grid=(parts // shards,), in_specs=[pl.BlockSp...  26.5 us
    all_to_all x3, starting transfers between devices, exchange(): return lax.all_to_all(array, axis, 0, 0, tiled=True)  24.8 us
    ppermute x9, starting transfers between devices, from_hops(): lax.ppermute(array, axis, [(at, at ^ hop) for at in range(size)])  15.9 us
    pallas_call x1, Pallas kernels, slot_spots(): pl.pallas_call(spots_kernel, grid=(parts // shards,), in_specs=[pl.BlockS...  10.1 us
    ppermute x9, waiting for transfers between devices, from_hops(): lax.ppermute(array, axis, [(at, at ^ hop) for at in range(size)])  9.04 us
    pallas_call x1, Pallas kernels, slot_terms(): pl.pallas_call(functools.partial(terms_kernel, more), grid=(parts // shar...  6.14 us
  transfers between devices with their start and end apart: 12, of which 4 were waited for; matrix products, arithmetic and copies ran while one was open for 0% of the time, Pallas kernels for 39%

profile of v6, /device:TPU:2, one launch (start us, length us, event | category | flops | bytes accessed | tf_op | source)
XLA Modules:
  0.0 166.0 jit_solution(5942837770624959274)
XLA Ops:
  0.6 0.6 pad_add_fusion.start_ref.own_ref
  1.2 5.9 %shard_map.102 = (bf16[16,704,128]{2,1,0:T(8,128)(2,1)}, s32[2,64,128]{2,1,0:T(8,128)}) custom-call(s32[2]{0:T(128)} %pad_add_fusion.start_ref.own_ref, bf16[2,128,3584]{2,1,0:T(8,128)(2,1)} %cot_ref.1, bf16[2,128,3584]{2,1,0:T(8,128)(2,1)} %res_ref.1, s32[2,64,128]{2,1,0:T(8,128)} %bitcast.13, s32[2,128]{1,0:T(2,128)} %live_ref.1), custom_call_target="tpu_custom_call" | custom-call | bytes 5242880 | tf_op jit(solution)/shard_map/pallas_call | solution.py:91
  7.1 7.6 %all-to-all-start = ((bf16[16,704,128]{2,1,0:T(8,128)(2,1)}), bf16[16,704,128]{2,1,0:T(8,128)(2,1)}, u32[]{:S(2)}, u32[]{:S(2)}) async-start(bf16[16,704,128]{2,1,0:T(8,128)(2,1)} %get-tuple-element.25), calls=%async_computation | async-start | bytes 5767168 | tf_op jit(solution)/shard_map/all_to_all | solution.py:458
  14.8 0.4 shard_map.103.val_ref
  15.1 35.8 %all-to-all-done.got_ref = bf16[16,704,128]{2,1,0:T(8,128)(2,1)} async-done(((bf16[16,704,128]{2,1,0:T(8,128)(2,1)}), bf16[16,704,128]{2,1,0:T(8,128)(2,1)}, u32[]{:S(2)}, u32[]{:S(2)}) %all-to-all-start) | async-done | bytes 2883616 | tf_op jit(solution)/shard_map/all_to_all | solution.py:458
  50.9 6.1 %shard_map.104 = (bf16[16,256,128]{2,1,0:T(8,128)(2,1)}, bf16[16,128,128]{2,1,0:T(8,128)(2,1)S(1)}) custom-call(bf16[2,224,512]{2,1,0:T(8,128)(2,1)S(1)} %bitcast.11, bf16[224,512]{1,0:T(8,128)(2,1)S(1)} %bitcast.12, bf16[128,128]{1,0:T(8,128)(2,1)S(1)} %shard_map.103.val_ref, bf16[16,704,128]{2,1,0:T(8,128)(2,1)} %all-to-all-done.got_ref), custom_call_target="tpu_custom_call" | custom-call | flops 1409286144 | bytes 6291456 | tf_op jit(solution)/shard_map/pallas_call | solution.py:178
  57.1 9.3 %all-to-all-start.1 = ((bf16[16,256,128]{2,1,0:T(8,128)(2,1)}), bf16[16,256,128]{2,1,0:T(8,128)(2,1)S(1)}, u32[]{:S(2)}, u32[]{:S(2)}) async-start(bf16[16,256,128]{2,1,0:T(8,128)(2,1)} %get-tuple-element.26), calls=%async_computation.1 | async-start | bytes 2097152 | tf_op jit(solution)/shard_map/all_to_all | solution.py:458
  66.4 1.9 %collective-permute-start = (bf16[16,128,128]{2,1,0:T(8,128)(2,1)S(1)}, bf16[16,128,128]{2,1,0:T(8,128)(2,1)S(1)}, u32[]{:S(2)}, u32[]{:S(2)}) collective-permute-start(bf16[16,128,128]{2,1,0:T(8,128)(2,1)S(1)} %get-tuple-element.27.refs_0_), channel_id=1, source_target_pairs={{0,32},{16,48},{32,0},{48,16},{64,96},{80,112},{96,64},{112,80},{1... | collective-permute-start | bytes 1572872 | tf_op jit(solution)/shard_map/ppermute | solution.py:462
  68.3 0.7 collective-permute-start.1
  69.0 10.1 %shard_map.105.spot_ref.refs_4_ = s32[16,256,128]{2,1,0:T(8,128)} custom-call(bf16[16,704,128]{2,1,0:T(8,128)(2,1)} %all-to-all-done.got_ref), custom_call_target="tpu_custom_call" | custom-call | flops 4294967296 | bytes 8388608 | tf_op jit(solution)/shard_map/pallas_call | solution.py:282
  79.1 1.5 collective-permute-done.refs_2_
  80.6 1.7 %all-to-all-done.1.got_ref.val_ref = bf16[16,256,128]{2,1,0:T(8,128)(2,1)S(1)} async-done(((bf16[16,256,128]{2,1,0:T(8,128)(2,1)}), bf16[16,256,128]{2,1,0:T(8,128)(2,1)S(1)}, u32[]{:S(2)}, u32[]{:S(2)}) %all-to-all-start.1) | async-done | bytes 1048608 | tf_op jit(solution)/shard_map/all_to_all | solution.py:458
  82.3 0.9 shard_map.106
  83.2 7.5 %collective-permute-done.1.refs_1_ = bf16[16,128,128]{2,1,0:T(8,128)(2,1)S(1)} collective-permute-done((bf16[16,128,128]{2,1,0:T(8,128)(2,1)S(1)}, bf16[16,128,128]{2,1,0:T(8,128)(2,1)S(1)}, u32[]{:S(2)}, u32[]{:S(2)}) %collective-permute-start.1) | collective-permute-done | bytes 524320 | tf_op jit(solution)/shard_map/ppermute | solution.py:462
  90.8 1.9 %collective-permute-start.8 = (bf16[16,128,128]{2,1,0:T(8,128)(2,1)S(1)}, bf16[16,128,128]{2,1,0:T(8,128)(2,1)}, u32[]{:S(2)}, u32[]{:S(2)}) collective-permute-start(bf16[16,128,128]{2,1,0:T(8,128)(2,1)S(1)} %collective-permute-done.1.refs_1_), channel_id=1, source_target_pairs={{0,32},{16,48},{32,0},{48,16},{64,96},{80,112},{96,64},{112,80},{1... | collective-permute-start | bytes 1572872 | tf_op jit(solution)/shard_map/ppermute | solution.py:462
  92.7 7.8 %all-to-all-start.2 = ((bf16[16,128,128]{2,1,0:T(8,128)(2,1)}), bf16[16,128,128]{2,1,0:T(8,128)(2,1)S(1)}, u32[]{:S(2)}, u32[]{:S(2)}) async-start(bf16[16,128,128]{2,1,0:T(8,128)(2,1)} %get-tuple-element.30), calls=%async_computation.2 | async-start | bytes 1048576 | tf_op jit(solution)/shard_map/all_to_all | solution.py:458
  100.5 0.2 collective-permute-start.2
  100.7 0.1 collective-permute-start.3
  100.9 3.2 %collective-permute-start.4 = (bf16[2,64,128]{2,1,0:T(8,128)(2,1)S(1)}, bf16[2,64,128]{2,1,0:T(8,128)(2,1)S(1)}, u32[]{:S(2)}, u32[]{:S(2)}) collective-permute-start(bf16[2,64,128]{2,1,0:T(8,128)(2,1)S(1)} %get-tuple-element.33), channel_id=1, source_target_pairs={{0,48},{16,32},{32,16},{48,0},{64,112},{80,96},{96,80},{112,64},{1... | collective-permute-start | bytes 98312 | tf_op jit(solution)/shard_map/ppermute | solution.py:462
  104.1 26.9 %shard_map.107 = (bf16[2,224,512]{2,1,0:T(8,128)(2,1)}, bf16[224,512]{1,0:T(8,128)(2,1)}) custom-call(bf16[16,704,128]{2,1,0:T(8,128)(2,1)} %all-to-all-done.got_ref, bf16[16,256,128]{2,1,0:T(8,128)(2,1)S(1)} %all-to-all-done.1.got_ref.val_ref, s32[16,256,128]{2,1,0:T(8,128)} %shard_map.105.spot_ref.refs_4_), custom_call_target="tpu_custom_call" | custom-call | flops 1409286144 | bytes 8388608 | tf_op jit(solution)/shard_map/pallas_call | solution.py:374
  131.0 3.4 %collective-permute-start.5 = (bf16[2,64,128]{2,1,0:T(8,128)(2,1)S(1)}, bf16[2,64,128]{2,1,0:T(8,128)(2,1)S(1)}, u32[]{:S(2)}, u32[]{:S(2)}) collective-permute-start(bf16[2,64,128]{2,1,0:T(8,128)(2,1)S(1)} %add_add_fusion), channel_id=1, source_target_pairs={{0,64},{16,80},{32,96},{48,112},{64,0},{80,16},{96,32},{112,48},{1... | collective-permute-start | bytes 98312 | tf_op jit(solution)/shard_map/ppermute | solution.py:462
  134.4 4.5 %collective-permute-start.6 = (bf16[2,64,128]{2,1,0:T(8,128)(2,1)S(1)}, bf16[2,64,128]{2,1,0:T(8,128)(2,1)S(1)}, u32[]{:S(2)}, u32[]{:S(2)}) collective-permute-start(bf16[2,64,128]{2,1,0:T(8,128)(2,1)S(1)} %add_add_fusion), channel_id=1, source_target_pairs={{0,128},{16,144},{32,160},{48,176},{64,192},{80,208},{96,224},{112... | collective-permute-start | bytes 98312 | tf_op jit(solution)/shard_map/ppermute | solution.py:462
  138.9 26.5 %shard_map.108 = bf16[224,2,512]{2,1,0:T(2,128)(2,1)} custom-call(s32[2]{0:T(128)S(1)} %copy-done.2, bf16[16,128,128]{2,1,0:T(8,128)(2,1)S(1)} %get-tuple-element.27.refs_0_, bf16[16,128,128]{2,1,0:T(8,128)(2,1)S(1)} %collective-permute-done.1.refs_1_, bf16[16,128,128]{2,1,0:T(8,128)(2,1)S(1)} %collective-permute-done.refs_2_, ...), custom_call_target="tpu_custom_call" | custom-call | flops 939524096 | bytes 8388608 | tf_op jit(solution)/shard_map/pallas_call | solution.py:437
  165.4 0.6 convert_bitcast_fusion
  (20 shorter events, 0.1 us)
Async XLA Ops:
  7.1 7.7 %copy-start = (s32[2,64,128]{2,1,0:T(8,128)S(1)}, s32[2,64,128]{2,1,0:T(8,128)}, u32[]{:S(2)}) copy-start(s32[2,64,128]{2,1,0:T(8,128)} %get-tuple-element.24.rank_ref) | copy-start | bytes 196612
  7.1 7.7 %copy-start.1 = (bf16[2,128,64]{1,2,0:T(8,128)(2,1)S(1)}, bf16[2,128,64]{1,2,0:T(8,128)(2,1)}, u32[]{:S(2)}) copy-start(bf16[2,128,64]{1,2,0:T(8,128)(2,1)} %param.12) | copy-start | bytes 98308
  7.1 43.8 %copy-start.3 = (bf16[512,2,224]{0,2,1:T(8,128)(2,1)S(1)}, bf16[512,2,224]{0,2,1:T(8,128)(2,1)}, u32[]{:S(2)}) copy-start(bf16[512,2,224]{0,2,1:T(8,128)(2,1)} %param.9) | copy-start | bytes 1376260
  7.1 43.8 %copy-start.4 = (bf16[512,224]{0,1:T(8,128)(2,1)S(1)}, bf16[512,224]{0,1:T(8,128)(2,1)}, u32[]{:S(2)}) copy-start(bf16[512,224]{0,1:T(8,128)(2,1)} %param.10) | copy-start | bytes 688132
  7.1 43.8 %all-to-all-start = ((bf16[16,704,128]{2,1,0:T(8,128)(2,1)}), bf16[16,704,128]{2,1,0:T(8,128)(2,1)}, u32[]{:S(2)}, u32[]{:S(2)}) async-start(bf16[16,704,128]{2,1,0:T(8,128)(2,1)} %get-tuple-element.25), calls=%async_computation | async-start | bytes 5767168 | tf_op jit(solution)/shard_map/all_to_all | solution.py:458
  57.1 25.2 %all-to-all-start.1 = ((bf16[16,256,128]{2,1,0:T(8,128)(2,1)}), bf16[16,256,128]{2,1,0:T(8,128)(2,1)S(1)}, u32[]{:S(2)}, u32[]{:S(2)}) async-start(bf16[16,256,128]{2,1,0:T(8,128)(2,1)} %get-tuple-element.26), calls=%async_computation.1 | async-start | bytes 2097152 | tf_op jit(solution)/shard_map/all_to_all | solution.py:458
  66.4 14.2 %collective-permute-start = (bf16[16,128,128]{2,1,0:T(8,128)(2,1)S(1)}, bf16[16,128,128]{2,1,0:T(8,128)(2,1)S(1)}, u32[]{:S(2)}, u32[]{:S(2)}) collective-permute-start(bf16[16,128,128]{2,1,0:T(8,128)(2,1)S(1)} %get-tuple-element.27.refs_0_), channel_id=1, source_target_pairs={{0,32},{16,48},{32,0},{48,16},{64,96},{80,112},{96,64},{112,80},{1... | collective-permute-start | bytes 1572872 | tf_op jit(solution)/shard_map/ppermute | solution.py:462
  68.3 22.4 %collective-permute-start.1 = (bf16[16,128,128]{2,1,0:T(8,128)(2,1)S(1)}, bf16[16,128,128]{2,1,0:T(8,128)(2,1)S(1)}, u32[]{:S(2)}, u32[]{:S(2)}) collective-permute-start(bf16[16,128,128]{2,1,0:T(8,128)(2,1)S(1)} %get-tuple-element.27.refs_0_), channel_id=1, source_target_pairs={{0,16},{16,0},{32,48},{48,32},{64,80},{80,64},{96,112},{112,96},{1... | collective-permute-start | bytes 1572872 | tf_op jit(solution)/shard_map/ppermute | solution.py:462
  90.8 48.1 %collective-permute-start.8 = (bf16[16,128,128]{2,1,0:T(8,128)(2,1)S(1)}, bf16[16,128,128]{2,1,0:T(8,128)(2,1)}, u32[]{:S(2)}, u32[]{:S(2)}) collective-permute-start(bf16[16,128,128]{2,1,0:T(8,128)(2,1)S(1)} %collective-permute-done.1.refs_1_), channel_id=1, source_target_pairs={{0,32},{16,48},{32,0},{48,16},{64,96},{80,112},{96,64},{112,80},{1... | collective-permute-start | bytes 1572872 | tf_op jit(solution)/shard_map/ppermute | solution.py:462
  92.7 38.3 %all-to-all-start.2 = ((bf16[16,128,128]{2,1,0:T(8,128)(2,1)}), bf16[16,128,128]{2,1,0:T(8,128)(2,1)S(1)}, u32[]{:S(2)}, u32[]{:S(2)}) async-start(bf16[16,128,128]{2,1,0:T(8,128)(2,1)} %get-tuple-element.30), calls=%async_computation.2 | async-start | bytes 1048576 | tf_op jit(solution)/shard_map/all_to_all | solution.py:458
  100.5 38.4 %copy-start.2 = (s32[2]{0:T(128)S(1)}, s32[2]{0:T(128)}, u32[]{:S(2)}) copy-start(s32[2]{0:T(128)} %pad_add_fusion.start_ref.own_ref) | copy-start | bytes 28
  100.5 30.5 %collective-permute-start.2 = (bf16[2,64,128]{2,1,0:T(8,128)(2,1)S(1)}, bf16[2,64,128]{2,1,0:T(8,128)(2,1)S(1)}, u32[]{:S(2)}, u32[]{:S(2)}) collective-permute-start(bf16[2,64,128]{2,1,0:T(8,128)(2,1)S(1)} %get-tuple-element.33), channel_id=1, source_target_pairs={{0,16},{16,0},{32,48},{48,32},{64,80},{80,64},{96,112},{112,96},{1... | collective-permute-start | bytes 98312 | tf_op jit(solution)/shard_map/ppermute | solution.py:462
  100.7 30.2 %collective-permute-start.3 = (bf16[2,64,128]{2,1,0:T(8,128)(2,1)S(1)}, bf16[2,64,128]{2,1,0:T(8,128)(2,1)S(1)}, u32[]{:S(2)}, u32[]{:S(2)}) collective-permute-start(bf16[2,64,128]{2,1,0:T(8,128)(2,1)S(1)} %get-tuple-element.33), channel_id=1, source_target_pairs={{0,32},{16,48},{32,0},{48,16},{64,96},{80,112},{96,64},{112,80},{1... | collective-permute-start | bytes 98312 | tf_op jit(solution)/shard_map/ppermute | solution.py:462
  100.9 30.1 %collective-permute-start.4 = (bf16[2,64,128]{2,1,0:T(8,128)(2,1)S(1)}, bf16[2,64,128]{2,1,0:T(8,128)(2,1)S(1)}, u32[]{:S(2)}, u32[]{:S(2)}) collective-permute-start(bf16[2,64,128]{2,1,0:T(8,128)(2,1)S(1)} %get-tuple-element.33), channel_id=1, source_target_pairs={{0,48},{16,32},{32,16},{48,0},{64,112},{80,96},{96,80},{112,64},{1... | collective-permute-start | bytes 98312 | tf_op jit(solution)/shard_map/ppermute | solution.py:462
  131.0 34.4 %collective-permute-start.5 = (bf16[2,64,128]{2,1,0:T(8,128)(2,1)S(1)}, bf16[2,64,128]{2,1,0:T(8,128)(2,1)S(1)}, u32[]{:S(2)}, u32[]{:S(2)}) collective-permute-start(bf16[2,64,128]{2,1,0:T(8,128)(2,1)S(1)} %add_add_fusion), channel_id=1, source_target_pairs={{0,64},{16,80},{32,96},{48,112},{64,0},{80,16},{96,32},{112,48},{1... | collective-permute-start | bytes 98312 | tf_op jit(solution)/shard_map/ppermute | solution.py:462
  134.4 31.0 %collective-permute-start.6 = (bf16[2,64,128]{2,1,0:T(8,128)(2,1)S(1)}, bf16[2,64,128]{2,1,0:T(8,128)(2,1)S(1)}, u32[]{:S(2)}, u32[]{:S(2)}) collective-permute-start(bf16[2,64,128]{2,1,0:T(8,128)(2,1)S(1)} %add_add_fusion), channel_id=1, source_target_pairs={{0,128},{16,144},{32,160},{48,176},{64,192},{80,208},{96,224},{112... | collective-permute-start | bytes 98312 | tf_op jit(solution)/shard_map/ppermute | solution.py:462
  138.9 26.5 %collective-permute-start.7 = (bf16[2,64,128]{2,1,0:T(8,128)(2,1)S(1)}, bf16[2,64,128]{2,1,0:T(8,128)(2,1)S(1)}, u32[]{:S(2)}, u32[]{:S(2)}) collective-permute-start(bf16[2,64,128]{2,1,0:T(8,128)(2,1)S(1)} %add_add_fusion), channel_id=1, source_target_pairs={{0,192},{16,208},{32,224},{48,240},{64,128},{80,144},{96,160},{112... | collective-permute-start | bytes 98312 | tf_op jit(solution)/shard_map/ppermute | solution.py:462
